TPU v7x, 128 devices: a whole 4x4x4 slice. The times are simulated.
128 devices in a mesh: dp: 8 (over x, z_hi), tensor: 8 (over z_lo, y), section: 2 (over core).
Axes of the slice: x: 4, y: 4, z: 4 (z_hi: 2, z_lo: 2; z = z_hi * 2 + z_lo), core: 2. Of those that a mesh axis runs over, the one named last changes fastest.
Arguments:
- text_hidden: bfloat16 [2, 8, 128, 8192], P(None, 'dp', None, 'tensor'), may hold values from -6 to 6
- image_tokens: bfloat16 [8, 3200, 8192], P('dp', 'section', 'tensor'), may hold values from -6 to 6
- attn_gain: float32 [2, 8192], P('section'), may hold values from 0.25 to 1.75
- w_query: bfloat16 [2, 8192, 4096], P('section', None, 'tensor'), may hold values from -0.0625 to 0.0625
- w_keyval: bfloat16 [2, 8192, 8, 256], P('section', 'tensor'), may hold values from -0.09375 to 0.09375
- q_gain: float32 [2, 128], P('section'), may hold values from 0.5 to 2
- k_gain: float32 [2, 128], P('section'), may hold values from 0.5 to 2
- w_out: bfloat16 [2, 4096, 8192], P('section', 'tensor'), may hold values from -0.375 to 0.375
- gate: float32 [2], P('section'), may hold values from 0.3 to 1.5
- image_choice: int32 [2, 8, 2], P(None, 'dp'), may hold values from 0 to 7
- valid_tiles: int32 [8], replicated, may hold values from 1 to 2
Outputs:
- layer_outputs: bfloat16 [2, 2, 8, 128, 8192], P('section', None, 'dp', None, 'tensor')
Inputs may be any that keep to these rules, and one draw needn't show every extreme that they name: `image_choice`: image indices.
All inputs are finite; a program needn't handle non-finite values.
Results may differ from a plain program's by a relative error of at most 0.029.
Values may be sent and summed in bfloat16 or wider, within the bound.
A program may use at most 128 MiB of HBM per device.

v0:
```python
import jax
import jax.numpy as jnp
from jax import lax
from jax.sharding import PartitionSpec as P

TILE_TOK = 1600


def shifted(value, axis, by):
    count = lax.axis_size(axis)
    pairs = [(i, i + by) for i in range(count) if 0 <= i + by < count]
    return lax.ppermute(value, axis, pairs)


def rms_scale(values, gain):
    return values * lax.rsqrt(jnp.mean(values * values, axis=-1, keepdims=True) + 1e-05) * gain


def local(
    text_hidden,
    image_tokens,
    attn_gain,
    w_query,
    w_keyval,
    q_gain,
    k_gain,
    w_out,
    gate,
    image_choice,
    valid_tiles,
):
    section_id = lax.axis_index("section")
    tensor_id = lax.axis_index("tensor")
    head_dim = q_gain.shape[1]
    kv_heads = w_keyval.shape[2] // lax.axis_size("tensor")
    width_dev = image_tokens.shape[2]
    width_full = w_query.shape[1]
    heads_dev = w_query.shape[2] // head_dim
    group_size = heads_dev // kv_heads
    batches = text_hidden.shape[0]
    seqs_dev = text_hidden.shape[1]
    seq_len = text_hidden.shape[2]
    whole_images = lax.all_gather(image_tokens, "section", axis=1, tiled=True)
    images_dev = whole_images.shape[0]
    patches = whole_images.shape[1]
    flat_images = whole_images.reshape(images_dev * patches, width_dev)
    block = w_keyval[0]
    keyval = lax.psum_scatter(
        jnp.einsum("pd,dkc->kpc", flat_images, block, preferred_element_type=jnp.float32).astype(
            jnp.bfloat16
        ),
        "tensor",
        scatter_dimension=0,
        tiled=True,
    ).astype(jnp.float32)
    keys_local = rms_scale(keyval[..., :head_dim], k_gain[0]).astype(jnp.bfloat16)
    vals_local = keyval[..., head_dim:].astype(jnp.bfloat16)
    local_pairs = jnp.concatenate([keys_local, vals_local], axis=2)
    all_pairs = lax.all_gather(local_pairs, "dp", axis=1, tiled=True)
    n_images = all_pairs.shape[1] // patches
    pairs_img = all_pairs.reshape(kv_heads, n_images, patches, 2 * head_dim)
    tile_of = jnp.arange(patches, dtype=jnp.int32) // TILE_TOK
    gate_value = jnp.tanh(gate[0])

    def one_sequence(item):
        query_one, chosen_one = item
        first = chosen_one[0]
        second = chosen_one[1]
        pair_rows = jnp.concatenate(
            [
                lax.dynamic_index_in_dim(pairs_img, first, 1, keepdims=False),
                lax.dynamic_index_in_dim(pairs_img, second, 1, keepdims=False),
            ],
            axis=1,
        )
        keys_pair = pair_rows[..., :head_dim]
        vals_pair = pair_rows[..., head_dim:]
        allowed = jnp.concatenate(
            [tile_of < valid_tiles[first], (tile_of < valid_tiles[second]) & (second != first)]
        )
        scores = jnp.einsum(
            "qkgd,knd->kgqn", query_one, keys_pair, preferred_element_type=jnp.float32
        )
        scores = jnp.where(allowed[None, None, None, :], scores, -1e30)
        peak = jnp.max(scores, axis=-1, keepdims=True)
        expo = jnp.exp(scores - peak)
        weights = (expo / jnp.sum(expo, axis=-1, keepdims=True)).astype(jnp.bfloat16)
        attended = jnp.einsum(
            "kgqn,knd->qkgd", weights, vals_pair, preferred_element_type=jnp.float32
        )
        return attended.astype(jnp.bfloat16).reshape(seq_len, heads_dev * head_dim)

    results = []
    received = jnp.zeros((seqs_dev, seq_len, width_full), jnp.bfloat16)
    for tick in range(batches + 1):
        if tick < batches:
            entering = lax.all_gather(text_hidden[tick], "tensor", axis=2, tiled=True)
        else:
            entering = jnp.zeros_like(received)
        hidden = jnp.where(section_id == 0, entering, received)
        normed = rms_scale(hidden.astype(jnp.float32), attn_gain[0]).astype(jnp.bfloat16)
        query = jnp.dot(
            normed.reshape(-1, width_full), w_query[0], preferred_element_type=jnp.float32
        )
        query = query.reshape(seqs_dev, seq_len, kv_heads, group_size, head_dim)
        query = (rms_scale(query, q_gain[0]) * head_dim ** (-0.5)).astype(jnp.bfloat16)
        chosen_first = image_choice[min(tick, batches - 1)]
        chosen_second = image_choice[max(tick - 1, 0)]
        partial_attended = lax.map(
            one_sequence, (query, jnp.where(section_id == 0, chosen_first, chosen_second))
        )
        partial_attended = partial_attended.reshape(seqs_dev * seq_len, heads_dev * head_dim)
        proj = jnp.dot(partial_attended, w_out[0], preferred_element_type=jnp.float32)
        total = lax.psum(
            proj.reshape(seqs_dev, seq_len, width_full).astype(jnp.bfloat16), "tensor"
        ).astype(jnp.float32)
        updated = (hidden.astype(jnp.float32) + gate_value * total).astype(jnp.bfloat16)
        results.append(lax.dynamic_slice_in_dim(updated, tensor_id * width_dev, width_dev, 2))
        if tick < batches:
            received = shifted(updated, "section", 1)
    slots = [
        jnp.where(section_id == 0, results[batch], results[batch + 1]) for batch in range(batches)
    ]
    return jnp.stack(slots)[None]


def solution(mesh):
    placed = (
        P(None, "dp", None, "tensor"),
        P("dp", "section", "tensor"),
        P("section", None),
        P("section", None, "tensor"),
        P("section", "tensor", None, None),
        P("section", None),
        P("section", None),
        P("section", "tensor", None),
        P("section"),
        P(None, "dp", None),
        P(),
    )
    return jax.shard_map(
        local,
        mesh=mesh,
        in_specs=placed,
        out_specs=P("section", None, "dp", None, "tensor"),
        check_vma=False,
    )
```

profile of v0, /device:TPU:1, one launch (start us, length us, event | category | flops | bytes accessed | tf_op | source)
XLA Modules:
  0.0 813.5 jit_solution(12989925918594288741)
XLA Ops:
  7.3 25.2 %all-gather.7.cloned.1.call-done = bf16[1,3200,1024]{2,1,0:T(8,128)(2,1)} async-done(((bf16[1,1600,1024]{2,1,0:T(8,128)(2,1)}), bf16[1,3200,1024]{2,1,0:T(8,128)(2,1)}) %all-gather.7.cloned.1.call-update) | async-done | bytes 6553616 | tf_op jit(solution)/shard_map/all_gather | solution.py:43
  32.5 21.1 %convert_bitcast_fusion = bf16[8,3200,256]{1,2,0:T(8,128)(2,1)} fusion(bf16[1,3200,1024]{2,1,0:T(8,128)(2,1)} %all-gather.7.cloned.1.call-done, bf16[1024,8,256]{2,1,0:T(8,128)(2,1)} %bitcast.354), kind=kOutput, calls=%fused_computation.15 | convolution fusion | flops 13428326400 | bytes 23855104 | tf_op jit(solution)/shard_map/pd,dkc->kpc/dot_general | solution.py:49
  55.6 136.5 %reduce-scatter.2.cloned.1.call-done = bf16[1,3200,256]{1,2,0:T(8,128)(2,1)} async-done(((bf16[8,3200,256]{1,2,0:T(8,128)(2,1)}), bf16[1,3200,256]{1,2,0:T(8,128)(2,1)}) %reduce-scatter.2.cloned.1.call-update) | async-done | bytes 1638416 | tf_op jit(solution)/shard_map/reduce_scatter | solution.py:48
  212.1 17.1 %all-gather.11.cloned.1.call-done = bf16[1,1,128,8192]{3,2,1,0:T(8,128)(2,1)} async-done(((bf16[1,1,128,1024]{3,2,1,0:T(8,128)(2,1)}), bf16[1,1,128,8192]{3,2,1,0:T(8,128)(2,1)}) %all-gather.11.cloned.1.call-update) | async-done | bytes 2097168 | tf_op jit(solution)/shard_map/all_gather | solution.py:97
  229.8 4.7 fusion.130
  235.5 151.7 %all-gather.9.cloned.1.call-done = bf16[1,25600,256]{1,2,0:T(8,128)(2,1)} async-done(((bf16[1,3200,256]{1,2,0:T(8,128)(2,1)}), bf16[1,25600,256]{1,2,0:T(8,128)(2,1)}) %all-gather.9.cloned.1.call-update) | async-done | bytes 13107216 | tf_op jit(solution)/shard_map/all_gather | solution.py:59
  387.2 8.5 %copy.84 = bf16[32,8,8,3200]{3,2,1,0:T(8,128)(2,1)S(1)} copy(bf16[32,8,8,3200]{3,1,2,0:T(8,128)(2,1)} %bitcast.334) | data formatting | bytes 26214400
  395.7 22.1 %constant_dynamic-slice_fusion.1 = (bf16[1,1,3200,256]{2,1,3,0:T(2,128)(2,1)}, bf16[1,1,3200,256]{2,1,3,0:T(2,128)(2,1)S(1)}, bf16[1,1,3200,256]{2,1,3,0:T(2,128...) fusion(bf16[1,8,3200,256]{2,1,3,0:T(8,128)(2,1)S(1)} %bitcast.32, ...), kind=kLoop, calls=%fused_computation.156 | loop fusion | bytes 19660824 | tf_op jit(solution)/shard_map/while/body/eval_jaxpr/jit(dynamic_index_in_dim)/dynamic_slice | solution.py:71
  417.8 7.4 copy.51
  425.1 7.4 copy.50
  433.6 5.6 bitcast_reduce_fusion.2
  450.6 75.2 %all-reduce.4.cloned.1.call-done = bf16[1,128,8192]{2,1,0:T(8,128)(2,1)} async-done(((bf16[1,128,8192]{2,1,0:T(8,128)(2,1)}), bf16[1,128,8192]{2,1,0:T(8,128)(2,1)}) %all-reduce.4.cloned.1.call-update) | async-done | bytes 2097168 | tf_op jit(solution)/shard_map/psum | solution.py:114
  533.2 7.4 copy.57
  540.6 7.4 copy.58
  548.0 19.8 %all-gather.13.cloned.1.call-done = bf16[1,1,128,8192]{3,2,1,0:T(8,128)(2,1)} async-done(((bf16[1,1,128,1024]{3,2,1,0:T(8,128)(2,1)}), bf16[1,1,128,8192]{3,2,1,0:T(8,128)(2,1)}) %all-gather.13.cloned.1.call-update) | async-done | bytes 2097168 | tf_op jit(solution)/shard_map/all_gather | solution.py:97
  570.9 6.3 fusion.131
  580.2 5.7 bitcast_reduce_fusion.1
  595.8 82.1 %all-reduce.6.cloned.1.call-done = bf16[1,128,8192]{2,1,0:T(8,128)(2,1)} async-done(((bf16[1,128,8192]{2,1,0:T(8,128)(2,1)}), bf16[1,128,8192]{2,1,0:T(8,128)(2,1)}) %all-reduce.6.cloned.1.call-update) | async-done | bytes 2097168 | tf_op jit(solution)/shard_map/psum | solution.py:114
  677.9 4.2 fusion.28
  686.1 7.4 copy.64
  693.4 4.7 copy.65
  700.4 6.3 fusion.132
  722.3 3.8 fusion.72
  726.2 77.8 %all-reduce.8.cloned.1.call-done = bf16[1,128,8192]{2,1,0:T(8,128)(2,1)} async-done(((bf16[1,128,8192]{2,1,0:T(8,128)(2,1)}), bf16[1,128,8192]{2,1,0:T(8,128)(2,1)}) %all-reduce.8.cloned.1.call-update) | async-done | bytes 2097168 | tf_op jit(solution)/shard_map/psum | solution.py:114
  (116 shorter events, 68.2 us)
Async XLA Ops:
  6.5 205.5 %copy-start = (f32[1,128]{1,0:T(1,128)S(1)}, f32[1,128]{1,0:T(1,128)}, u32[]{:S(2)}) copy-start(f32[1,128]{1,0:T(1,128)} %param.16) | copy-start | bytes 1540
  6.5 26.0 %all-gather.7.cloned.1.call-start = ((), (), s32[]{:S(2)}) async-start(), calls=%async_computation.1 | async-start | bytes 9830400 | tf_op jit(solution)/shard_map/all_gather | solution.py:43
  7.3 184.9 %reduce-scatter.2.cloned.1.call-start = ((), (), s32[]{:S(2)}) async-start(), calls=%async_computation.2 | async-start | bytes 14745600 | tf_op jit(solution)/shard_map/reduce_scatter | solution.py:48
  53.7 139.9 %copy-start.12 = (f32[1,128]{1,0:T(1,128)S(1)}, f32[1,128]{1,0:T(1,128)}, u32[]{:S(2)}) copy-start(f32[1,128]{1,0:T(1,128)} %param.17) | copy-start | bytes 1540
  53.7 175.5 %all-gather.11.cloned.1.call-start = ((), (), s32[]{:S(2)}) async-start(), calls=%async_computation.7 | async-start | bytes 2359296 | tf_op jit(solution)/shard_map/all_gather | solution.py:97
  55.5 331.6 %all-gather.9.cloned.1.call-start = ((), (), s32[]{:S(2)}) async-start(), calls=%async_computation.3 | async-start | bytes 14745600 | tf_op jit(solution)/shard_map/all_gather | solution.py:59
  193.6 16.4 %copy-start.10 = (s32[8]{0:T(128)S(1)}, s32[8]{0:T(128)}, u32[]{:S(2)}) copy-start(s32[8]{0:T(128)} %param.21) | copy-start | bytes 100
  195.0 34.8 %copy-start.13 = (f32[1,8192]{1,0:T(1,128)S(1)}, f32[1,8192]{1,0:T(1,128)}, u32[]{:S(2)}) copy-start(f32[1,8192]{1,0:T(1,128)} %param.13) | copy-start | bytes 98308
  196.3 329.5 %all-reduce.4.cloned.1.call-start = ((), (), s32[]{:S(2)}) async-start(), calls=%async_computation.4 | async-start | bytes 4194304 | tf_op jit(solution)/shard_map/psum | solution.py:114
  439.2 7.2 slice-start
  449.1 118.7 %all-gather.13.cloned.1.call-start = ((), (), s32[]{:S(2)}) async-start(), calls=%async_computation.8 | async-start | bytes 2359296 | tf_op jit(solution)/shard_map/all_gather | solution.py:97
  449.6 228.2 %all-reduce.6.cloned.1.call-start = ((), (), s32[]{:S(2)}) async-start(), calls=%async_computation.5 | async-start | bytes 4194304 | tf_op jit(solution)/shard_map/psum | solution.py:114
  529.4 38.4 %collective-permute-start = (bf16[1,128,8192]{2,1,0:T(8,128)(2,1)}, bf16[1,128,8192]{2,1,0:T(8,128)(2,1)}, u32[]{:S(2)}, u32[]{:S(2)}) collective-permute-start(bf16[1,128,8192]{2,1,0:T(8,128)(2,1)} %fusion.32), channel_id=1, source_target_pairs={{0,1},{2,3},{4,5},{6,7},{8,9},{10,11},{12,13},{14,15},{16,17},{18,... | collective-permute-start | bytes 6291464 | tf_op jit(solution)/shard_map/ppermute | solution.py:12
  548.0 22.9 %copy-start.14 = (f32[1,8192]{1,0:T(1,128)S(1)}, f32[1,8192]{1,0:T(1,128)}, u32[]{:S(2)}) copy-start(f32[1,8192]{1,0:T(1,128)} %param.13) | copy-start | bytes 98308
  570.9 6.4 copy-start.2
  585.8 3.7 copy-start.3
  585.9 7.2 slice-start.2
  595.8 208.2 %all-reduce.8.cloned.1.call-start = ((), (), s32[]{:S(2)}) async-start(), calls=%async_computation.6 | async-start | bytes 4194304 | tf_op jit(solution)/shard_map/psum | solution.py:114
  682.1 16.1 %collective-permute-start.1 = (bf16[1,128,8192]{2,1,0:T(8,128)(2,1)}, bf16[1,128,8192]{2,1,0:T(8,128)(2,1)}, u32[]{:S(2)}, u32[]{:S(2)}) collective-permute-start(bf16[1,128,8192]{2,1,0:T(8,128)(2,1)} %fusion.28), channel_id=1, source_target_pairs={{0,1},{2,3},{4,5},{6,7},{8,9},{10,11},{12,13},{14,15},{16,17},{18,... | collective-permute-start | bytes 6291464 | tf_op jit(solution)/shard_map/ppermute | solution.py:12
  693.4 6.9 copy-start.15
  700.4 9.2 %copy-start.5 = (bf16[1,1,3200,256]{3,2,1,0:T(8,128)(2,1)S(1)}, bf16[1,1,3200,256]{3,2,1,0:T(8,128)(2,1)}, u32[]{:S(2)}) copy-start(bf16[1,1,3200,256]{3,2,1,0:T(8,128)(2,1)} %copy.64) | copy-start | bytes 4915204
  700.4 9.2 %copy-start.6 = (bf16[1,1,3200,256]{3,2,1,0:T(8,128)(2,1)S(1)}, bf16[1,1,3200,256]{3,2,1,0:T(8,128)(2,1)}, u32[]{:S(2)}) copy-start(bf16[1,1,3200,256]{3,2,1,0:T(8,128)(2,1)} %copy.65) | copy-start | bytes 4915204
  712.5 7.2 slice-start.4
  722.3 83.9 %copy-start.1 = (f32[1,128]{1,0:T(1,128)S(1)}, f32[1,128]{1,0:T(1,128)}, u32[]{:S(2)}) copy-start(f32[1,128]{1,0:T(1,128)} %param.16) | copy-start | bytes 1540
  (9 other events, 28.3 us)
Sparse Core Ops, SparseCore 0:
  9.0 23.4 all-gather.6
  53.8 138.2 reduce-scatter.1
  193.8 35.3 all-gather.10
  231.4 155.7 all-gather.8
  449.2 76.5 all-reduce.3
  527.3 40.4 all-gather.12
  595.9 81.9 all-reduce.5
  722.4 81.4 all-reduce.7
where the time goes:
time: 826 us; the launch traced here: 813 us
  waiting for transfers between devices  587 us (71%)
  local copies, waits for them, and re-layouts  79.7 us (10%)
  matrix products  70.9 us (9%)
  other arithmetic  42.9 us (5%)
  between operations  30 us (4%)
    psum x3, waiting for transfers between devices, local(): lax.psum(proj.reshape(seqs_dev, seq_len, width_full).astype(jnp.bfloat16)...  235 us
    all_gather x1, waiting for transfers between devices, local(): all_pairs = lax.all_gather(local_pairs, 'dp', axis=1, tiled=True)  152 us
    reduce_scatter x1, waiting for transfers between devices, local(): lax.psum_scatter(jnp.einsum('pd,dkc->kpc', flat_images, block, preferred_...  137 us
    dynamic_slice x4, local copies, waits for them, and re-layouts, one_sequence(): lax.dynamic_index_in_dim(pairs_img, first, 1, keepdims=False)  44.2 us
    all_gather x2, waiting for transfers between devices, local(): entering = lax.all_gather(text_hidden[tick], 'tensor', axis=2, tiled=True)  36.9 us
    all_gather x1, waiting for transfers between devices, local(): whole_images = lax.all_gather(image_tokens, 'section', axis=1, tiled=True)  25.2 us
    dot_general x1, matrix products, local(): jnp.einsum('pd,dkc->kpc', flat_images, block, preferred_element_type=jnp....  21.1 us
    dynamic_slice x3, local copies, waits for them, and re-layouts, one_sequence(): lax.dynamic_index_in_dim(pairs_img, second, 1, keepdims=False)  19.5 us
  transfers between devices with their start and end apart: 10, of which 8 were waited for; matrix products, arithmetic and copies ran while one was open for 6% of the time, Pallas kernels for 0%

commit v1 on v0

v1 whole, which is shorter than its diff:
```python
import functools

import jax
import jax.numpy as jnp
from jax import lax
from jax.experimental import pallas as pl
from jax.experimental.pallas import tpu as pltpu
from jax.sharding import PartitionSpec as P

TILE_TOK = 1600
PIECES = 10
MESH = pl.DeviceIdType.MESH
BF = jnp.bfloat16
F32 = jnp.float32


def position():
    dp = lax.axis_index("dp")
    tensor = lax.axis_index("tensor")
    return dp // 2, dp % 2, tensor // 4, tensor % 4, lax.axis_index("section")


def device(x, zh, zl, y, core):
    return (x * 2 + zh, zl * 4 + y, core)


def kv_kernel(
    tok_ref, w_ref, gain_ref, text_ref,
    out_ref, text_out_ref,
    tok, wgt, part, from_y1, from_y2, from_z, done,
    tok_sem, w_sem, loc_sem, core_sem, text_send, text_recv, send, recv,
):
    x, zh, zl, y, core = position()
    dp = x * 2 + zh
    tensor = zl * 4 + y
    half = tok_ref.shape[0]
    rows = half * 2 // PIECES
    y_up, y_dn = (y + 1) % 4, (y + 3) % 4
    x_up, x_dn = (x + 1) % 4, (x + 3) % 4
    to_y_up = device(x, zh, zl, y_up, core)
    to_y_dn = device(x, zh, zl, y_dn, core)
    to_z_lo = device(x, zh, 1 - zl, y, core)
    to_z_hi = device(x, 1 - zh, zl, y, core)
    to_x_up = device(x_up, zh, zl, y, core)
    to_x_dn = device(x_dn, zh, zl, y, core)
    to_core = device(x, zh, zl, y, 1 - core)

    def tensor_peer(step):
        return (dp, (tensor + step) % 8, core)

    barrier = pltpu.get_barrier_semaphore()
    for peer in [to_z_hi, to_x_up, to_x_dn, to_core] + [tensor_peer(s) for s in range(1, 8)]:
        pl.semaphore_signal(barrier, inc=1, device_id=peer, device_id_type=MESH)

    def first_row(piece):
        return pl.multiple_of(((piece + core * (PIECES // 2)) % PIECES) * rows, rows)

    def head_of(slot):
        ring = (y + 2) % 4 if slot < 2 else y_up if slot < 4 else y_dn if slot < 6 else y
        return (slot % 2) * 4 + ring

    def tok_copy(piece):
        return pltpu.make_async_copy(
            tok_ref.at[pl.ds(pl.multiple_of(piece * rows, rows), rows)],
            tok.at[pl.ds(pl.multiple_of(core * half + piece * rows, rows), rows)],
            tok_sem.at[piece],
        )

    def w_copy(slot):
        return pltpu.make_async_copy(w_ref.at[head_of(slot)], wgt.at[slot], w_sem.at[slot])

    def core_copy():
        return pltpu.make_async_remote_copy(
            src_ref=tok_ref,
            dst_ref=tok.at[pl.ds(pl.multiple_of(core * half, half), half)],
            send_sem=core_sem.at[0], recv_sem=core_sem.at[1],
            device_id=to_core, device_id_type=MESH,
        )

    def text_copy(step):
        return pltpu.make_async_remote_copy(
            src_ref=text_ref, dst_ref=text_out_ref.at[tensor],
            send_sem=text_send.at[step - 1], recv_sem=text_recv.at[step - 1],
            device_id=tensor_peer(step), device_id_type=MESH,
        )

    def text_own():
        return pltpu.make_async_copy(text_ref, text_out_ref.at[tensor], loc_sem.at[PIECES])

    def remote(kind, piece, src, dst, peer):
        return pltpu.make_async_remote_copy(
            src_ref=src, dst_ref=dst,
            send_sem=send.at[kind, piece], recv_sem=recv.at[kind, piece],
            device_id=peer, device_id_type=MESH,
        )

    def y1_copy(way, piece):
        at = pl.ds(first_row(piece), rows)
        return remote(way, piece, part.at[way, at], from_y1.at[way, at], (to_y_up, to_y_dn)[way])

    def y2_copy(way, piece):
        at = pl.ds(first_row(piece), rows)
        src = part.at[pl.ds(2 + 2 * way, 2), at]
        return remote(2 + way, piece, src, from_y2.at[pl.ds(2 * way, 2), at], (to_y_up, to_y_dn)[way])

    def z_copy(piece):
        at = pl.ds(first_row(piece), rows)
        return remote(4, piece, part.at[7 - zl, at], from_z.at[at], to_z_lo)

    def own_copy(way, piece):
        at = pl.ds(first_row(piece), rows)
        return remote(5 + way, piece, done.at[at], out_ref.at[dp, at], (to_z_hi, to_x_up, to_x_dn)[way])

    def own_local(piece):
        at = pl.ds(first_row(piece), rows)
        return pltpu.make_async_copy(done.at[at], out_ref.at[dp, at], loc_sem.at[piece])

    def pair_copy(way, piece):
        at = pl.ds(first_row(piece), rows)
        pair = x * 2 + 1 - zh
        return remote(8 + way, piece, out_ref.at[pair, at], out_ref.at[pair, at], (to_x_up, to_x_dn)[way])

    def forward_copy(way, piece):
        at = pl.ds(first_row(piece), rows)
        image = (x_dn * 2 + zh, x_up * 2 + 1 - zh)[way]
        return remote(10 + way, piece, out_ref.at[image, at], out_ref.at[image, at], (to_x_up, to_x_dn)[way])

    for slot in range(8):
        w_copy(slot).start()

    def start_tok(piece, carry):
        tok_copy(piece).start()
        return carry

    lax.fori_loop(0, PIECES // 2, start_tok, 0)
    text_own().start()
    pl.semaphore_wait(barrier, 11)
    core_copy().start()

    @pl.when(core == 0)
    def _():
        for step in range(1, 8):
            text_copy(step).start()

    def step_fn(it, carry):
        @pl.when(it < PIECES)
        def _():
            piece = it

            @pl.when(piece < PIECES // 2)
            def _():
                tok_copy(piece).wait()

            @pl.when(piece == PIECES // 2)
            def _():
                core_copy().wait_recv()

            at = pl.ds(first_row(piece), rows)
            for slot in range(8):
                @pl.when(it == 0)
                def _():
                    w_copy(slot).wait()

                part[slot, at, :] = jnp.dot(
                    tok[at, :], wgt[slot], preferred_element_type=F32
                ).astype(BF)
                if slot < 2:
                    y1_copy(slot, piece).start()

        @pl.when((it >= 1) & (it < PIECES + 1))
        def _():
            piece = it - 1
            at = pl.ds(first_row(piece), rows)
            for way, slot in ((0, 2), (1, 5)):
                y1_copy(way, piece).wait_recv()
                part[slot, at, :] = (
                    part[slot, at, :].astype(F32) + from_y1[way, at, :].astype(F32)
                ).astype(BF)
                y2_copy(way, piece).start()

        @pl.when((it >= 2) & (it < PIECES + 2))
        def _():
            piece = it - 2
            at = pl.ds(first_row(piece), rows)
            for way in range(2):
                y2_copy(way, piece).wait_recv()
            part[7 - zl, at, :] = (
                part[7 - zl, at, :].astype(F32)
                + from_y2[1 - zl, at, :].astype(F32)
                + from_y2[3 - zl, at, :].astype(F32)
            ).astype(BF)
            z_copy(piece).start()

        @pl.when((it >= 3) & (it < PIECES + 3))
        def _():
            piece = it - 3
            at = pl.ds(first_row(piece), rows)
            z_copy(piece).wait_recv()
            total = (
                part[6 + zl, at, :].astype(F32)
                + from_y2[zl, at, :].astype(F32)
                + from_y2[2 + zl, at, :].astype(F32)
                + from_z[at, :].astype(F32)
            )
            keys = total[:, :128]
            keys = keys * lax.rsqrt(jnp.mean(keys * keys, axis=-1, keepdims=True) + 1e-05)
            done[at, 0:128] = (keys * gain_ref[...]).astype(BF)
            done[at, 128:256] = total[:, 128:].astype(BF)
            for way in range(3):
                own_copy(way, piece).start()
            own_local(piece).start()

        @pl.when((it >= 4) & (it < PIECES + 4))
        def _():
            piece = it - 4
            own_copy(0, piece).wait_recv()
            for way in range(2):
                pair_copy(way, piece).start()

        @pl.when(it >= 5)
        def _():
            piece = it - 5
            own_copy(1, piece).wait_recv()
            pair_copy(1, piece).wait_recv()
            for way in range(2):
                forward_copy(way, piece).start()

        return carry

    lax.fori_loop(0, PIECES + 5, step_fn, 0)

    def finish(piece, carry):
        for way in range(2):
            y1_copy(way, piece).wait_send()
            y2_copy(way, piece).wait_send()
            pair_copy(way, piece).wait_send()
            forward_copy(way, piece).wait()
        for way in range(3):
            own_copy(way, piece).wait_send()
        z_copy(piece).wait_send()
        own_local(piece).wait()
        own_copy(2, piece).wait_recv()
        pair_copy(0, piece).wait_recv()
        return carry

    lax.fori_loop(0, PIECES, finish, 0)
    core_copy().wait_send()
    text_own().wait()

    @pl.when(core == 0)
    def _():
        for step in range(1, 8):
            text_copy(step).wait()


def image_pairs(tokens, weights, gain, text):
    half, width = tokens.shape
    heads = weights.shape[0]
    patches = half * 2
    any_spec = pl.BlockSpec(memory_space=pl.ANY)
    return pl.pallas_call(
        kv_kernel,
        name="kv",
        out_shape=[
            jax.ShapeDtypeStruct((8, patches, 256), BF),
            jax.ShapeDtypeStruct((8,) + text.shape, BF),
        ],
        in_specs=[any_spec, any_spec, pl.BlockSpec(memory_space=pltpu.VMEM), any_spec],
        out_specs=[any_spec, any_spec],
        scratch_shapes=[
            pltpu.VMEM((patches, width), BF),
            pltpu.VMEM((heads, width, 256), BF),
            pltpu.VMEM((heads, patches, 256), BF),
            pltpu.VMEM((2, patches, 256), BF),
            pltpu.VMEM((4, patches, 256), BF),
            pltpu.VMEM((patches, 256), BF),
            pltpu.VMEM((patches, 256), BF),
            pltpu.SemaphoreType.DMA((PIECES // 2,)),
            pltpu.SemaphoreType.DMA((8,)),
            pltpu.SemaphoreType.DMA((PIECES + 1,)),
            pltpu.SemaphoreType.DMA((2,)),
            pltpu.SemaphoreType.DMA((7,)),
            pltpu.SemaphoreType.DMA((7,)),
            pltpu.SemaphoreType.DMA((12, PIECES)),
            pltpu.SemaphoreType.DMA((12, PIECES)),
        ],
        compiler_params=pltpu.CompilerParams(
            collective_id=0, has_side_effects=True, vmem_limit_bytes=58 * 2**20
        ),
        cost_estimate=pl.CostEstimate(
            flops=2 * patches * width * heads * 256, bytes_accessed=40 * 2**20, transcendentals=0
        ),
    )(tokens, weights, gain, text)


Q_STEPS = 4
TILE_STEPS = 4
OUT_STEPS = 4
KEY_PARTS = ((0, 512), (512, 512), (1024, 576))


def layer_kernel(
    meta_ref, h_ref, gain_ref, wq_ref, qgain_ref, pair_ref, wo_ref, out_ref, acc, sq, query, total, norm, att
):
    step = pl.program_id(0)

    @pl.when(step < Q_STEPS)
    def _():
        @pl.when(step == 0)
        def _():
            acc[...] = jnp.zeros_like(acc)
            sq[...] = jnp.zeros_like(sq)

        for block in range(2):
            values = h_ref[block].astype(F32)
            sq[...] += jnp.sum(values * values, axis=-1, keepdims=True)
            scaled = (values * gain_ref[step * 2 + block]).astype(BF)
            acc[...] += jnp.dot(
                scaled, wq_ref[block * 1024:(block + 1) * 1024, :], preferred_element_type=F32
            )

        @pl.when(step == Q_STEPS - 1)
        def _():
            inverse = lax.rsqrt(sq[:, :1] * (1.0 / 8192.0) + 1e-05)
            for head in range(4):
                one = acc[:, head * 128:(head + 1) * 128] * inverse
                one = one * lax.rsqrt(jnp.mean(one * one, axis=-1, keepdims=True) + 1e-05)
                query[head * 128:(head + 1) * 128, :] = (one * qgain_ref[...] * 128.0 ** -0.5).astype(BF)
            total[...] = jnp.zeros_like(total)
            norm[...] = jnp.zeros_like(norm)

    tile = step - Q_STEPS

    @pl.when((tile >= 0) & (tile < TILE_STEPS) & (meta_ref[jnp.clip(tile, 0, 3) + 8] > 0))
    def _():
        for start, size in KEY_PARTS:
            scores = lax.dot_general(
                query[...], pair_ref[0, start:start + size, 0:128],
                (((1,), (1,)), ((), ())), preferred_element_type=F32,
            )
            expo = jnp.exp(scores)
            norm[...] += jnp.sum(expo, axis=-1, keepdims=True)
            total[...] += jnp.dot(
                expo.astype(BF), pair_ref[0, start:start + size, 128:256], preferred_element_type=F32
            )

    @pl.when(step >= Q_STEPS + TILE_STEPS)
    def _():
        @pl.when(step == Q_STEPS + TILE_STEPS)
        def _():
            for head in range(4):
                at = slice(head * 128, (head + 1) * 128)
                att[:, at] = (total[at, :] / norm[at, :1]).astype(BF)

        for block in range(2):
            out_ref[block] = jnp.dot(
                att[...], wo_ref[:, block * 1024:(block + 1) * 1024], preferred_element_type=F32
            ).astype(BF)


def layer_part(meta, hidden, gain, w_query, q_gain, pairs, w_out):
    attn_end = Q_STEPS + TILE_STEPS

    def out_step(i):
        return jnp.clip(i - attn_end, 0, OUT_STEPS - 1)

    def tile_map(i, m):
        j = jnp.clip(i - Q_STEPS, 0, TILE_STEPS - 1)
        return (m[j], m[j + 4], 0)

    return pl.pallas_call(
        layer_kernel,
        name="layer",
        out_shape=jax.ShapeDtypeStruct((8, 128, 1024), BF),
        grid_spec=pltpu.PrefetchScalarGridSpec(
            num_scalar_prefetch=1,
            grid=(Q_STEPS + TILE_STEPS + OUT_STEPS,),
            in_specs=[
                pl.BlockSpec((2, 128, 1024), lambda i, m: (jnp.minimum(i, Q_STEPS - 1), 0, 0)),
                pl.BlockSpec((8, 1, 1024), lambda i, m: (0, 0, 0)),
                pl.BlockSpec((2048, 512), lambda i, m: (jnp.minimum(i, Q_STEPS - 1), 0)),
                pl.BlockSpec((1, 128), lambda i, m: (0, 0)),
                pl.BlockSpec((1, TILE_TOK, 256), tile_map),
                pl.BlockSpec((512, 2048), lambda i, m: (0, out_step(i))),
            ],
            out_specs=pl.BlockSpec((2, 128, 1024), lambda i, m: (out_step(i), 0, 0)),
            scratch_shapes=[
                pltpu.VMEM((128, 512), F32),
                pltpu.VMEM((128, 128), F32),
                pltpu.VMEM((512, 128), BF),
                pltpu.VMEM((512, 128), F32),
                pltpu.VMEM((512, 128), F32),
                pltpu.VMEM((128, 512), BF),
            ],
        ),
        compiler_params=pltpu.CompilerParams(vmem_limit_bytes=48 * 2**20),
        cost_estimate=pl.CostEstimate(flops=4 * 10**9, bytes_accessed=20 * 2**20, transcendentals=3 * 10**6),
    )(meta, hidden, gain, w_query, q_gain, pairs, w_out)


def sum_kernel(
    first_core, second_core, part_ref, resid_ref, gate_ref, upd_ref, next_ref, came, rs_send, rs_recv, ag_send, ag_recv
):
    dp = lax.axis_index("dp")
    tensor = lax.axis_index("tensor")
    core = lax.axis_index("section")

    barrier = pltpu.get_barrier_semaphore()
    for step in range(8):
        peer = (tensor + step) % 8
        if step:
            pl.semaphore_signal(barrier, inc=1, device_id=(dp, peer, core), device_id_type=MESH)
        pl.semaphore_signal(barrier, inc=1, device_id=(dp, peer, 1 - core), device_id_type=MESH)
    pl.semaphore_wait(barrier, 15)

    def rs_copy(step):
        peer = (tensor + step) % 8
        return pltpu.make_async_remote_copy(
            src_ref=part_ref.at[peer], dst_ref=came.at[step - 1],
            send_sem=rs_send.at[step - 1], recv_sem=rs_recv.at[step - 1],
            device_id=(dp, peer, core), device_id_type=MESH,
        )

    def ag_copy(step):
        return pltpu.make_async_remote_copy(
            src_ref=upd_ref, dst_ref=next_ref.at[tensor],
            send_sem=ag_send.at[step], recv_sem=ag_recv.at[step],
            device_id=(dp, (tensor + step) % 8, 1 - core), device_id_type=MESH,
        )

    def reduce():
        for step in range(1, 8):
            rs_copy(step).start()
        total = part_ref[tensor].astype(F32)
        for step in range(1, 8):
            rs_copy(step).wait_recv()
            total = total + came[step - 1].astype(F32)
        upd_ref[...] = (resid_ref[...].astype(F32) + gate_ref[...] * total).astype(BF)

    if first_core and second_core:
        reduce()
    elif first_core:
        pl.when(core == 0)(reduce)
    else:
        pl.when(core == 1)(reduce)
    if first_core:
        @pl.when(core == 0)
        def _():
            for step in range(8):
                ag_copy(step).start()
            for step in range(8):
                ag_copy(step).wait_send()

        @pl.when(core == 1)
        def _():
            for step in range(8):
                ag_copy(step).wait_recv()

    def drain():
        for step in range(1, 8):
            rs_copy(step).wait_send()

    if first_core and second_core:
        drain()
    elif first_core:
        pl.when(core == 0)(drain)
    else:
        pl.when(core == 1)(drain)


def sum_and_pass(tick, first_core, second_core, part, resid, gate):
    vmem = pl.BlockSpec(memory_space=pltpu.VMEM)
    return pl.pallas_call(
        functools.partial(sum_kernel, first_core, second_core),
        name="sum" + str(tick),
        out_shape=[jax.ShapeDtypeStruct((128, 1024), BF), jax.ShapeDtypeStruct((8, 128, 1024), BF)],
        in_specs=[vmem] * 3,
        out_specs=[vmem] * 2,
        scratch_shapes=[
            pltpu.VMEM((7, 128, 1024), BF),
            pltpu.SemaphoreType.DMA((7,)),
            pltpu.SemaphoreType.DMA((7,)),
            pltpu.SemaphoreType.DMA((8,)),
            pltpu.SemaphoreType.DMA((8,)),
        ],
        compiler_params=pltpu.CompilerParams(
            collective_id=1 + tick, has_side_effects=True, vmem_limit_bytes=48 * 2**20
        ),
    )(part, resid, gate)


def tile_plan(chosen, valid_tiles):
    first, second = chosen[0], chosen[1]
    two = valid_tiles[first] > 1
    other = second != first
    two_other = other & (valid_tiles[second] > 1)
    one = jnp.int32(1)
    zero = jnp.int32(0)
    last_tile = jnp.where(two, one, zero)
    image = [first, first, jnp.where(other, second, first)]
    image.append(image[2])
    third_tile = jnp.where(other, zero, last_tile)
    tile = [zero, last_tile, third_tile, jnp.where(two_other, one, third_tile)]
    use = [one, last_tile, jnp.where(other, one, zero), jnp.where(two_other, one, zero)]
    return jnp.stack(image + tile + use).astype(jnp.int32)


def local(
    text_hidden,
    image_tokens,
    attn_gain,
    w_query,
    w_keyval,
    q_gain,
    k_gain,
    w_out,
    gate,
    image_choice,
    valid_tiles,
):
    core = lax.axis_index("section")
    tensor = lax.axis_index("tensor")
    text = text_hidden[:, 0]
    weights = jnp.transpose(w_keyval[0], (1, 0, 2))
    pairs, text_all = image_pairs(image_tokens[0], weights, k_gain, text)
    gate_row = jnp.broadcast_to(jnp.tanh(gate)[:, None], (1, 1024))
    gain = attn_gain.reshape(8, 1, 1024)
    received = None
    results = []
    for tick in range(3):
        own = text_all[:, min(tick, 1)]
        resid = text[min(tick, 1)]
        if received is None:
            hidden = own
        else:
            hidden = jnp.where(core == 0, own, received)
            resid = jnp.where(core == 0, resid, lax.dynamic_index_in_dim(received, tensor, 0, keepdims=False))
        chosen = jnp.where(core == 0, image_choice[min(tick, 1), 0], image_choice[max(tick - 1, 0), 0])
        meta = tile_plan(chosen, valid_tiles)
        part = layer_part(meta, hidden, gain, w_query[0], q_gain, pairs, w_out[0])
        updated, received = sum_and_pass(tick, tick < 2, tick > 0, part, resid, gate_row)
        results.append(updated)
    slots = [jnp.where(core == 0, results[batch], results[batch + 1]) for batch in range(2)]
    return jnp.stack(slots)[None, :, None]


def solution(mesh):
    placed = (
        P(None, "dp", None, "tensor"),
        P("dp", "section", "tensor"),
        P("section", None),
        P("section", None, "tensor"),
        P("section", "tensor", None, None),
        P("section", None),
        P("section", None),
        P("section", "tensor", None),
        P("section"),
        P(None, "dp", None),
        P(),
    )
    return jax.shard_map(
        local,
        mesh=mesh,
        in_specs=placed,
        out_specs=P("section", None, "dp", None, "tensor"),
        check_vma=False,
    )
```

time: 826 us -> 379 us (0.46); the launches traced: 813 us -> 378 us
  waiting for transfers between devices: 587 us -> 0 us
  Pallas kernels: 0 us -> 335 us
  matrix products: 70.9 us -> 0 us
  local copies, waits for them, and re-layouts: 79.7 us -> 15.4 us
  other arithmetic: 42.9 us -> 3.58 us
    pallas_call x0 -> x7, Pallas kernels: none -> 335 us  [the longest x1 158 us: image_pairs(): pl.pallas_call(kv_kernel, name='kv', out_shape=[jax.ShapeDtypeStruct((8,...]
    psum x3 -> x0, waiting for transfers between devices: 235 us -> none  [local(): lax.psum(proj.reshape(seqs_dev, seq_len, width_full).astype(jnp.bfloat16)...]
    all_gather x4 -> x0, waiting for transfers between devices: 214 us -> none  [the longest x1 152 us: local(): all_pairs = lax.all_gather(local_pairs, 'dp', axis=1, tiled=True)]
    reduce_scatter x1 -> x0, waiting for transfers between devices: 137 us -> none  [local(): lax.psum_scatter(jnp.einsum('pd,dkc->kpc', flat_images, block, preferred_...]
    dot_general x13 -> x0, matrix products: 70.9 us -> none  [the longest x1 21.1 us: local(): jnp.einsum('pd,dkc->kpc', flat_images, block, preferred_element_type=jnp....]
    dynamic_slice x8 -> x1, local copies, waits for them, and re-layouts: 64.4 us -> 1.58 us  [tile_plan(): two_other = other & (valid_tiles[second] > 1)]
    reduce_sum x10 -> x0, other arithmetic: 20.1 us -> none  [the longest x3 10.9 us: one_sequence(): jnp.sum(expo, axis=-1, keepdims=True)]
    convert_element_type x4 -> x0, other arithmetic: 13 us -> none  [the longest x2 7.84 us: local(): (hidden.astype(jnp.float32) + gate_value * total).astype(jnp.bfloat16)]
  transfers between devices with their start and end apart: 10 -> 0, of which waited for: 8 -> 0; matrix products, arithmetic and copies ran while one was open for 6% -> 0% of each run, Pallas kernels for 0% -> 0%
where the time goes in v1:
time: 379 us; the launch traced here: 378 us
  Pallas kernels  335 us (88%)
  between operations  24.6 us (6%)
  local copies, waits for them, and re-layouts  15.4 us (4%)
    pallas_call x1, Pallas kernels, image_pairs(): pl.pallas_call(kv_kernel, name='kv', out_shape=[jax.ShapeDtypeStruct((8,...  158 us
    pallas_call x3, Pallas kernels, sum_and_pass(): pl.pallas_call(functools.partial(sum_kernel, first_core, second_core), na...  130 us
    pallas_call x3, Pallas kernels, layer_part(): pl.pallas_call(layer_kernel, name='layer', out_shape=jax.ShapeDtypeStruct...  47.2 us

profile of v1, /device:TPU:1, one launch (start us, length us, event | category | flops | bytes accessed | tf_op | source)
XLA Modules:
  0.0 378.4 jit_solution(4568091349056024392)
XLA Ops:
  0.7 0.7 broadcast_select_fusion.2
  1.4 0.6 fusion.2
  8.3 1.4 fusion
  23.0 1.6 fusion.1
  28.6 1.5 stack.90.meta_ref
  30.1 1.3 stack.83.meta_ref
  31.4 1.4 stack.77.meta_ref
  32.8 1.0 slice_bitcast_fusion.2.resid_ref
  33.8 5.0 %copy.23 = bf16[1,1024,8,256]{3,1,2,0:T(8,128)(2,1)} copy(bf16[1,1024,8,256]{3,2,1,0:T(8,128)(2,1)} %param.15) | data formatting | bytes 8388608 | tf_op args[4]
  38.8 157.8 %kv.1 = (bf16[8,3200,256]{2,1,0:T(8,128)(2,1)}, bf16[8,2,128,1024]{3,2,1,0:T(8,128)(2,1)}) custom-call(bf16[1600,1024]{1,0:T(8,128)(2,1)} %bitcast.77, bf16[8,1024,256]{2,1,0:T(8,128)(2,1)} %bitcast.75, f32[1,128]{1,0:T(1,128)} %gain_ref.1, bf16[2,128,1024]{2,1,0:T(8,128)(2,1)} %bitcast.76), custom_call_target="tpu_custom_call" | custom-call | flops 13421772800 | bytes 41943040 | tf_op jit(solution)/shard_map/kv/pallas_call | solution.py:261
  196.6 0.0 copy-start
  196.6 0.0 copy-start.1
  196.6 1.8 slice_bitcast_fusion.1.h_ref
  198.4 0.0 copy-start.3
  198.4 15.9 %layer.3.part_ref = bf16[8,128,1024]{2,1,0:T(8,128)(2,1)S(1)} custom-call(s32[12]{0:T(128)S(1)} %stack.77.meta_ref, bf16[8,128,1024]{2,1,0:T(8,128)(2,1)S(1)} %slice_bitcast_fusion.1.h_ref, f32[8,1,1024]{2,1,0:T(1,128)S(1)} %bitcast.66, bf16[8192,512]{1,0:T(8,128)(2,1)} %bitcast.69, f32[1,128]{1,0:T(1,128)S(1)} %copy-done.1, ...), custom_call_target="tpu_custom_call" | custom-call | flops 4000000000 | bytes 20971520 | tf_op jit(solution)/shard_map/layer/pallas_call | solution.py:371
  214.3 59.4 %sum0.1 = (bf16[128,1024]{1,0:T(8,128)(2,1)S(1)}, bf16[8,128,1024]{2,1,0:T(8,128)(2,1)S(1)}) custom-call(bf16[8,128,1024]{2,1,0:T(8,128)(2,1)S(1)} %layer.3.part_ref, bf16[128,1024]{1,0:T(8,128)(2,1)S(1)} %slice_bitcast_fusion.2.resid_ref, f32[1,1024]{1,0:T(1,128)S(1)} %broadcast_in_dim.12.gate_ref), custom_call_target="tpu_custom_call" | custom-call | tf_op jit(solution)/shard_map/sum0/pallas_call | solution.py:473
  273.9 1.0 broadcast_select_fusion.1.h_ref
  274.8 15.6 %layer.4.part_ref = bf16[8,128,1024]{2,1,0:T(8,128)(2,1)S(1)} custom-call(s32[12]{0:T(128)S(1)} %stack.83.meta_ref, bf16[8,128,1024]{2,1,0:T(8,128)(2,1)S(1)} %broadcast_select_fusion.1.h_ref, f32[8,1,1024]{2,1,0:T(1,128)S(1)} %bitcast.67, bf16[8192,512]{1,0:T(8,128)(2,1)} %bitcast.70, f32[1,128]{1,0:T(1,128)S(1)} %copy-done.1, ...), custom_call_target="tpu_custom_call" | custom-call | flops 4000000000 | bytes 20971520 | tf_op jit(solution)/shard_map/layer/pallas_call | solution.py:371
  290.4 49.5 %sum1.1 = (bf16[128,1024]{1,0:T(8,128)(2,1)S(1)}, bf16[8,128,1024]{2,1,0:T(8,128)(2,1)S(1)}) custom-call(bf16[8,128,1024]{2,1,0:T(8,128)(2,1)S(1)} %layer.4.part_ref, bf16[128,1024]{1,0:T(8,128)(2,1)S(1)} %bitcast_select_fusion.1.resid_ref, f32[1,1024]{1,0:T(1,128)S(1)} %broadcast_in_dim.12.gate_ref), custom_call_target="tpu_custom_call" | custom-call | tf_op jit(solution)/shard_map/sum1/pallas_call | solution.py:473
  339.9 1.0 broadcast_select_fusion.h_ref
  340.9 15.7 %layer.5.part_ref = bf16[8,128,1024]{2,1,0:T(8,128)(2,1)S(1)} custom-call(s32[12]{0:T(128)S(1)} %stack.90.meta_ref, bf16[8,128,1024]{2,1,0:T(8,128)(2,1)S(1)} %broadcast_select_fusion.h_ref, f32[8,1,1024]{2,1,0:T(1,128)S(1)} %bitcast.68, bf16[8192,512]{1,0:T(8,128)(2,1)} %bitcast.71, f32[1,128]{1,0:T(1,128)S(1)} %copy-done.1, ...), custom_call_target="tpu_custom_call" | custom-call | flops 4000000000 | bytes 20971520 | tf_op jit(solution)/shard_map/layer/pallas_call | solution.py:371
  356.6 20.8 %sum2.1 = (bf16[128,1024]{1,0:T(8,128)(2,1)S(1)}, bf16[8,128,1024]{2,1,0:T(8,128)(2,1)}) custom-call(bf16[8,128,1024]{2,1,0:T(8,128)(2,1)S(1)} %layer.5.part_ref, bf16[128,1024]{1,0:T(8,128)(2,1)S(1)} %bitcast_select_fusion.resid_ref, f32[1,1024]{1,0:T(1,128)S(1)} %broadcast_in_dim.12.gate_ref), custom_call_target="tpu_custom_call" | custom-call | tf_op jit(solution)/shard_map/sum2/pallas_call | solution.py:473
  377.5 0.1 select_bitcast_fusion.1
  377.5 0.8 maximum_bitcast_fusion
  (8 shorter events, 0.1 us)
Async XLA Ops:
  196.6 1.8 copy-start
  196.6 1.8 copy-start.1
  198.4 75.4 %copy-start.3 = (bf16[2,1,128,1024]{3,2,1,0:T(8,128)(2,1)S(1)}, bf16[2,1,128,1024]{3,2,1,0:T(8,128)(2,1)}, u32[]{:S(2)}) copy-start(bf16[2,1,128,1024]{3,2,1,0:T(8,128)(2,1)} %param.11) | copy-start | bytes 1572868
  198.4 75.4 %copy-start.2 = (bf16[8,2,128,1024]{3,2,1,0:T(8,128)(2,1)S(1)}, bf16[8,2,128,1024]{3,2,1,0:T(8,128)(2,1)}, u32[]{:S(2)}) copy-start(bf16[8,2,128,1024]{3,2,1,0:T(8,128)(2,1)} %get-tuple-element.12) | copy-start | bytes 12582916

commit v2 on v1

v2 whole, which is shorter than its diff:
```python
import functools

import jax
import jax.numpy as jnp
from jax import lax
from jax.experimental import pallas as pl
from jax.experimental.pallas import tpu as pltpu
from jax.sharding import PartitionSpec as P

TILE_TOK = 1600
PIECES = 20
EARLY = (1, 3, 4)
LATE = (2, 5, 6, 7)
MESH = pl.DeviceIdType.MESH
BF = jnp.bfloat16
F32 = jnp.float32


def position():
    dp = lax.axis_index("dp")
    tensor = lax.axis_index("tensor")
    return dp // 2, dp % 2, tensor // 4, tensor % 4, lax.axis_index("section")


def device(x, zh, zl, y, core):
    return (x * 2 + zh, zl * 4 + y, core)


def kv_kernel(
    tok_ref, w_ref, gain_ref, text_ref, wq_ref, wo_ref, par_ref,
    pairs_ref, text_out_ref, wq_out_ref, wo_out_ref, par_out_ref,
    tok, wgt, part, from_y1, from_y2, from_z, done,
    tok_sem, w_sem, loc_sem, core_send, core_recv, text_send, text_recv, send, recv,
):
    x, zh, zl, y, core = position()
    dp = x * 2 + zh
    tensor = zl * 4 + y
    half = tok_ref.shape[0]
    out_ref = pairs_ref.at[core]
    rows = half * 2 // PIECES
    y_up, y_dn = (y + 1) % 4, (y + 3) % 4
    x_up, x_dn = (x + 1) % 4, (x + 3) % 4
    to_y_up = device(x, zh, zl, y_up, core)
    to_y_dn = device(x, zh, zl, y_dn, core)
    to_z_lo = device(x, zh, 1 - zl, y, core)
    to_z_hi = device(x, 1 - zh, zl, y, core)
    to_x_up = device(x_up, zh, zl, y, core)
    to_x_dn = device(x_dn, zh, zl, y, core)
    to_core = device(x, zh, zl, y, 1 - core)

    def tensor_peer(step):
        return (dp, (tensor + step) % 8, core)

    barrier = pltpu.get_barrier_semaphore()
    for peer in [to_z_hi, to_x_up, to_x_dn, to_core] + [tensor_peer(s) for s in range(1, 8)]:
        pl.semaphore_signal(barrier, inc=1, device_id=peer, device_id_type=MESH)

    def first_row(piece):
        return pl.multiple_of(((piece + core * (PIECES // 2)) % PIECES) * rows, rows)

    def head_of(slot):
        ring = (y + 2) % 4 if slot < 2 else y_up if slot < 4 else y_dn if slot < 6 else y
        return (slot % 2) * 4 + ring

    def tok_copy(piece):
        return pltpu.make_async_copy(
            tok_ref.at[pl.ds(pl.multiple_of(piece * rows, rows), rows)],
            tok.at[pl.ds(pl.multiple_of(core * half + piece * rows, rows), rows)],
            tok_sem.at[piece],
        )

    def w_copy(slot):
        return pltpu.make_async_copy(w_ref.at[head_of(slot)], wgt.at[slot], w_sem.at[slot])

    def to_other_core(kind):
        src, dst = (
            (tok_ref, tok.at[pl.ds(pl.multiple_of(core * half, half), half)]),
            (par_ref, par_out_ref),
            (wq_ref, wq_out_ref),
            (wo_ref, wo_out_ref),
        )[kind]
        return pltpu.make_async_remote_copy(
            src_ref=src, dst_ref=dst, send_sem=core_send.at[kind], recv_sem=core_recv.at[kind],
            device_id=to_core, device_id_type=MESH,
        )

    def text_copy(step):
        return pltpu.make_async_remote_copy(
            src_ref=text_ref.at[core], dst_ref=text_out_ref.at[tensor],
            send_sem=text_send.at[step - 1], recv_sem=text_recv.at[step - 1],
            device_id=tensor_peer(step), device_id_type=MESH,
        )

    def remote(kind, piece, src, dst, peer):
        return pltpu.make_async_remote_copy(
            src_ref=src, dst_ref=dst,
            send_sem=send.at[kind, piece], recv_sem=recv.at[kind, piece],
            device_id=peer, device_id_type=MESH,
        )

    def y1_copy(way, piece):
        at = pl.ds(first_row(piece), rows)
        return remote(way, piece, part.at[way, at], from_y1.at[way, at], (to_y_up, to_y_dn)[way])

    def y2_copy(way, piece):
        at = pl.ds(first_row(piece), rows)
        src = part.at[pl.ds(2 + 2 * way, 2), at]
        return remote(2 + way, piece, src, from_y2.at[pl.ds(2 * way, 2), at], (to_y_up, to_y_dn)[way])

    def z_copy(piece):
        at = pl.ds(first_row(piece), rows)
        return remote(4, piece, part.at[7 - zl, at], from_z.at[at], to_z_lo)

    def own_copy(way, piece):
        at = pl.ds(first_row(piece), rows)
        return remote(5 + way, piece, done.at[at], out_ref.at[dp, at], (to_z_hi, to_x_up, to_x_dn)[way])

    def own_local(piece):
        at = pl.ds(first_row(piece), rows)
        return pltpu.make_async_copy(done.at[at], out_ref.at[dp, at], loc_sem.at[piece])

    def pair_copy(way, piece):
        at = pl.ds(first_row(piece), rows)
        pair = x * 2 + 1 - zh
        return remote(8 + way, piece, out_ref.at[pair, at], out_ref.at[pair, at], (to_x_up, to_x_dn)[way])

    def forward_copy(way, piece):
        at = pl.ds(first_row(piece), rows)
        image = (x_dn * 2 + zh, x_up * 2 + 1 - zh)[way]
        return remote(10 + way, piece, out_ref.at[image, at], out_ref.at[image, at], (to_x_up, to_x_dn)[way])

    def mirror(kind, image, piece):
        at = pl.ds(first_row(piece), rows)
        src = done.at[at] if kind == 0 else out_ref.at[image, at]
        return remote(12 + kind, piece, src, out_ref.at[image, at], to_core)

    def mirrors(piece):
        ring = ((x, zh), (x, 1 - zh), (x_dn, zh), (x_up, zh), (x_dn, 1 - zh), (x_up, 1 - zh))
        images = [a * 2 + b for a, b in ring] + [((x + 2) % 4) * 2 + zh, ((x + 2) % 4) * 2 + 1 - zh]
        return [functools.partial(mirror, kind, image, piece) for kind, image in enumerate(images)]

    for slot in range(8):
        w_copy(slot).start()

    def start_tok(piece, carry):
        tok_copy(piece).start()
        return carry

    lax.fori_loop(0, PIECES // 2, start_tok, 0)
    pl.semaphore_wait(barrier, 11)
    to_other_core(0).start()
    for step in EARLY:
        text_copy(step).start()
    for kind in range(1, 4):
        to_other_core(kind).start()

    def step_fn(it, carry):
        @pl.when(it < PIECES)
        def _():
            piece = it

            @pl.when(piece < PIECES // 2)
            def _():
                tok_copy(piece).wait()

            @pl.when(piece == PIECES // 2)
            def _():
                to_other_core(0).wait_recv()

            at = pl.ds(first_row(piece), rows)
            for slot in range(8):
                @pl.when(it == 0)
                def _():
                    w_copy(slot).wait()

                part[slot, at, :] = jnp.dot(
                    tok[at, :], wgt[slot], preferred_element_type=F32
                ).astype(BF)
                if slot < 2:
                    y1_copy(slot, piece).start()

        @pl.when((it >= 1) & (it < PIECES + 1))
        def _():
            piece = it - 1
            at = pl.ds(first_row(piece), rows)
            for way, slot in ((0, 2), (1, 5)):
                y1_copy(way, piece).wait_recv()
                part[slot, at, :] = (
                    part[slot, at, :].astype(F32) + from_y1[way, at, :].astype(F32)
                ).astype(BF)
                y2_copy(way, piece).start()

            @pl.when(piece == PIECES - 1)
            def _():
                for step in LATE:
                    text_copy(step).start()

        @pl.when((it >= 2) & (it < PIECES + 2))
        def _():
            piece = it - 2
            at = pl.ds(first_row(piece), rows)
            for way in range(2):
                y2_copy(way, piece).wait_recv()
            part[7 - zl, at, :] = (
                part[7 - zl, at, :].astype(F32)
                + from_y2[1 - zl, at, :].astype(F32)
                + from_y2[3 - zl, at, :].astype(F32)
            ).astype(BF)
            z_copy(piece).start()

        @pl.when((it >= 3) & (it < PIECES + 3))
        def _():
            piece = it - 3
            at = pl.ds(first_row(piece), rows)
            z_copy(piece).wait_recv()
            total = (
                part[6 + zl, at, :].astype(F32)
                + from_y2[zl, at, :].astype(F32)
                + from_y2[2 + zl, at, :].astype(F32)
                + from_z[at, :].astype(F32)
            )
            keys = total[:, :128]
            keys = keys * lax.rsqrt(jnp.mean(keys * keys, axis=-1, keepdims=True) + 1e-05)
            done[at, 0:128] = (keys * gain_ref[...]).astype(BF)
            done[at, 128:256] = total[:, 128:].astype(BF)
            for way in range(3):
                own_copy(way, piece).start()
            own_local(piece).start()
            mirrors(piece)[0]().start()

        @pl.when((it >= 4) & (it < PIECES + 4))
        def _():
            piece = it - 4
            own_copy(0, piece).wait_recv()
            for way in range(2):
                pair_copy(way, piece).start()
            mirrors(piece)[1]().start()

        @pl.when((it >= 5) & (it < PIECES + 5))
        def _():
            piece = it - 5
            own_copy(1, piece).wait_recv()
            pair_copy(1, piece).wait_recv()
            for way in range(2):
                forward_copy(way, piece).start()
            own_copy(2, piece).wait_recv()
            pair_copy(0, piece).wait_recv()
            for kind in range(2, 6):
                mirrors(piece)[kind]().start()

        @pl.when(it >= 6)
        def _():
            piece = it - 6
            for way in range(2):
                forward_copy(way, piece).wait_recv()
            for kind in range(6, 8):
                mirrors(piece)[kind]().start()

        return carry

    lax.fori_loop(0, PIECES + 6, step_fn, 0)

    def finish(piece, carry):
        for way in range(2):
            y1_copy(way, piece).wait_send()
            y2_copy(way, piece).wait_send()
            pair_copy(way, piece).wait_send()
            forward_copy(way, piece).wait_send()
        for way in range(3):
            own_copy(way, piece).wait_send()
        z_copy(piece).wait_send()
        own_local(piece).wait()
        for copy in mirrors(piece):
            copy().wait()
        return carry

    lax.fori_loop(0, PIECES, finish, 0)
    to_other_core(0).wait_send()
    for kind in range(1, 4):
        to_other_core(kind).wait()
    for step in range(1, 8):
        text_copy(step).wait()


def image_pairs(tokens, weights, gain, text, w_query, w_out, params):
    half, width = tokens.shape
    heads = weights.shape[0]
    patches = half * 2
    any_spec = pl.BlockSpec(memory_space=pl.ANY)

    def like(array):
        return jax.ShapeDtypeStruct(array.shape, array.dtype)

    return pl.pallas_call(
        kv_kernel,
        name="kv",
        out_shape=[
            jax.ShapeDtypeStruct((2, 8, patches, 256), BF),
            jax.ShapeDtypeStruct((8,) + text.shape[1:], BF),
            like(w_query),
            like(w_out),
            like(params),
        ],
        in_specs=[any_spec, any_spec, pl.BlockSpec(memory_space=pltpu.VMEM)] + [any_spec] * 4,
        out_specs=[any_spec] * 5,
        scratch_shapes=[
            pltpu.VMEM((patches, width), BF),
            pltpu.VMEM((heads, width, 256), BF),
            pltpu.VMEM((heads, patches, 256), BF),
            pltpu.VMEM((2, patches, 256), BF),
            pltpu.VMEM((4, patches, 256), BF),
            pltpu.VMEM((patches, 256), BF),
            pltpu.VMEM((patches, 256), BF),
            pltpu.SemaphoreType.DMA((PIECES // 2,)),
            pltpu.SemaphoreType.DMA((8,)),
            pltpu.SemaphoreType.DMA((PIECES,)),
            pltpu.SemaphoreType.DMA((4,)),
            pltpu.SemaphoreType.DMA((4,)),
            pltpu.SemaphoreType.DMA((7,)),
            pltpu.SemaphoreType.DMA((7,)),
            pltpu.SemaphoreType.DMA((20, PIECES)),
            pltpu.SemaphoreType.DMA((20, PIECES)),
        ],
        compiler_params=pltpu.CompilerParams(
            collective_id=0, has_side_effects=True, vmem_limit_bytes=58 * 2**20
        ),
        cost_estimate=pl.CostEstimate(
            flops=2 * patches * width * heads * 256, bytes_accessed=40 * 2**20, transcendentals=0
        ),
    )(tokens, weights, gain, text, w_query, w_out, params)


KEY_PARTS = ((0, 512), (512, 512), (1024, 576))


class LayerLoad:
    def __init__(self, layer, own, other, dst, sem):
        self.here = lax.axis_index("section") == layer
        self.own = pltpu.make_async_copy(own, dst, sem)
        self.other = pltpu.make_async_copy(other, dst, sem)

    def start(self):
        pl.when(self.here)(lambda: self.own.start())
        pl.when(jnp.logical_not(self.here))(lambda: self.other.start())

    def wait(self):
        self.own.wait()


def add_to_query(acc, sq, block, gain, weights):
    values = block.astype(F32)
    sq[...] += jnp.sum(values * values, axis=-1, keepdims=True)
    acc[...] += jnp.dot((values * gain).astype(BF), weights, preferred_element_type=F32)


def finish_query(acc, sq, q_gain, query):
    inverse = lax.rsqrt(sq[:, :1] * (1.0 / 8192.0) + 1e-05)
    for head in range(4):
        one = acc[:, head * 128:(head + 1) * 128] * inverse
        one = one * lax.rsqrt(jnp.mean(one * one, axis=-1, keepdims=True) + 1e-05)
        query[head * 128:(head + 1) * 128, :] = (one * q_gain * 128.0 ** -0.5).astype(BF)


def attend(layer, choice_ref, valid_ref, query, pairs_ref, att_ref, tiles, total, norm, sem, before=None):
    core = lax.axis_index("section")
    first = choice_ref[2 * core]
    second = choice_ref[2 * core + 1]
    other = second != first
    plan = (
        (first, 0, None),
        (first, 1, valid_ref[first] > 1),
        (second, 0, other),
        (second, 1, other & (valid_ref[second] > 1)),
    )

    def copy(slot):
        image, tile, _ = plan[slot]
        return pltpu.make_async_copy(
            pairs_ref.at[layer, image, pl.ds(tile * TILE_TOK, TILE_TOK)], tiles.at[slot], sem.at[slot]
        )

    def run(slot, fn):
        allowed = plan[slot][2]
        if allowed is None:
            fn()
        else:
            pl.when(allowed)(fn)

    for slot in range(4):
        run(slot, lambda slot=slot: copy(slot).start())
    total[...] = jnp.zeros_like(total)
    norm[...] = jnp.zeros_like(norm)
    if before is not None:
        before()

    def one(slot):
        copy(slot).wait()
        for start, size in KEY_PARTS:
            scores = lax.dot_general(
                query[...], tiles[slot, start:start + size, 0:128],
                (((1,), (1,)), ((), ())), preferred_element_type=F32,
            )
            expo = jnp.exp(scores)
            norm[...] += jnp.sum(expo, axis=-1, keepdims=True)
            total[...] += jnp.dot(
                expo.astype(BF), tiles[slot, start:start + size, 128:256], preferred_element_type=F32
            )

    for slot in range(4):
        run(slot, functools.partial(one, slot))
    for head in range(4):
        at = slice(head * 128, (head + 1) * 128)
        att_ref[:, at] = (total[at, :] / norm[at, :1]).astype(BF)


def first_attention(
    choice_ref, valid_ref, pairs_ref, text_ref, text_all_ref, wq_ref, wq_other_ref, par_ref, par_other_ref, att_ref,
    tiles, total, norm, sem, hidden, wq, par, acc, sq, query, load_sem, wq_sem,
):
    core = lax.axis_index("section")
    tensor = lax.axis_index("tensor")
    par_load = LayerLoad(0, par_ref, par_other_ref, par, load_sem.at[8])
    par_load.start()
    chunks = []
    for step in range(8):
        block = (tensor + step) % 8
        src = text_ref.at[core] if step == 0 else text_all_ref.at[block]
        at = pl.ds(pl.multiple_of(block * 1024, 1024), 1024)
        chunks.append((
            block,
            pltpu.make_async_copy(src, hidden.at[step], load_sem.at[step]),
            LayerLoad(0, wq_ref.at[at], wq_other_ref.at[at], wq.at[step], wq_sem.at[step]),
        ))
        chunks[-1][1].start()
        chunks[-1][2].start()

    def before():
        acc[...] = jnp.zeros_like(acc)
        sq[...] = jnp.zeros_like(sq)
        par_load.wait()
        for step, (block, text_load, wq_load) in enumerate(chunks):
            text_load.wait()
            wq_load.wait()
            add_to_query(acc, sq, hidden[step], par[pl.ds(block, 1), :], wq[step])
        finish_query(acc, sq, par[9:10, 0:128], query)

    attend(0, choice_ref, valid_ref, query, pairs_ref, att_ref, tiles, total, norm, sem, before)


def second_attention(choice_ref, valid_ref, pairs_ref, query_ref, att_ref, tiles, total, norm, sem):
    attend(1, choice_ref, valid_ref, query_ref, pairs_ref, att_ref, tiles, total, norm, sem)


ATTEND_SCRATCH = [
    pltpu.VMEM((4, TILE_TOK, 256), BF),
    pltpu.VMEM((512, 128), F32),
    pltpu.VMEM((512, 128), F32),
    pltpu.SemaphoreType.DMA((4,)),
]


def attention_first(choice, valid, pairs, text, text_all, wq, wq_other, par, par_other):
    any_spec = pl.BlockSpec(memory_space=pl.ANY)
    smem = pl.BlockSpec(memory_space=pltpu.SMEM)
    return pl.pallas_call(
        first_attention,
        name="attend0",
        out_shape=jax.ShapeDtypeStruct((128, 512), BF),
        in_specs=[smem, smem] + [any_spec] * 7,
        out_specs=pl.BlockSpec(memory_space=pltpu.VMEM),
        scratch_shapes=ATTEND_SCRATCH + [
            pltpu.VMEM((8, 128, 1024), BF),
            pltpu.VMEM((8, 1024, 512), BF),
            pltpu.VMEM((16, 1024), F32),
            pltpu.VMEM((128, 512), F32),
            pltpu.VMEM((128, 128), F32),
            pltpu.VMEM((512, 128), BF),
            pltpu.SemaphoreType.DMA((9,)),
            pltpu.SemaphoreType.DMA((8,)),
        ],
        compiler_params=pltpu.CompilerParams(vmem_limit_bytes=48 * 2**20),
        cost_estimate=pl.CostEstimate(flops=3 * 10**9, bytes_accessed=14 * 2**20, transcendentals=3 * 10**6),
    )(choice, valid, pairs, text, text_all, wq, wq_other, par, par_other)


def attention_second(choice, valid, pairs, query):
    any_spec = pl.BlockSpec(memory_space=pl.ANY)
    smem = pl.BlockSpec(memory_space=pltpu.SMEM)
    vmem = pl.BlockSpec(memory_space=pltpu.VMEM)
    return pl.pallas_call(
        second_attention,
        name="attend1",
        out_shape=jax.ShapeDtypeStruct((128, 512), BF),
        in_specs=[smem, smem, any_spec, vmem],
        out_specs=vmem,
        scratch_shapes=ATTEND_SCRATCH,
        compiler_params=pltpu.CompilerParams(vmem_limit_bytes=48 * 2**20),
        cost_estimate=pl.CostEstimate(flops=2 * 10**9, bytes_accessed=4 * 2**20, transcendentals=3 * 10**6),
    )(choice, valid, pairs, query)


def project_and_sum(layer, att_ref, wo_ref, wo_other_ref, wo, part, from_y1, from_y2, from_z, wo_sem, send, recv, greet):
    x, zh, zl, y, core = position()
    y_up, y_dn = (y + 1) % 4, (y + 3) % 4
    to_y_up = device(x, zh, zl, y_up, core)
    to_y_dn = device(x, zh, zl, y_dn, core)
    to_z_lo = device(x, zh, 1 - zl, y, core)

    def block_of(slot):
        ring = (y + 2) % 4 if slot < 2 else y_up if slot < 4 else y_dn if slot < 6 else y
        return (slot % 2) * 4 + ring

    order = (0, 1, 4, 3, 2, 5, 6, 7)
    loads = {}
    for slot in order:
        at = pl.ds(pl.multiple_of(block_of(slot) * 1024, 1024), 1024)
        loads[slot] = LayerLoad(layer, wo_ref.at[:, at], wo_other_ref.at[:, at], wo.at[slot], wo_sem.at[slot])
        loads[slot].start()

    def remote(kind, src, dst, peer):
        return pltpu.make_async_remote_copy(
            src_ref=src, dst_ref=dst, send_sem=send.at[kind], recv_sem=recv.at[kind],
            device_id=peer, device_id_type=MESH,
        )

    far = [remote(0, part.at[0], from_y1.at[0], to_y_up), remote(1, part.at[1], from_y1.at[1], to_y_dn)]
    near = {
        4: remote(2, part.at[4], from_y2.at[2], to_y_dn),
        3: remote(3, part.at[3], from_y2.at[1], to_y_up),
        2: remote(4, part.at[2], from_y2.at[0], to_y_up),
        5: remote(5, part.at[5], from_y2.at[3], to_y_dn),
    }
    across = remote(6, part.at[7 - zl], from_z, to_z_lo)

    def project(slot):
        loads[slot].wait()
        part[slot] = jnp.dot(att_ref[...], wo[slot], preferred_element_type=F32).astype(BF)

    project(0)
    greet()
    far[0].start()
    project(1)
    far[1].start()
    for slot in (4, 3):
        project(slot)
        near[slot].start()
    for slot in (2, 5, 6, 7):
        project(slot)
    for way, slot in ((0, 2), (1, 5)):
        far[way].wait_recv()
        part[slot] = (part[slot].astype(F32) + from_y1[way].astype(F32)).astype(BF)
        near[slot].start()
    for slot in (4, 3, 2, 5):
        near[slot].wait_recv()
    part[7 - zl] = (
        part[7 - zl].astype(F32) + from_y2[1 - zl].astype(F32) + from_y2[3 - zl].astype(F32)
    ).astype(BF)
    across.start()
    total = part[6 + zl].astype(F32) + from_y2[zl].astype(F32) + from_y2[2 + zl].astype(F32)
    across.wait_recv()
    total = total + from_z[...].astype(F32)

    def drain():
        for copy in far + [near[slot] for slot in (4, 3, 2, 5)] + [across]:
            copy.wait_send()

    return total, drain


SUM_SCRATCH = [
    pltpu.VMEM((8, 512, 1024), BF),
    pltpu.VMEM((8, 128, 1024), BF),
    pltpu.VMEM((2, 128, 1024), BF),
    pltpu.VMEM((4, 128, 1024), BF),
    pltpu.VMEM((128, 1024), BF),
    pltpu.SemaphoreType.DMA((8,)),
    pltpu.SemaphoreType.DMA((7,)),
    pltpu.SemaphoreType.DMA((7,)),
]


def greeting(peers):
    barrier = pltpu.get_barrier_semaphore()
    for peer in peers:
        pl.semaphore_signal(barrier, inc=1, device_id=peer, device_id_type=MESH)
    pl.semaphore_wait(barrier, len(peers))


def middle_kernel(
    att_ref, text_ref, wo_ref, wo_other_ref, wq_ref, wq_other_ref, par_ref, par_other_ref, query_ref, upd_ref,
    wo, part, from_y1, from_y2, from_z, wo_sem, send, recv,
    hidden, wq, par, acc, sq, wq_sem, ag_send, ag_recv, par_sem,
):
    x, zh, zl, y, core = position()
    y_up, y_dn = (y + 1) % 4, (y + 3) % 4
    to_y_up = device(x, zh, zl, y_up, core)
    to_y_dn = device(x, zh, zl, y_dn, core)
    to_z_lo = device(x, zh, 1 - zl, y, core)
    other = 1 - zl
    par_copies = [
        LayerLoad(layer, par_ref, par_other_ref, par.at[layer], par_sem.at[layer]) for layer in range(2)
    ]
    for copy in par_copies:
        copy.start()

    total, drain = project_and_sum(
        0, att_ref, wo_ref, wo_other_ref, wo, part, from_y1, from_y2, from_z, wo_sem, send, recv,
        lambda: greeting([to_y_up, to_y_dn, to_z_lo]),
    )
    order = [
        zl * 4 + y, zl * 4 + y_dn, zl * 4 + y_up, other * 4 + y,
        other * 4 + y_dn, other * 4 + y_up, zl * 4 + (y + 2) % 4, other * 4 + (y + 2) % 4,
    ]
    chunks = []
    for k, block in enumerate(order):
        at = pl.ds(pl.multiple_of(block * 1024, 1024), 1024)
        chunks.append(LayerLoad(1, wq_ref.at[at], wq_other_ref.at[at], wq.at[k], wq_sem.at[k]))
        chunks[k].start()
    for copy in par_copies:
        copy.wait()
    own = order[0]
    hidden[own] = (text_ref[core].astype(F32) + par[0, 8:9, :] * total).astype(BF)

    def remote(kind, block, peer, half=None):
        ref = hidden.at[block] if half is None else hidden.at[block, pl.ds(half * 64, 64)]
        return pltpu.make_async_remote_copy(
            src_ref=ref, dst_ref=ref, send_sem=ag_send.at[kind], recv_sem=ag_recv.at[kind],
            device_id=peer, device_id_type=MESH,
        )

    up, down, cross = remote(0, own, to_y_up), remote(1, own, to_y_dn), remote(2, own, to_z_lo)
    up.start()
    down.start()
    cross.start()
    upd_ref[...] = hidden[own]
    acc[...] = jnp.zeros_like(acc)
    sq[...] = jnp.zeros_like(sq)

    def use(k):
        chunks[k].wait()
        block = order[k]
        add_to_query(acc, sq, hidden[block], par[1, pl.ds(block, 1), :], wq[k])

    use(0)
    cross.wait_recv()
    cross_up, cross_down = remote(3, order[3], to_y_up), remote(4, order[3], to_y_dn)
    cross_up.start()
    cross_down.start()
    up.wait_recv()
    far_up = remote(5, order[1], to_y_up, 0)
    far_up.start()
    down.wait_recv()
    far_down = remote(6, order[2], to_y_dn, 1)
    far_down.start()
    use(1)
    use(2)
    use(3)
    cross_up.wait_recv()
    cross_far_up = remote(7, order[4], to_y_up, 0)
    cross_far_up.start()
    cross_down.wait_recv()
    cross_far_down = remote(8, order[5], to_y_dn, 1)
    cross_far_down.start()
    use(4)
    use(5)
    far_up.wait_recv()
    far_down.wait_recv()
    use(6)
    cross_far_up.wait_recv()
    cross_far_down.wait_recv()
    use(7)
    finish_query(acc, sq, par[1, 9:10, 0:128], query_ref)
    drain()
    for copy in (up, down, cross, cross_up, cross_down, far_up, far_down, cross_far_up, cross_far_down):
        copy.wait_send()


def last_kernel(
    att_ref, upd_ref, wo_ref, wo_other_ref, par_ref, par_other_ref, out_ref, wo, part, from_y1, from_y2, from_z, wo_sem, send, recv,
    par, last, core_send, core_recv, par_sem,
):
    x, zh, zl, y, core = position()
    to_y_up = device(x, zh, zl, (y + 1) % 4, core)
    to_y_dn = device(x, zh, zl, (y + 3) % 4, core)
    to_z_lo = device(x, zh, 1 - zl, y, core)
    to_core = device(x, zh, zl, y, 1 - core)
    par_copy = LayerLoad(1, par_ref, par_other_ref, par, par_sem.at[0])
    par_copy.start()
    send_first = pltpu.make_async_remote_copy(
        src_ref=upd_ref, dst_ref=out_ref.at[1], send_sem=core_send.at[0], recv_sem=core_recv.at[0],
        device_id=to_core, device_id_type=MESH,
    )
    send_last = pltpu.make_async_remote_copy(
        src_ref=last, dst_ref=out_ref.at[0], send_sem=core_send.at[1], recv_sem=core_recv.at[1],
        device_id=to_core, device_id_type=MESH,
    )

    def greet():
        greeting([to_y_up, to_y_dn, to_z_lo, to_core])

        @pl.when(core == 1)
        def _():
            send_first.start()

    total, drain = project_and_sum(
        1, att_ref, wo_ref, wo_other_ref, wo, part, from_y1, from_y2, from_z, wo_sem, send, recv, greet
    )
    par_copy.wait()
    new = (upd_ref[...].astype(F32) + par[8:9, :] * total).astype(BF)

    @pl.when(core == 0)
    def _():
        last[...] = new
        send_last.start()
        out_ref[0] = upd_ref[...]
        send_first.wait_recv()
        send_last.wait_send()

    @pl.when(core == 1)
    def _():
        out_ref[1] = new
        send_first.wait_send()
        send_last.wait_recv()

    drain()


def middle(att, text, *weights):
    any_spec = pl.BlockSpec(memory_space=pl.ANY)
    vmem = pl.BlockSpec(memory_space=pltpu.VMEM)
    return pl.pallas_call(
        middle_kernel,
        name="middle",
        out_shape=[jax.ShapeDtypeStruct((512, 128), BF), jax.ShapeDtypeStruct((128, 1024), BF)],
        in_specs=[vmem, vmem] + [any_spec] * 6,
        out_specs=[vmem] * 2,
        scratch_shapes=SUM_SCRATCH + [
            pltpu.VMEM((8, 128, 1024), BF),
            pltpu.VMEM((8, 1024, 512), BF),
            pltpu.VMEM((2, 16, 1024), F32),
            pltpu.VMEM((128, 512), F32),
            pltpu.VMEM((128, 128), F32),
            pltpu.SemaphoreType.DMA((8,)),
            pltpu.SemaphoreType.DMA((9,)),
            pltpu.SemaphoreType.DMA((9,)),
            pltpu.SemaphoreType.DMA((2,)),
        ],
        compiler_params=pltpu.CompilerParams(
            collective_id=1, has_side_effects=True, vmem_limit_bytes=56 * 2**20
        ),
    )(att, text, *weights)


def last_step(att, upd, *weights):
    any_spec = pl.BlockSpec(memory_space=pl.ANY)
    vmem = pl.BlockSpec(memory_space=pltpu.VMEM)
    return pl.pallas_call(
        last_kernel,
        name="last",
        out_shape=jax.ShapeDtypeStruct((2, 128, 1024), BF),
        in_specs=[vmem, vmem] + [any_spec] * 4,
        out_specs=vmem,
        scratch_shapes=SUM_SCRATCH + [
            pltpu.VMEM((16, 1024), F32),
            pltpu.VMEM((128, 1024), BF),
            pltpu.SemaphoreType.DMA((2,)),
            pltpu.SemaphoreType.DMA((2,)),
            pltpu.SemaphoreType.DMA((1,)),
        ],
        compiler_params=pltpu.CompilerParams(
            collective_id=2, has_side_effects=True, vmem_limit_bytes=56 * 2**20
        ),
    )(att, upd, *weights)


def local(
    text_hidden,
    image_tokens,
    attn_gain,
    w_query,
    w_keyval,
    q_gain,
    k_gain,
    w_out,
    gate,
    image_choice,
    valid_tiles,
):
    text = text_hidden[:, 0]
    weights = jnp.transpose(w_keyval[0], (1, 0, 2))
    params = jnp.concatenate(
        [
            attn_gain.reshape(8, 1024),
            jnp.broadcast_to(jnp.tanh(gate)[:, None], (1, 1024)),
            jnp.tile(q_gain, (7, 8)),
        ]
    )
    wq, wo = w_query[0], w_out[0]
    pairs, text_all, wq_other, wo_other, par_other = image_pairs(
        image_tokens[0], weights, k_gain, text, wq, wo, params
    )
    choice = image_choice.reshape(4)
    att = attention_first(choice, valid_tiles, pairs, text, text_all, wq, wq_other, params, par_other)
    query, updated = middle(att, text, wo, wo_other, wq, wq_other, params, par_other)
    att = attention_second(choice, valid_tiles, pairs, query)
    result = last_step(att, updated, wo, wo_other, params, par_other)
    return result[None, :, None]


def solution(mesh):
    placed = (
        P(None, "dp", None, "tensor"),
        P("dp", "section", "tensor"),
        P("section", None),
        P("section", None, "tensor"),
        P("section", "tensor", None, None),
        P("section", None),
        P("section", None),
        P("section", "tensor", None),
        P("section"),
        P(None, "dp", None),
        P(),
    )
    return jax.shard_map(
        local,
        mesh=mesh,
        in_specs=placed,
        out_specs=P("section", None, "dp", None, "tensor"),
        check_vma=False,
    )
```

time: 379 us -> 290 us (0.77)
  Pallas kernels: 335 us -> 271 us
  between operations: 24.6 us -> 0.81 us
    pallas_call x7 -> x5, Pallas kernels: 335 us -> 271 us  [the longest x1 166 us: image_pairs(): pl.pallas_call(kv_kernel, name='kv', out_shape=[jax.ShapeDtypeStruct((2,...]
    unnamed x9 -> x26, local copies, waits for them, and re-layouts: 5 us -> 12.6 us
    another operation x3 -> x2, local copies, waits for them, and re-layouts: 4.14 us -> 0.01 us  [local(): jnp.tile(q_gain, (7, 8))]
where the time goes in v2:
time: 290 us; the launch traced here: 288 us
  Pallas kernels  271 us (93%)
  local copies, waits for them, and re-layouts  12.8 us (4%)
    pallas_call x1, Pallas kernels, image_pairs(): pl.pallas_call(kv_kernel, name='kv', out_shape=[jax.ShapeDtypeStruct((2,...  166 us
    pallas_call x1, Pallas kernels, middle(): pl.pallas_call(middle_kernel, name='middle', out_shape=[jax.ShapeDtypeStr...  59.7 us
    pallas_call x1, Pallas kernels, last_step(): pl.pallas_call(last_kernel, name='last', out_shape=jax.ShapeDtypeStruct((...  34.1 us
    unnamed x26, local copies, waits for them, and re-layouts  12.6 us
    pallas_call x1, Pallas kernels, attention_first(): pl.pallas_call(first_attention, name='attend0', out_shape=jax.ShapeDtypeS...  7.78 us

profile of v2, /device:TPU:1, one launch (start us, length us, event | category | flops | bytes accessed | tf_op | source)
XLA Modules:
  0.0 287.7 jit_solution(11682404891221539212)
XLA Ops:
  0.0 0.0 copy-start
  0.0 0.5 broadcast.13
  0.5 1.5 reduce.7
  2.7 0.1 pad.1.clone
  2.8 0.7 pad_maximum_fusion.par_ref
  3.5 5.1 %copy.15 = bf16[1,1024,8,256]{3,1,2,0:T(8,128)(2,1)} copy(bf16[1,1024,8,256]{3,2,1,0:T(8,128)(2,1)} %param.15) | data formatting | bytes 8388608 | tf_op args[4]
  8.6 165.5 %kv.1 = (bf16[2,8,3200,256]{3,2,1,0:T(8,128)(2,1)}, bf16[8,128,1024]{2,1,0:T(8,128)(2,1)}, bf16[8192,512]{1,0:T(8,128)(2,1)}, bf16[512,8192]{1,0:T(8,128)(2,1)}, f32[16,1024]{1,0:T(8,128)}) custom-call(bf16[1600,1024]{1,0:T(8,128)(2,1)} %bitcast.28, bf16[8,1024,256]{2,1,0:T(8,128)(2,1)} %bitcast.26, f32[1,128]{1,0:T(1,128)} %gain_ref.1, ...), custom_call_target="tpu_custom_call" | custom-call | flops 13421772800 | bytes 41943040 | tf_op jit(solution)/shard_map/kv/pallas_call | solution.py:294
  174.1 0.5 broadcast.12
  174.7 0.7 reduce.6
  175.3 0.1 reshape.13.choice_ref
  175.4 0.0 copy-done.4
  175.4 1.6 copy-done.3
  177.0 0.8 copy-done.5
  177.8 7.8 %attend0.1.att_ref = bf16[128,512]{1,0:T(8,128)(2,1)S(1)} custom-call(s32[4]{0:T(128)S(1)} %reshape.13.choice_ref, s32[8]{0:T(128)S(1)} %copy-done.9, bf16[2,8,3200,256]{3,2,1,0:T(8,128)(2,1)} %get-tuple-element.12.pairs_ref, bf16[2,128,1024]{2,1,0:T(8,128)(2,1)S(1)} %bitcast.19, bf16[8,128,1024]{2,1,0:T(8,128)(2,1)S(1)} %copy-done.3, ...), custom_call_target="tpu_custom_call" | custom-call | flops 3000000000 | bytes 14680064 | tf_op jit(solution)/shard_map/attend0/pallas_call | solution.py:465
  185.6 0.0 copy-start.7
  185.6 0.6 copy-done.7
  186.3 59.7 %middle.1 = (bf16[512,128]{1,0:T(8,128)(2,1)}, bf16[128,1024]{1,0:T(8,128)(2,1)}) custom-call(bf16[128,512]{1,0:T(8,128)(2,1)} %copy-done.7, bf16[2,128,1024]{2,1,0:T(8,128)(2,1)} %bitcast.18, bf16[512,8192]{1,0:T(8,128)(2,1)} %bitcast.24, bf16[512,8192]{1,0:T(8,128)(2,1)} %get-tuple-element.16.wo_other_ref, bf16[8192,512]{1,0:T(8,128)(2,1)} %bitcast.22, ...), custom_call_target="tpu_custom_call" | custom-call | tf_op jit(solution)/shard_map/middle/pallas_call | solution.py:731
  246.0 0.0 copy-start.8
  246.0 0.9 copy-done.8
  246.9 4.1 %attend1.1.att_ref = bf16[128,512]{1,0:T(8,128)(2,1)S(1)} custom-call(s32[4]{0:T(128)S(1)} %reshape.13.choice_ref, s32[8]{0:T(128)S(1)} %copy-done.9, bf16[2,8,3200,256]{3,2,1,0:T(8,128)(2,1)} %get-tuple-element.12.pairs_ref, bf16[512,128]{1,0:T(8,128)(2,1)S(1)} %copy-done.8), custom_call_target="tpu_custom_call" | custom-call | flops 2000000000 | bytes 4194304 | tf_op jit(solution)/shard_map/attend1/pallas_call | solution.py:490
  251.1 0.0 copy-start.6
  251.1 0.6 copy-done.6
  251.7 34.1 %last.1 = bf16[2,128,1024]{2,1,0:T(8,128)(2,1)} custom-call(bf16[128,512]{1,0:T(8,128)(2,1)} %copy-done.6, bf16[128,1024]{1,0:T(8,128)(2,1)} %get-tuple-element.18.upd_ref, bf16[512,8192]{1,0:T(8,128)(2,1)} %bitcast.25, bf16[512,8192]{1,0:T(8,128)(2,1)} %get-tuple-element.16.wo_other_ref, f32[16,1024]{1,0:T(8,128)} %pad_maximum_fusion.par_ref, ...), custom_call_target="tpu_custom_call" | custom-call | tf_op jit(solution)/shard_map/last/pallas_call | solution.py:757
  285.8 1.9 copy.18
  (15 shorter events, 0.0 us)
Async XLA Ops:
  0.0 2.0 copy-start
  8.6 166.1 %copy-start.10 = (s32[2,1,2]{2,1,0:T(1,128)S(1)}, s32[2,1,2]{2,1,0:T(1,128)}, u32[]{:S(2)}) copy-start(s32[2,1,2]{2,1,0:T(1,128)} %param.20) | copy-start | bytes 52
  8.6 166.8 %copy-start.2 = (bf16[2,1,128,1024]{3,2,1,0:T(8,128)(2,1)S(1)}, bf16[2,1,128,1024]{3,2,1,0:T(8,128)(2,1)}, u32[]{:S(2)}) copy-start(bf16[2,1,128,1024]{3,2,1,0:T(8,128)(2,1)} %param.11) | copy-start | bytes 1572868
  8.6 166.8 %copy-start.4 = (f32[16,1024]{1,0:T(8,128)S(1)}, f32[16,1024]{1,0:T(8,128)}, u32[]{:S(2)}) copy-start(f32[16,1024]{1,0:T(8,128)} %pad_maximum_fusion.par_ref) | copy-start | bytes 196612
  8.6 166.8 %copy-start.9 = (s32[8]{0:T(128)S(1)}, s32[8]{0:T(128)}, u32[]{:S(2)}) copy-start(s32[8]{0:T(128)} %valid_ref.3) | copy-start | bytes 100
  175.4 1.6 copy-start.3
  177.0 0.8 copy-start.5
  185.6 0.7 copy-start.7
  246.0 0.9 copy-start.8
  251.1 0.7 copy-start.6
  251.7 36.0 %copy-start.1 = (f32[1,128]{1,0:T(1,128)S(1)}, f32[1,128]{1,0:T(1,128)}, u32[]{:S(2)}) copy-start(f32[1,128]{1,0:T(1,128)} %param.16) | copy-start | bytes 1540

commit v3 on v2

v3 whole, which is shorter than its diff:
```python
import functools

import jax
import jax.numpy as jnp
from jax import lax
from jax.experimental import pallas as pl
from jax.experimental.pallas import tpu as pltpu
from jax.sharding import PartitionSpec as P

TILE_TOK = 1600
PIECES = 20
MESH = pl.DeviceIdType.MESH
BF = jnp.bfloat16
F32 = jnp.float32


def position():
    dp = lax.axis_index("dp")
    tensor = lax.axis_index("tensor")
    return dp // 2, dp % 2, tensor // 4, tensor % 4, lax.axis_index("section")


def device(x, zh, zl, y, core):
    return (x * 2 + zh, zl * 4 + y, core)


def kv_kernel(
    tok_ref, w_ref, gain_ref, text_ref, wq_ref, wo_ref, attn_ref, small_ref,
    pairs_ref, text_out_ref, wq_out_ref, wo_out_ref, attn_out_ref, small_out_ref,
    tok, wgt, part, from_y1, from_y2, from_z, done,
    tok_sem, w_sem, loc_sem, core_send, core_recv, text_send, text_recv, send, recv,
):
    x, zh, zl, y, core = position()
    dp = x * 2 + zh
    half = tok_ref.shape[0]
    out_ref = pairs_ref.at[core]
    rows = half * 2 // PIECES
    y_up, y_dn = (y + 1) % 4, (y + 3) % 4
    x_up, x_dn = (x + 1) % 4, (x + 3) % 4
    to_y = (device(x, zh, zl, y_up, core), device(x, zh, zl, y_dn, core))
    to_x = (device(x_up, zh, zl, y, core), device(x_dn, zh, zl, y, core))
    to_z_lo = device(x, zh, 1 - zl, y, core)
    to_z_hi = device(x, 1 - zh, zl, y, core)
    to_core = device(x, zh, zl, y, 1 - core)
    peers = to_y + to_x + (to_z_lo, to_z_hi, to_core)

    barrier = pltpu.get_barrier_semaphore()
    for peer in peers:
        pl.semaphore_signal(barrier, inc=1, device_id=peer, device_id_type=MESH)

    def first_row(piece):
        return pl.multiple_of(((piece + core * (PIECES // 2)) % PIECES) * rows, rows)

    def rows_of(piece):
        return pl.ds(first_row(piece), rows)

    def head_of(ring, side):
        return side * 4 + ((y + 2) % 4, y_up, y_dn, y)[ring]

    def tok_copy(piece):
        return pltpu.make_async_copy(
            tok_ref.at[pl.ds(pl.multiple_of(piece * rows, rows), rows)],
            tok.at[pl.ds(pl.multiple_of(core * half + piece * rows, rows), rows)],
            tok_sem.at[piece],
        )

    def w_copy(ring, side):
        return pltpu.make_async_copy(
            w_ref.at[head_of(ring, side)], wgt.at[ring, side], w_sem.at[ring * 2 + side]
        )

    def to_other_core(kind):
        src, dst = (
            (tok_ref, tok.at[pl.ds(pl.multiple_of(core * half, half), half)]),
            (attn_ref, attn_out_ref),
            (small_ref, small_out_ref),
            (wq_ref, wq_out_ref),
            (wo_ref, wo_out_ref),
        )[kind]
        return pltpu.make_async_remote_copy(
            src_ref=src, dst_ref=dst, send_sem=core_send.at[kind], recv_sem=core_recv.at[kind],
            device_id=to_core, device_id_type=MESH,
        )

    def text_copy(kind):
        own = zl * 4
        other = (1 - zl) * 4
        block = (
            own + y, own + y, own + y, other + y, other + y, own + y_dn, own + y_up, other + y_dn, other + y_up
        )[kind]
        dst = text_out_ref.at[block]
        src = text_ref.at[core] if kind < 3 else dst
        if kind >= 5:
            at = pl.ds(((kind - 5) % 2) * 64, 64)
            src, dst = src.at[at], dst.at[at]
        peer = to_z_lo if kind == 2 else to_y[(0, 1, 2, 0, 1, 0, 1, 0, 1)[kind]]
        return pltpu.make_async_remote_copy(
            src_ref=src, dst_ref=dst, send_sem=text_send.at[kind], recv_sem=text_recv.at[kind],
            device_id=peer, device_id_type=MESH,
        )

    def remote(kind, piece, src, dst, peer):
        return pltpu.make_async_remote_copy(
            src_ref=src, dst_ref=dst,
            send_sem=send.at[kind, piece], recv_sem=recv.at[kind, piece],
            device_id=peer, device_id_type=MESH,
        )

    def y1_copy(way, piece):
        at = rows_of(piece)
        return remote(way, piece, part.at[0, way, at], from_y1.at[way, at], to_y[way])

    def y2_copy(way, piece):
        at = rows_of(piece)
        return remote(2 + way, piece, part.at[1 + way, :, at], from_y2.at[way, :, at], to_y[way])

    def z_copy(piece):
        at = rows_of(piece)
        return remote(4, piece, part.at[3, 1 - zl, at], from_z.at[at], to_z_lo)

    def own_copy(way, piece):
        at = rows_of(piece)
        return remote(5 + way, piece, done.at[at], out_ref.at[dp, at], to_z_hi if way == 0 else to_x[way - 1])

    def own_local(piece):
        at = rows_of(piece)
        return pltpu.make_async_copy(done.at[at], out_ref.at[dp, at], loc_sem.at[piece])

    def pair_copy(way, piece):
        ref = out_ref.at[x * 2 + 1 - zh, rows_of(piece)]
        return remote(8 + way, piece, ref, ref, to_x[way])

    def forward_copy(way, piece):
        image = (x_dn * 2 + zh, x_up * 2 + 1 - zh)[way]
        ref = out_ref.at[image, rows_of(piece)]
        return remote(10 + way, piece, ref, ref, to_x[way])

    def mirror(kind, piece):
        across = (x + 2) % 4
        place = (
            (x, zh), (x, 1 - zh), (x_dn, zh), (x_up, zh), (x_dn, 1 - zh), (x_up, 1 - zh), (across, zh), (across, 1 - zh)
        )[kind]
        ref = out_ref.at[place[0] * 2 + place[1], rows_of(piece)]
        return remote(12 + kind, piece, done.at[rows_of(piece)] if kind == 0 else ref, ref, to_core)

    for ring in range(4):
        for side in range(2):
            w_copy(ring, side).start()

    def start_tok(piece, carry):
        tok_copy(piece).start()
        return carry

    lax.fori_loop(0, PIECES // 2, start_tok, 0)
    pl.semaphore_wait(barrier, len(peers))
    for kind in range(3):
        text_copy(kind).start()
    for kind in range(5):
        to_other_core(kind).start()

    def add(ring, side, at, addend):
        part[ring, side, at, :] = (part[ring, side, at, :].astype(F32) + addend.astype(F32)).astype(BF)

    def step_fn(it, carry):
        @pl.when(it < PIECES)
        def _():
            piece = it

            @pl.when(piece < PIECES // 2)
            def _():
                tok_copy(piece).wait()

            @pl.when(piece == PIECES // 2)
            def _():
                to_other_core(0).wait_recv()

            at = rows_of(piece)
            for ring in range(4):
                for side in range(2):
                    @pl.when(it == 0)
                    def _():
                        w_copy(ring, side).wait()

                    part[ring, side, at, :] = jnp.dot(
                        tok[at, :], wgt[ring, side], preferred_element_type=F32
                    ).astype(BF)
                    if ring == 0:
                        y1_copy(side, piece).start()

        @pl.when((it >= 1) & (it < PIECES + 1))
        def _():
            piece = it - 1
            at = rows_of(piece)
            for way in range(2):
                y1_copy(way, piece).wait_recv()
                add(1 + way, way, at, from_y1[way, at, :])
                y2_copy(way, piece).start()

        @pl.when((it >= 2) & (it < PIECES + 2))
        def _():
            piece = it - 2
            at = rows_of(piece)
            for way in range(2):
                y2_copy(way, piece).wait_recv()
            add(
                3, 1 - zl, at,
                from_y2[0, 1 - zl, at, :].astype(F32) + from_y2[1, 1 - zl, at, :].astype(F32),
            )
            z_copy(piece).start()

            @pl.when(piece == PIECES - 1)
            def _():
                for kind in range(3):
                    text_copy(kind).wait_recv()
                for kind in range(3, 7):
                    text_copy(kind).start()

        @pl.when((it >= 3) & (it < PIECES + 3))
        def _():
            piece = it - 3
            at = rows_of(piece)
            z_copy(piece).wait_recv()
            total = (
                part[3, zl, at, :].astype(F32)
                + from_y2[0, zl, at, :].astype(F32) + from_y2[1, zl, at, :].astype(F32)
                + from_z[at, :].astype(F32)
            )
            keys = total[:, :128]
            keys = keys * lax.rsqrt(jnp.mean(keys * keys, axis=-1, keepdims=True) + 1e-05)
            done[at, 0:128] = (keys * gain_ref[...]).astype(BF)
            done[at, 128:256] = total[:, 128:].astype(BF)
            for way in range(3):
                own_copy(way, piece).start()
            own_local(piece).start()
            mirror(0, piece).start()

        @pl.when((it >= 4) & (it < PIECES + 4))
        def _():
            piece = it - 4
            own_copy(0, piece).wait_recv()
            for way in range(2):
                pair_copy(way, piece).start()
            mirror(1, piece).start()

        @pl.when((it >= 5) & (it < PIECES + 5))
        def _():
            piece = it - 5
            own_copy(1, piece).wait_recv()
            pair_copy(1, piece).wait_recv()
            for way in range(2):
                forward_copy(way, piece).start()
            own_copy(2, piece).wait_recv()
            pair_copy(0, piece).wait_recv()
            for kind in range(2, 6):
                mirror(kind, piece).start()

            @pl.when(piece == PIECES - 1)
            def _():
                for kind in range(3, 5):
                    text_copy(kind).wait_recv()
                    text_copy(kind + 4).start()

        @pl.when(it >= 6)
        def _():
            piece = it - 6
            for way in range(2):
                forward_copy(way, piece).wait_recv()
            for kind in range(6, 8):
                mirror(kind, piece).start()

        return carry

    lax.fori_loop(0, PIECES + 6, step_fn, 0)

    def finish(piece, carry):
        z_copy(piece).wait_send()
        for way in range(2):
            y1_copy(way, piece).wait_send()
            y2_copy(way, piece).wait_send()
        for way in range(2):
            pair_copy(way, piece).wait_send()
            forward_copy(way, piece).wait_send()
        for way in range(3):
            own_copy(way, piece).wait_send()
        own_local(piece).wait()
        for kind in range(8):
            mirror(kind, piece).wait()
        return carry

    lax.fori_loop(0, PIECES, finish, 0)
    to_other_core(0).wait_send()
    for kind in range(1, 5):
        to_other_core(kind).wait()
    for kind in range(9):
        text_copy(kind).wait_send()
    for kind in range(5, 9):
        text_copy(kind).wait_recv()


def image_pairs(tokens, weights, gain, text, w_query, w_out, attn_gain, small):
    half, width = tokens.shape
    heads = weights.shape[0]
    patches = half * 2
    any_spec = pl.BlockSpec(memory_space=pl.ANY)

    def like(array):
        return jax.ShapeDtypeStruct(array.shape, array.dtype)

    return pl.pallas_call(
        kv_kernel,
        name="kv",
        out_shape=[
            jax.ShapeDtypeStruct((2, 8, patches, 256), BF),
            jax.ShapeDtypeStruct((8,) + text.shape[1:], BF),
            like(w_query),
            like(w_out),
            like(attn_gain),
            like(small),
        ],
        in_specs=[any_spec, any_spec, pl.BlockSpec(memory_space=pltpu.VMEM)] + [any_spec] * 5,
        out_specs=[any_spec] * 6,
        scratch_shapes=[
            pltpu.VMEM((patches, width), BF),
            pltpu.VMEM((4, 2, width, 256), BF),
            pltpu.VMEM((4, 2, patches, 256), BF),
            pltpu.VMEM((2, patches, 256), BF),
            pltpu.VMEM((2, 2, patches, 256), BF),
            pltpu.VMEM((patches, 256), BF),
            pltpu.VMEM((patches, 256), BF),
            pltpu.SemaphoreType.DMA((PIECES // 2,)),
            pltpu.SemaphoreType.DMA((8,)),
            pltpu.SemaphoreType.DMA((PIECES,)),
            pltpu.SemaphoreType.DMA((5,)),
            pltpu.SemaphoreType.DMA((5,)),
            pltpu.SemaphoreType.DMA((9,)),
            pltpu.SemaphoreType.DMA((9,)),
            pltpu.SemaphoreType.DMA((20, PIECES)),
            pltpu.SemaphoreType.DMA((20, PIECES)),
        ],
        compiler_params=pltpu.CompilerParams(
            collective_id=0, has_side_effects=True, vmem_limit_bytes=60 * 2**20
        ),
        cost_estimate=pl.CostEstimate(
            flops=2 * patches * width * heads * 256, bytes_accessed=40 * 2**20, transcendentals=0
        ),
    )(tokens, weights, gain, text, w_query, w_out, attn_gain, small)


KEY_PARTS = ((0, 512), (512, 512), (1024, 576))


class LayerLoad:
    def __init__(self, layer, own, other, dst, sem):
        self.here = lax.axis_index("section") == layer
        self.own = pltpu.make_async_copy(own, dst, sem)
        self.other = pltpu.make_async_copy(other, dst, sem)

    def start(self):
        pl.when(self.here)(lambda: self.own.start())
        pl.when(jnp.logical_not(self.here))(lambda: self.other.start())

    def wait(self):
        self.own.wait()


def add_to_query(acc, sq, block, gain, weights):
    values = block.astype(F32)
    sq[...] += jnp.sum(values * values, axis=-1, keepdims=True)
    acc[...] += jnp.dot((values * gain).astype(BF), weights, preferred_element_type=F32)


def finish_query(acc, sq, q_gain, query):
    inverse = lax.rsqrt(sq[:, :1] * (1.0 / 8192.0) + 1e-05)
    for head in range(4):
        one = acc[:, head * 128:(head + 1) * 128] * inverse
        one = one * lax.rsqrt(jnp.mean(one * one, axis=-1, keepdims=True) + 1e-05)
        query[head * 128:(head + 1) * 128, :] = (one * q_gain * 128.0 ** -0.5).astype(BF)


def attend(layer, choice_ref, valid_ref, query, pairs_ref, att_ref, tiles, total, norm, sem, before=None):
    core = lax.axis_index("section")
    first = choice_ref[core, 0, 0]
    second = choice_ref[core, 0, 1]
    other = second != first
    plan = (
        (first, 0, None),
        (first, 1, valid_ref[first] > 1),
        (second, 0, other),
        (second, 1, other & (valid_ref[second] > 1)),
    )

    def copy(slot):
        image, tile, _ = plan[slot]
        return pltpu.make_async_copy(
            pairs_ref.at[layer, image, pl.ds(tile * TILE_TOK, TILE_TOK)], tiles.at[slot], sem.at[slot]
        )

    def run(slot, fn):
        allowed = plan[slot][2]
        if allowed is None:
            fn()
        else:
            pl.when(allowed)(fn)

    for slot in range(4):
        run(slot, lambda slot=slot: copy(slot).start())
    total[...] = jnp.zeros_like(total)
    norm[...] = jnp.zeros_like(norm)
    if before is not None:
        before()

    def one(slot):
        copy(slot).wait()
        for start, size in KEY_PARTS:
            scores = lax.dot_general(
                query[...], tiles[slot, start:start + size, 0:128],
                (((1,), (1,)), ((), ())), preferred_element_type=F32,
            )
            expo = jnp.exp(scores)
            norm[...] += jnp.sum(expo, axis=-1, keepdims=True)
            total[...] += jnp.dot(
                expo.astype(BF), tiles[slot, start:start + size, 128:256], preferred_element_type=F32
            )

    for slot in range(4):
        run(slot, functools.partial(one, slot))
    for head in range(4):
        at = slice(head * 128, (head + 1) * 128)
        att_ref[:, at] = (total[at, :] / norm[at, :1]).astype(BF)


def first_attention(
    choice_ref, valid_ref, pairs_ref, text_ref, text_all_ref, wq_ref, wq_other_ref,
    attn_ref, attn_other_ref, small_ref, small_other_ref, att_ref,
    tiles, total, norm, sem, hidden, wq, attn, small, acc, sq, query, load_sem, wq_sem,
):
    core = lax.axis_index("section")
    tensor = lax.axis_index("tensor")
    attn_load = LayerLoad(0, attn_ref, attn_other_ref, attn, load_sem.at[8])
    small_load = LayerLoad(0, small_ref, small_other_ref, small, load_sem.at[9])
    attn_load.start()
    small_load.start()
    chunks = []
    for step in range(8):
        block = (tensor + step) % 8
        src = text_ref.at[core] if step == 0 else text_all_ref.at[block]
        at = pl.ds(pl.multiple_of(block * 1024, 1024), 1024)
        chunks.append((
            at,
            pltpu.make_async_copy(src, hidden.at[step], load_sem.at[step]),
            LayerLoad(0, wq_ref.at[at], wq_other_ref.at[at], wq.at[step], wq_sem.at[step]),
        ))
        chunks[-1][1].start()
        chunks[-1][2].start()

    def before():
        acc[...] = jnp.zeros_like(acc)
        sq[...] = jnp.zeros_like(sq)
        attn_load.wait()
        small_load.wait()
        for step, (at, text_load, wq_load) in enumerate(chunks):
            text_load.wait()
            wq_load.wait()
            add_to_query(acc, sq, hidden[step], attn[:, at], wq[step])
        finish_query(acc, sq, small[0:1, :], query)

    attend(0, choice_ref, valid_ref, query, pairs_ref, att_ref, tiles, total, norm, sem, before)


def second_attention(choice_ref, valid_ref, pairs_ref, query_ref, att_ref, tiles, total, norm, sem):
    attend(1, choice_ref, valid_ref, query_ref, pairs_ref, att_ref, tiles, total, norm, sem)


ATTEND_SCRATCH = [
    pltpu.VMEM((4, TILE_TOK, 256), BF),
    pltpu.VMEM((512, 128), F32),
    pltpu.VMEM((512, 128), F32),
    pltpu.SemaphoreType.DMA((4,)),
]


def attention_first(choice, valid, *arrays):
    any_spec = pl.BlockSpec(memory_space=pl.ANY)
    smem = pl.BlockSpec(memory_space=pltpu.SMEM)
    return pl.pallas_call(
        first_attention,
        name="attend0",
        out_shape=jax.ShapeDtypeStruct((128, 512), BF),
        in_specs=[smem, smem] + [any_spec] * 9,
        out_specs=pl.BlockSpec(memory_space=pltpu.VMEM),
        scratch_shapes=ATTEND_SCRATCH + [
            pltpu.VMEM((8, 128, 1024), BF),
            pltpu.VMEM((8, 1024, 512), BF),
            pltpu.VMEM((1, 8192), F32),
            pltpu.VMEM((2, 128), F32),
            pltpu.VMEM((128, 512), F32),
            pltpu.VMEM((128, 128), F32),
            pltpu.VMEM((512, 128), BF),
            pltpu.SemaphoreType.DMA((10,)),
            pltpu.SemaphoreType.DMA((8,)),
        ],
        compiler_params=pltpu.CompilerParams(vmem_limit_bytes=60 * 2**20),
        cost_estimate=pl.CostEstimate(flops=3 * 10**9, bytes_accessed=14 * 2**20, transcendentals=3 * 10**6),
    )(choice, valid, *arrays)


def attention_second(choice, valid, pairs, query):
    any_spec = pl.BlockSpec(memory_space=pl.ANY)
    smem = pl.BlockSpec(memory_space=pltpu.SMEM)
    vmem = pl.BlockSpec(memory_space=pltpu.VMEM)
    return pl.pallas_call(
        second_attention,
        name="attend1",
        out_shape=jax.ShapeDtypeStruct((128, 512), BF),
        in_specs=[smem, smem, any_spec, vmem],
        out_specs=vmem,
        scratch_shapes=ATTEND_SCRATCH,
        compiler_params=pltpu.CompilerParams(vmem_limit_bytes=60 * 2**20),
        cost_estimate=pl.CostEstimate(flops=2 * 10**9, bytes_accessed=4 * 2**20, transcendentals=3 * 10**6),
    )(choice, valid, pairs, query)


Y_ROWS = 80
NEAR = pl.ds(0, Y_ROWS)
REST = pl.ds(Y_ROWS, 128 - Y_ROWS)
HALF = (pl.ds(0, 512), pl.ds(512, 512))


def project_and_sum(layer, att_ref, wo_ref, wo_other_ref, scratch, greet):
    wo, part, from_y1, from_y2, from_z, from_c, from_c1, from_c2, wo_sem, send, recv = scratch
    x, zh, zl, y, core = position()
    y_up, y_dn = (y + 1) % 4, (y + 3) % 4
    to_y = (device(x, zh, zl, y_up, core), device(x, zh, zl, y_dn, core))
    to_z = device(x, zh, 1 - zl, y, core)
    order = ((0, 0), (0, 1), (2, 0), (1, 1), (1, 0), (2, 1), (3, 0), (3, 1))
    loads = {}
    for ring, side in order:
        block = side * 4 + ((y + 2) % 4, y_up, y_dn, y)[ring]
        at = pl.ds(pl.multiple_of(block * 1024, 1024), 1024)
        loads[ring, side] = LayerLoad(
            layer, wo_ref.at[:, at], wo_other_ref.at[:, at], wo.at[ring, side], wo_sem.at[ring * 2 + side]
        )
        loads[ring, side].start()

    def remote(kind, src, dst, peer):
        return pltpu.make_async_remote_copy(
            src_ref=src, dst_ref=dst, send_sem=send.at[kind], recv_sem=recv.at[kind],
            device_id=peer, device_id_type=MESH,
        )

    far = [remote(way, part.at[0, way, NEAR], from_y1.at[way], to_y[way]) for way in range(2)]
    near = {
        (ring, side): remote(2 + ring * 2 + side - 2, part.at[ring, side, NEAR], from_y2.at[ring - 1, side], to_y[ring - 1])
        for ring in (1, 2) for side in range(2)
    }
    cross = [remote(6 + ring, part.at[ring, 1 - zl, REST], from_c.at[ring], to_z) for ring in range(4)]
    cross_far = [
        remote(10 + way, part.at[0, zl, REST, HALF[way]], from_c1.at[way], to_y[way]) for way in range(2)
    ]
    cross_near = [remote(12 + way, part.at[1 + way, zl, REST], from_c2.at[way], to_y[way]) for way in range(2)]
    last = remote(14, part.at[3, 1 - zl, NEAR], from_z, to_z)
    at_once = {(0, 0): far[0], (0, 1): far[1], (2, 0): near[2, 0], (1, 1): near[1, 1]}

    for ring, side in order:
        loads[ring, side].wait()
        part[ring, side] = jnp.dot(att_ref[...], wo[ring, side], preferred_element_type=F32).astype(BF)
        if (ring, side) == (0, 0):
            greet()
        if (ring, side) in at_once:
            at_once[ring, side].start()

        @pl.when(zl != side)
        def _():
            cross[ring].start()

    def add(ring, side, rows, columns, addend):
        part[ring, side, rows, columns] = (
            part[ring, side, rows, columns].astype(F32) + addend.astype(F32)
        ).astype(BF)

    every = slice(None)
    for way, key in ((0, (1, 0)), (1, (2, 1))):
        far[way].wait_recv()
        add(*key, NEAR, every, from_y1[way])
        near[key].start()
    cross[0].wait_recv()
    add(0, zl, REST, every, from_c[0])
    for way in range(2):
        cross_far[way].start()
    for ring in range(1, 4):
        cross[ring].wait_recv()
        add(ring, zl, REST, every, from_c[ring])
    for key in near:
        near[key].wait_recv()
    add(3, 1 - zl, NEAR, every, from_y2[0, 1 - zl].astype(F32) + from_y2[1, 1 - zl].astype(F32))
    last.start()
    for way in range(2):
        cross_far[way].wait_recv()
        add(1 + way, zl, REST, HALF[way], from_c1[way])
        cross_near[way].start()
    first = part[3, zl, NEAR, :].astype(F32) + from_y2[0, zl].astype(F32) + from_y2[1, zl].astype(F32)
    second = part[3, zl, REST, :].astype(F32)
    last.wait_recv()
    first = first + from_z[...].astype(F32)
    for way in range(2):
        cross_near[way].wait_recv()
        second = second + from_c2[way].astype(F32)

    def drain():
        for copy in far + list(near.values()) + cross + cross_far + cross_near + [last]:
            copy.wait_send()

    return first, second, drain


SUM_SCRATCH = [
    pltpu.VMEM((4, 2, 512, 1024), BF),
    pltpu.VMEM((4, 2, 128, 1024), BF),
    pltpu.VMEM((2, Y_ROWS, 1024), BF),
    pltpu.VMEM((2, 2, Y_ROWS, 1024), BF),
    pltpu.VMEM((Y_ROWS, 1024), BF),
    pltpu.VMEM((4, 128 - Y_ROWS, 1024), BF),
    pltpu.VMEM((2, 128 - Y_ROWS, 512), BF),
    pltpu.VMEM((2, 128 - Y_ROWS, 1024), BF),
    pltpu.SemaphoreType.DMA((8,)),
    pltpu.SemaphoreType.DMA((15,)),
    pltpu.SemaphoreType.DMA((15,)),
]


def greeting(peers):
    barrier = pltpu.get_barrier_semaphore()
    for peer in peers:
        pl.semaphore_signal(barrier, inc=1, device_id=peer, device_id_type=MESH)
    pl.semaphore_wait(barrier, len(peers))


def middle_kernel(
    att_ref, text_ref, wo_ref, wo_other_ref, wq_ref, wq_other_ref,
    attn_ref, attn_other_ref, small_ref, small_other_ref, query_ref, upd_ref, *scratch,
):
    hidden, wq, attn, small, text, acc, sq, wq_sem, ag_send, ag_recv, par_sem = scratch[len(SUM_SCRATCH):]
    x, zh, zl, y, core = position()
    y_up, y_dn = (y + 1) % 4, (y + 3) % 4
    to_up = device(x, zh, zl, y_up, core)
    to_dn = device(x, zh, zl, y_dn, core)
    to_z = device(x, zh, 1 - zl, y, core)
    par_copies = [
        LayerLoad(0, small_ref, small_other_ref, small.at[0], par_sem.at[0]),
        LayerLoad(1, small_ref, small_other_ref, small.at[1], par_sem.at[1]),
        LayerLoad(1, attn_ref, attn_other_ref, attn, par_sem.at[2]),
        pltpu.make_async_copy(text_ref.at[core], text, par_sem.at[3]),
    ]
    for copy in par_copies:
        copy.start()

    first, second, drain = project_and_sum(
        0, att_ref, wo_ref, wo_other_ref, scratch[:len(SUM_SCRATCH)], lambda: greeting([to_up, to_dn, to_z])
    )
    mine, across = zl * 4, (1 - zl) * 4
    own, left, right, far = mine + y, mine + y_dn, mine + y_up, mine + (y + 2) % 4
    z_own, z_left, z_right, z_far = across + y, across + y_dn, across + y_up, across + (y + 2) % 4
    order = [own, left, right, z_own, z_left, z_right, far, z_far]
    chunks = []
    for k, block in enumerate(order):
        at = pl.ds(pl.multiple_of(block * 1024, 1024), 1024)
        chunks.append(LayerLoad(1, wq_ref.at[at], wq_other_ref.at[at], wq.at[k], wq_sem.at[k]))
        chunks[k].start()
    for copy in par_copies:
        copy.wait()
    gate = small[0, 1:2, 0:1]

    def remote(kind, block, rows, peer, half=None):
        ref = hidden.at[block, rows] if half is None else hidden.at[block, rows, HALF[half]]
        return pltpu.make_async_remote_copy(
            src_ref=ref, dst_ref=ref, send_sem=ag_send.at[kind], recv_sem=ag_recv.at[kind],
            device_id=peer, device_id_type=MESH,
        )

    copies = [
        remote(0, own, NEAR, to_z), remote(1, own, NEAR, to_up), remote(2, own, NEAR, to_dn),
        remote(3, own, REST, to_up), remote(4, own, REST, to_dn), remote(5, own, REST, to_z),
        remote(6, left, REST, to_up, 0), remote(7, right, REST, to_dn, 1),
        remote(8, left, REST, to_z), remote(9, right, REST, to_z), remote(10, far, REST, to_z),
        remote(11, z_own, NEAR, to_up), remote(12, z_own, NEAR, to_dn),
        remote(13, left, NEAR, to_up, 0), remote(14, right, NEAR, to_dn, 1),
        remote(15, z_left, NEAR, to_up, 0), remote(16, z_right, NEAR, to_dn, 1),
    ]

    def begin(*kinds):
        for kind in kinds:
            copies[kind].start()

    def arrive(*kinds):
        for kind in kinds:
            copies[kind].wait_recv()

    def use(k):
        chunks[k].wait()
        block = order[k]
        at = pl.ds(pl.multiple_of(block * 1024, 1024), 1024)
        add_to_query(acc, sq, hidden[block], attn[:, at], wq[k])

    hidden[own, NEAR, :] = (text[NEAR, :].astype(F32) + gate * first).astype(BF)
    begin(0)
    hidden[own, REST, :] = (text[REST, :].astype(F32) + gate * second).astype(BF)
    begin(3, 4, 1, 2, 5)
    upd_ref[...] = hidden[own]
    acc[...] = jnp.zeros_like(acc)
    sq[...] = jnp.zeros_like(sq)
    use(0)
    arrive(3)
    begin(6, 8)
    arrive(4)
    begin(7, 9)
    arrive(0)
    begin(11, 12)
    arrive(1)
    begin(13)
    arrive(2)
    begin(14)
    use(1)
    use(2)
    arrive(6, 7)
    begin(10)
    arrive(11)
    begin(15)
    arrive(12)
    begin(16)
    arrive(5)
    use(3)
    arrive(8)
    use(4)
    arrive(9)
    use(5)
    arrive(13, 14)
    use(6)
    arrive(10, 15, 16)
    use(7)
    finish_query(acc, sq, small[1, 0:1, :], query_ref)
    drain()
    for copy in copies:
        copy.wait_send()


def last_kernel(
    att_ref, upd_ref, wo_ref, wo_other_ref, small_ref, small_other_ref, out_ref, *scratch,
):
    small, last, core_send, core_recv, par_sem = scratch[len(SUM_SCRATCH):]
    x, zh, zl, y, core = position()
    to_y_up = device(x, zh, zl, (y + 1) % 4, core)
    to_y_dn = device(x, zh, zl, (y + 3) % 4, core)
    to_z_lo = device(x, zh, 1 - zl, y, core)
    to_core = device(x, zh, zl, y, 1 - core)
    par_copy = LayerLoad(1, small_ref, small_other_ref, small, par_sem.at[0])
    par_copy.start()
    send_first = pltpu.make_async_remote_copy(
        src_ref=upd_ref, dst_ref=out_ref.at[1], send_sem=core_send.at[0], recv_sem=core_recv.at[0],
        device_id=to_core, device_id_type=MESH,
    )
    send_last = pltpu.make_async_remote_copy(
        src_ref=last, dst_ref=out_ref.at[0], send_sem=core_send.at[1], recv_sem=core_recv.at[1],
        device_id=to_core, device_id_type=MESH,
    )

    def greet():
        greeting([to_y_up, to_y_dn, to_z_lo, to_core])

        @pl.when(core == 1)
        def _():
            send_first.start()

    first, second, drain = project_and_sum(1, att_ref, wo_ref, wo_other_ref, scratch[:len(SUM_SCRATCH)], greet)
    par_copy.wait()
    gate = small[1:2, 0:1]
    last[NEAR, :] = (upd_ref[NEAR, :].astype(F32) + gate * first).astype(BF)
    last[REST, :] = (upd_ref[REST, :].astype(F32) + gate * second).astype(BF)

    @pl.when(core == 0)
    def _():
        send_last.start()
        out_ref[0] = upd_ref[...]
        send_first.wait_recv()
        send_last.wait_send()

    @pl.when(core == 1)
    def _():
        out_ref[1] = last[...]
        send_first.wait_send()
        send_last.wait_recv()

    drain()


def middle(att, text, *weights):
    any_spec = pl.BlockSpec(memory_space=pl.ANY)
    vmem = pl.BlockSpec(memory_space=pltpu.VMEM)
    return pl.pallas_call(
        middle_kernel,
        name="middle",
        out_shape=[jax.ShapeDtypeStruct((512, 128), BF), jax.ShapeDtypeStruct((128, 1024), BF)],
        in_specs=[vmem] + [any_spec] * 9,
        out_specs=[vmem] * 2,
        scratch_shapes=SUM_SCRATCH + [
            pltpu.VMEM((8, 128, 1024), BF),
            pltpu.VMEM((8, 1024, 512), BF),
            pltpu.VMEM((1, 8192), F32),
            pltpu.VMEM((2, 2, 128), F32),
            pltpu.VMEM((128, 1024), BF),
            pltpu.VMEM((128, 512), F32),
            pltpu.VMEM((128, 128), F32),
            pltpu.SemaphoreType.DMA((8,)),
            pltpu.SemaphoreType.DMA((17,)),
            pltpu.SemaphoreType.DMA((17,)),
            pltpu.SemaphoreType.DMA((4,)),
        ],
        compiler_params=pltpu.CompilerParams(
            collective_id=1, has_side_effects=True, vmem_limit_bytes=60 * 2**20
        ),
    )(att, text, *weights)


def last_step(att, upd, *weights):
    any_spec = pl.BlockSpec(memory_space=pl.ANY)
    vmem = pl.BlockSpec(memory_space=pltpu.VMEM)
    return pl.pallas_call(
        last_kernel,
        name="last",
        out_shape=jax.ShapeDtypeStruct((2, 128, 1024), BF),
        in_specs=[vmem, vmem] + [any_spec] * 4,
        out_specs=vmem,
        scratch_shapes=SUM_SCRATCH + [
            pltpu.VMEM((2, 128), F32),
            pltpu.VMEM((128, 1024), BF),
            pltpu.SemaphoreType.DMA((2,)),
            pltpu.SemaphoreType.DMA((2,)),
            pltpu.SemaphoreType.DMA((1,)),
        ],
        compiler_params=pltpu.CompilerParams(
            collective_id=2, has_side_effects=True, vmem_limit_bytes=60 * 2**20
        ),
    )(att, upd, *weights)


def local(
    text_hidden,
    image_tokens,
    attn_gain,
    w_query,
    w_keyval,
    q_gain,
    k_gain,
    w_out,
    gate,
    image_choice,
    valid_tiles,
):
    text = text_hidden[:, 0]
    weights = jnp.transpose(w_keyval[0], (1, 0, 2))
    small = jnp.concatenate([q_gain, jnp.broadcast_to(jnp.tanh(gate)[:, None], (1, 128))])
    wq, wo = w_query[0], w_out[0]
    pairs, text_all, wq_other, wo_other, attn_other, small_other = image_pairs(
        image_tokens[0], weights, k_gain, text, wq, wo, attn_gain, small
    )
    gains = (attn_gain, attn_other, small, small_other)
    att = attention_first(image_choice, valid_tiles, pairs, text, text_all, wq, wq_other, *gains)
    query, updated = middle(att, text, wo, wo_other, wq, wq_other, *gains)
    att = attention_second(image_choice, valid_tiles, pairs, query)
    result = last_step(att, updated, wo, wo_other, small, small_other)
    return result[None, :, None]


def solution(mesh):
    placed = (
        P(None, "dp", None, "tensor"),
        P("dp", "section", "tensor"),
        P("section", None),
        P("section", None, "tensor"),
        P("section", "tensor", None, None),
        P("section", None),
        P("section", None),
        P("section", "tensor", None),
        P("section"),
        P(None, "dp", None),
        P(),
    )
    return jax.shard_map(
        local,
        mesh=mesh,
        in_specs=placed,
        out_specs=P("section", None, "dp", None, "tensor"),
        check_vma=False,
    )
```

time: 290 us -> 247 us (0.85)
  Pallas kernels: 271 us -> 238 us
  local copies, waits for them, and re-layouts: 12.8 us -> 8.19 us
    pallas_call x1, Pallas kernels: 59.7 us -> 39.5 us  [middle(): pl.pallas_call(middle_kernel, name='middle', out_shape=[jax.ShapeDtypeStr...]
    pallas_call x1, Pallas kernels: 34.1 us -> 24.7 us  [last_step(): pl.pallas_call(last_kernel, name='last', out_shape=jax.ShapeDtypeStruct((...]
    pallas_call x1, Pallas kernels: 166 us -> 157 us  [image_pairs(): pl.pallas_call(kv_kernel, name='kv', out_shape=[jax.ShapeDtypeStruct((2,...]
    unnamed x26 -> x2, local copies, waits for them, and re-layouts: 12.6 us -> 6.95 us
where the time goes in v3:
time: 247 us
  Pallas kernels  238 us (96%)
  local copies, waits for them, and re-layouts  8.19 us (3%)
    pallas_call x1, Pallas kernels, image_pairs(): pl.pallas_call(kv_kernel, name='kv', out_shape=[jax.ShapeDtypeStruct((2,...  157 us
    pallas_call x1, Pallas kernels, middle(): pl.pallas_call(middle_kernel, name='middle', out_shape=[jax.ShapeDtypeStr...  39.5 us
    pallas_call x1, Pallas kernels, last_step(): pl.pallas_call(last_kernel, name='last', out_shape=jax.ShapeDtypeStruct((...  24.7 us
    pallas_call x1, Pallas kernels, attention_first(): pl.pallas_call(first_attention, name='attend0', out_shape=jax.ShapeDtypeS...  10.2 us
    unnamed x2, local copies, waits for them, and re-layouts  6.95 us
    pallas_call x1, Pallas kernels, attention_second(): pl.pallas_call(second_attention, name='attend1', out_shape=jax.ShapeDtype...  6.25 us

profile of v3, /device:TPU:1, one launch (start us, length us, event | category | flops | bytes accessed | tf_op | source)
XLA Modules:
  0.0 247.1 jit_solution(9617021582944575903)
XLA Ops:
  0.7 1.2 concatenate.3.small_ref
  1.9 5.1 %copy.15 = bf16[1,1024,8,256]{3,1,2,0:T(8,128)(2,1)} copy(bf16[1,1024,8,256]{3,2,1,0:T(8,128)(2,1)} %param.15) | data formatting | bytes 8388608 | tf_op args[4]
  7.0 157.5 %kv.1 = (bf16[2,8,3200,256]{3,2,1,0:T(8,128)(2,1)}, bf16[8,128,1024]{2,1,0:T(8,128)(2,1)}, bf16[8192,512]{1,0:T(8,128)(2,1)}, bf16[512,8192]{1,0:T(8,128)(2,1)}, f32[1,8192]{1,0:T(1,128)}, /*index=5*/f32[2,128]{1,0:T(2,128)}) custom-call(bf16[1600,1024]{1,0:T(8,128)(2,1)} %bitcast.24, bf16[8,1024,256]{2,1,0:T(8,128)(2,1)} %bitcast.19, f32[1,128]{1,0:T(1,128)} %gain_ref.1, ...), custom_call_target="tpu_custom_call" | custom-call | flops 13421772800 | bytes 41943040 | tf_op jit(solution)/shard_map/kv/pallas_call | solution.py:309
  164.5 10.2 %attend0.1.att_ref = bf16[128,512]{1,0:T(8,128)(2,1)} custom-call(s32[2,1,2]{2,1,0:T(1,128)} %choice_ref.3, s32[8]{0:T(128)} %valid_ref.3, bf16[2,8,3200,256]{3,2,1,0:T(8,128)(2,1)} %get-tuple-element.13.pairs_ref, bf16[2,128,1024]{2,1,0:T(8,128)(2,1)} %bitcast.21, bf16[8,128,1024]{2,1,0:T(8,128)(2,1)} %get-tuple-element.14.text_all_ref, ...), custom_call_target="tpu_custom_call" | custom-call | flops 3000000000 | bytes 14680064 | tf_op jit(solution)/shard_map/attend0/pallas_call | solution.py:485
  174.7 39.5 %middle.1 = (bf16[512,128]{1,0:T(8,128)(2,1)}, bf16[128,1024]{1,0:T(8,128)(2,1)}) custom-call(bf16[128,512]{1,0:T(8,128)(2,1)} %attend0.1.att_ref, bf16[2,128,1024]{2,1,0:T(8,128)(2,1)} %bitcast.22, bf16[512,8192]{1,0:T(8,128)(2,1)} %bitcast.14, bf16[512,8192]{1,0:T(8,128)(2,1)} %get-tuple-element.18.wo_other_ref, bf16[8192,512]{1,0:T(8,128)(2,1)} %bitcast.18, ...), custom_call_target="tpu_custom_call" | custom-call | tf_op jit(solution)/shard_map/middle/pallas_call | solution.py:798
  214.3 6.3 %attend1.1.att_ref = bf16[128,512]{1,0:T(8,128)(2,1)} custom-call(s32[2,1,2]{2,1,0:T(1,128)} %choice_ref.3, s32[8]{0:T(128)} %valid_ref.3, bf16[2,8,3200,256]{3,2,1,0:T(8,128)(2,1)} %get-tuple-element.13.pairs_ref, bf16[512,128]{1,0:T(8,128)(2,1)} %get-tuple-element.19.query_ref), custom_call_target="tpu_custom_call" | custom-call | flops 2000000000 | bytes 4194304 | tf_op jit(solution)/shard_map/attend1/pallas_call | solution.py:511
  220.5 24.7 %last.1 = bf16[2,128,1024]{2,1,0:T(8,128)(2,1)} custom-call(bf16[128,512]{1,0:T(8,128)(2,1)} %attend1.1.att_ref, bf16[128,1024]{1,0:T(8,128)(2,1)} %get-tuple-element.20.upd_ref, bf16[512,8192]{1,0:T(8,128)(2,1)} %bitcast.15, bf16[512,8192]{1,0:T(8,128)(2,1)} %get-tuple-element.18.wo_other_ref, f32[2,128]{1,0:T(2,128)} %concatenate.3.small_ref, ...), custom_call_target="tpu_custom_call" | custom-call | tf_op jit(solution)/shard_map/last/pallas_call | solution.py:826
  245.2 1.9 copy.18

commit v4 on v3

--- a/solution.py
+++ b/solution.py
@@ -9,6 +9,8 @@
 
 TILE_TOK = 1600
 PIECES = 20
+GROUP = 2
+JOINT = 1
 MESH = pl.DeviceIdType.MESH
 BF = jnp.bfloat16
 F32 = jnp.float32
@@ -25,10 +27,10 @@
 
 
 def kv_kernel(
-    tok_ref, w_ref, gain_ref, text_ref, wq_ref, wo_ref, attn_ref, small_ref,
+    tok_ref, w_ref, gain_ref, q_gain_ref, gate_ref, text_ref, wq_ref, wo_ref, attn_ref,
     pairs_ref, text_out_ref, wq_out_ref, wo_out_ref, attn_out_ref, small_out_ref,
-    tok, wgt, part, from_y1, from_y2, from_z, done,
-    tok_sem, w_sem, loc_sem, core_send, core_recv, text_send, text_recv, send, recv,
+    small, tok, wgt, part, from_y1, from_y2, from_z, done,
+    tok_sem, w_sem, loc_sem, core_send, core_recv, text_send, text_recv, send, recv, mirror_recv,
 ):
     x, zh, zl, y, core = position()
     dp = x * 2 + zh
@@ -73,7 +75,7 @@
         src, dst = (
             (tok_ref, tok.at[pl.ds(pl.multiple_of(core * half, half), half)]),
             (attn_ref, attn_out_ref),
-            (small_ref, small_out_ref),
+            (small, small_out_ref.at[core]),
             (wq_ref, wq_out_ref),
             (wo_ref, wo_out_ref),
         )[kind]
@@ -102,7 +104,7 @@
     def remote(kind, piece, src, dst, peer):
         return pltpu.make_async_remote_copy(
             src_ref=src, dst_ref=dst,
-            send_sem=send.at[kind, piece], recv_sem=recv.at[kind, piece],
+            send_sem=send.at[kind], recv_sem=recv.at[kind, piece],
             device_id=peer, device_id_type=MESH,
         )
 
@@ -124,7 +126,7 @@
 
     def own_local(piece):
         at = rows_of(piece)
-        return pltpu.make_async_copy(done.at[at], out_ref.at[dp, at], loc_sem.at[piece])
+        return pltpu.make_async_copy(done.at[at], out_ref.at[dp, at], loc_sem.at[0])
 
     def pair_copy(way, piece):
         ref = out_ref.at[x * 2 + 1 - zh, rows_of(piece)]
@@ -135,13 +137,24 @@
         ref = out_ref.at[image, rows_of(piece)]
         return remote(10 + way, piece, ref, ref, to_x[way])
 
-    def mirror(kind, piece):
+    def mirror_copy(kind, at):
         across = (x + 2) % 4
         place = (
             (x, zh), (x, 1 - zh), (x_dn, zh), (x_up, zh), (x_dn, 1 - zh), (x_up, 1 - zh), (across, zh), (across, 1 - zh)
         )[kind]
-        ref = out_ref.at[place[0] * 2 + place[1], rows_of(piece)]
-        return remote(12 + kind, piece, done.at[rows_of(piece)] if kind == 0 else ref, ref, to_core)
+        ref = out_ref.at[place[0] * 2 + place[1], at]
+        return pltpu.make_async_remote_copy(
+            src_ref=done.at[at] if kind == 0 else ref, dst_ref=ref,
+            send_sem=send.at[12 + kind], recv_sem=mirror_recv.at[kind],
+            device_id=to_core, device_id_type=MESH,
+        )
+
+    def mirror(kinds, piece):
+        @pl.when(piece % GROUP == GROUP - 1)
+        def _():
+            at = pl.ds(first_row(piece - (GROUP - 1)), rows * GROUP)
+            for kind in kinds:
+                mirror_copy(kind, at).start()
 
     for ring in range(4):
         for side in range(2):
@@ -152,29 +165,34 @@
         return carry
 
     lax.fori_loop(0, PIECES // 2, start_tok, 0)
+    small[0:1, :] = q_gain_ref[...]
+    small[1:2, :] = jnp.tanh(jnp.broadcast_to(gate_ref[0], (1, 128)))
+    small_own = pltpu.make_async_copy(small, small_out_ref.at[core], loc_sem.at[1])
+    small_own.start()
     pl.semaphore_wait(barrier, len(peers))
-    for kind in range(3):
-        text_copy(kind).start()
-    for kind in range(5):
+    to_other_core(0).start()
+    text_copy(2).start()
+    for kind in range(1, 5):
         to_other_core(kind).start()
 
     def add(ring, side, at, addend):
         part[ring, side, at, :] = (part[ring, side, at, :].astype(F32) + addend.astype(F32)).astype(BF)
 
     def step_fn(it, carry):
-        @pl.when(it < PIECES)
+        @pl.when((it < PIECES) & (it % JOINT == 0))
         def _():
             piece = it
 
             @pl.when(piece < PIECES // 2)
             def _():
-                tok_copy(piece).wait()
+                for more in range(JOINT):
+                    tok_copy(piece + more).wait()
 
             @pl.when(piece == PIECES // 2)
             def _():
                 to_other_core(0).wait_recv()
 
-            at = rows_of(piece)
+            at = pl.ds(first_row(piece), rows * JOINT)
             for ring in range(4):
                 for side in range(2):
                     @pl.when(it == 0)
@@ -185,7 +203,8 @@
                         tok[at, :], wgt[ring, side], preferred_element_type=F32
                     ).astype(BF)
                     if ring == 0:
-                        y1_copy(side, piece).start()
+                        for more in range(JOINT):
+                            y1_copy(side, piece + more).start()
 
         @pl.when((it >= 1) & (it < PIECES + 1))
         def _():
@@ -195,6 +214,12 @@
                 y1_copy(way, piece).wait_recv()
                 add(1 + way, way, at, from_y1[way, at, :])
                 y2_copy(way, piece).start()
+
+            @pl.when(piece == PIECES - 1)
+            def _():
+                text_copy(2).wait_recv()
+                for kind in (0, 1, 3, 4):
+                    text_copy(kind).start()
 
         @pl.when((it >= 2) & (it < PIECES + 2))
         def _():
@@ -207,13 +232,6 @@
                 from_y2[0, 1 - zl, at, :].astype(F32) + from_y2[1, 1 - zl, at, :].astype(F32),
             )
             z_copy(piece).start()
-
-            @pl.when(piece == PIECES - 1)
-            def _():
-                for kind in range(3):
-                    text_copy(kind).wait_recv()
-                for kind in range(3, 7):
-                    text_copy(kind).start()
 
         @pl.when((it >= 3) & (it < PIECES + 3))
         def _():
@@ -232,7 +250,7 @@
             for way in range(3):
                 own_copy(way, piece).start()
             own_local(piece).start()
-            mirror(0, piece).start()
+            mirror((0,), piece)
 
         @pl.when((it >= 4) & (it < PIECES + 4))
         def _():
@@ -240,7 +258,13 @@
             own_copy(0, piece).wait_recv()
             for way in range(2):
                 pair_copy(way, piece).start()
-            mirror(1, piece).start()
+
+            @pl.when(piece == PIECES - 1)
+            def _():
+                for kind in (0, 1):
+                    text_copy(kind).wait_recv()
+                    text_copy(kind + 5).start()
+            mirror((1,), piece)
 
         @pl.when((it >= 5) & (it < PIECES + 5))
         def _():
@@ -251,12 +275,11 @@
                 forward_copy(way, piece).start()
             own_copy(2, piece).wait_recv()
             pair_copy(0, piece).wait_recv()
-            for kind in range(2, 6):
-                mirror(kind, piece).start()
+            mirror((2, 3, 4, 5), piece)
 
             @pl.when(piece == PIECES - 1)
             def _():
-                for kind in range(3, 5):
+                for kind in (3, 4):
                     text_copy(kind).wait_recv()
                     text_copy(kind + 4).start()
 
@@ -265,29 +288,29 @@
             piece = it - 6
             for way in range(2):
                 forward_copy(way, piece).wait_recv()
-            for kind in range(6, 8):
-                mirror(kind, piece).start()
+            mirror((6, 7), piece)
 
         return carry
 
     lax.fori_loop(0, PIECES + 6, step_fn, 0)
 
-    def finish(piece, carry):
-        z_copy(piece).wait_send()
-        for way in range(2):
-            y1_copy(way, piece).wait_send()
-            y2_copy(way, piece).wait_send()
-        for way in range(2):
-            pair_copy(way, piece).wait_send()
-            forward_copy(way, piece).wait_send()
-        for way in range(3):
-            own_copy(way, piece).wait_send()
-        own_local(piece).wait()
-        for kind in range(8):
-            mirror(kind, piece).wait()
-        return carry
-
-    lax.fori_loop(0, PIECES, finish, 0)
+    whole = pl.ds(0, half * 2)
+
+    def sent(kind, ref):
+        pltpu.make_async_remote_copy(
+            src_ref=ref, dst_ref=ref, send_sem=send.at[kind], recv_sem=recv.at[kind, 0],
+            device_id=to_core, device_id_type=MESH,
+        ).wait_send()
+
+    for way in range(2):
+        sent(way, part.at[0, way])
+        sent(2 + way, part.at[1 + way])
+    for kind in range(4, 12):
+        sent(kind, done)
+    for kind in range(8):
+        mirror_copy(kind, whole).wait()
+    pltpu.make_async_copy(done, out_ref.at[dp], loc_sem.at[0]).wait()
+    small_own.wait()
     to_other_core(0).wait_send()
     for kind in range(1, 5):
         to_other_core(kind).wait()
@@ -297,7 +320,7 @@
         text_copy(kind).wait_recv()
 
 
-def image_pairs(tokens, weights, gain, text, w_query, w_out, attn_gain, small):
+def image_pairs(tokens, weights, gain, q_gain, gate, text, w_query, w_out, attn_gain):
     half, width = tokens.shape
     heads = weights.shape[0]
     patches = half * 2
@@ -315,11 +338,15 @@
             like(w_query),
             like(w_out),
             like(attn_gain),
-            like(small),
+            jax.ShapeDtypeStruct((2, 2, 128), F32),
         ],
-        in_specs=[any_spec, any_spec, pl.BlockSpec(memory_space=pltpu.VMEM)] + [any_spec] * 5,
+        in_specs=[any_spec] * 2
+        + [pl.BlockSpec(memory_space=pltpu.VMEM)] * 2
+        + [pl.BlockSpec(memory_space=pltpu.SMEM)]
+        + [any_spec] * 4,
         out_specs=[any_spec] * 6,
         scratch_shapes=[
+            pltpu.VMEM((2, 128), F32),
             pltpu.VMEM((patches, width), BF),
             pltpu.VMEM((4, 2, width, 256), BF),
             pltpu.VMEM((4, 2, patches, 256), BF),
@@ -329,13 +356,14 @@
             pltpu.VMEM((patches, 256), BF),
             pltpu.SemaphoreType.DMA((PIECES // 2,)),
             pltpu.SemaphoreType.DMA((8,)),
-            pltpu.SemaphoreType.DMA((PIECES,)),
+            pltpu.SemaphoreType.DMA((2,)),
             pltpu.SemaphoreType.DMA((5,)),
             pltpu.SemaphoreType.DMA((5,)),
             pltpu.SemaphoreType.DMA((9,)),
             pltpu.SemaphoreType.DMA((9,)),
-            pltpu.SemaphoreType.DMA((20, PIECES)),
-            pltpu.SemaphoreType.DMA((20, PIECES)),
+            pltpu.SemaphoreType.DMA((20,)),
+            pltpu.SemaphoreType.DMA((12, PIECES)),
+            pltpu.SemaphoreType.DMA((8,)),
         ],
         compiler_params=pltpu.CompilerParams(
             collective_id=0, has_side_effects=True, vmem_limit_bytes=60 * 2**20
@@ -343,7 +371,7 @@
         cost_estimate=pl.CostEstimate(
             flops=2 * patches * width * heads * 256, bytes_accessed=40 * 2**20, transcendentals=0
         ),
-    )(tokens, weights, gain, text, w_query, w_out, attn_gain, small)
+    )(tokens, weights, gain, q_gain, gate, text, w_query, w_out, attn_gain)
 
 
 KEY_PARTS = ((0, 512), (512, 512), (1024, 576))
@@ -431,13 +459,13 @@
 
 def first_attention(
     choice_ref, valid_ref, pairs_ref, text_ref, text_all_ref, wq_ref, wq_other_ref,
-    attn_ref, attn_other_ref, small_ref, small_other_ref, att_ref,
+    attn_ref, attn_other_ref, small_ref, att_ref,
     tiles, total, norm, sem, hidden, wq, attn, small, acc, sq, query, load_sem, wq_sem,
 ):
     core = lax.axis_index("section")
     tensor = lax.axis_index("tensor")
     attn_load = LayerLoad(0, attn_ref, attn_other_ref, attn, load_sem.at[8])
-    small_load = LayerLoad(0, small_ref, small_other_ref, small, load_sem.at[9])
+    small_load = pltpu.make_async_copy(small_ref.at[0], small, load_sem.at[9])
     attn_load.start()
     small_load.start()
     chunks = []
@@ -486,7 +514,7 @@
         first_attention,
         name="attend0",
         out_shape=jax.ShapeDtypeStruct((128, 512), BF),
-        in_specs=[smem, smem] + [any_spec] * 9,
+        in_specs=[smem, smem] + [any_spec] * 8,
         out_specs=pl.BlockSpec(memory_space=pltpu.VMEM),
         scratch_shapes=ATTEND_SCRATCH + [
             pltpu.VMEM((8, 128, 1024), BF),
@@ -637,7 +665,7 @@
 
 def middle_kernel(
     att_ref, text_ref, wo_ref, wo_other_ref, wq_ref, wq_other_ref,
-    attn_ref, attn_other_ref, small_ref, small_other_ref, query_ref, upd_ref, *scratch,
+    attn_ref, attn_other_ref, small_ref, query_ref, upd_ref, *scratch,
 ):
     hidden, wq, attn, small, text, acc, sq, wq_sem, ag_send, ag_recv, par_sem = scratch[len(SUM_SCRATCH):]
     x, zh, zl, y, core = position()
@@ -646,10 +674,9 @@
     to_dn = device(x, zh, zl, y_dn, core)
     to_z = device(x, zh, 1 - zl, y, core)
     par_copies = [
-        LayerLoad(0, small_ref, small_other_ref, small.at[0], par_sem.at[0]),
-        LayerLoad(1, small_ref, small_other_ref, small.at[1], par_sem.at[1]),
-        LayerLoad(1, attn_ref, attn_other_ref, attn, par_sem.at[2]),
-        pltpu.make_async_copy(text_ref.at[core], text, par_sem.at[3]),
+        pltpu.make_async_copy(small_ref, small, par_sem.at[0]),
+        LayerLoad(1, attn_ref, attn_other_ref, attn, par_sem.at[1]),
+        pltpu.make_async_copy(text_ref.at[core], text, par_sem.at[2]),
     ]
     for copy in par_copies:
         copy.start()
@@ -744,7 +771,7 @@
 
 
 def last_kernel(
-    att_ref, upd_ref, wo_ref, wo_other_ref, small_ref, small_other_ref, out_ref, *scratch,
+    att_ref, upd_ref, wo_ref, wo_other_ref, small_ref, out_ref, *scratch,
 ):
     small, last, core_send, core_recv, par_sem = scratch[len(SUM_SCRATCH):]
     x, zh, zl, y, core = position()
@@ -752,7 +779,7 @@
     to_y_dn = device(x, zh, zl, (y + 3) % 4, core)
     to_z_lo = device(x, zh, 1 - zl, y, core)
     to_core = device(x, zh, zl, y, 1 - core)
-    par_copy = LayerLoad(1, small_ref, small_other_ref, small, par_sem.at[0])
+    par_copy = pltpu.make_async_copy(small_ref.at[1], small, par_sem.at[0])
     par_copy.start()
     send_first = pltpu.make_async_remote_copy(
         src_ref=upd_ref, dst_ref=out_ref.at[1], send_sem=core_send.at[0], recv_sem=core_recv.at[0],
@@ -799,7 +826,7 @@
         middle_kernel,
         name="middle",
         out_shape=[jax.ShapeDtypeStruct((512, 128), BF), jax.ShapeDtypeStruct((128, 1024), BF)],
-        in_specs=[vmem] + [any_spec] * 9,
+        in_specs=[vmem] + [any_spec] * 8,
         out_specs=[vmem] * 2,
         scratch_shapes=SUM_SCRATCH + [
             pltpu.VMEM((8, 128, 1024), BF),
@@ -812,7 +839,7 @@
             pltpu.SemaphoreType.DMA((8,)),
             pltpu.SemaphoreType.DMA((17,)),
             pltpu.SemaphoreType.DMA((17,)),
-            pltpu.SemaphoreType.DMA((4,)),
+            pltpu.SemaphoreType.DMA((3,)),
         ],
         compiler_params=pltpu.CompilerParams(
             collective_id=1, has_side_effects=True, vmem_limit_bytes=60 * 2**20
@@ -827,7 +854,7 @@
         last_kernel,
         name="last",
         out_shape=jax.ShapeDtypeStruct((2, 128, 1024), BF),
-        in_specs=[vmem, vmem] + [any_spec] * 4,
+        in_specs=[vmem, vmem] + [any_spec] * 3,
         out_specs=vmem,
         scratch_shapes=SUM_SCRATCH + [
             pltpu.VMEM((2, 128), F32),
@@ -857,16 +884,15 @@
 ):
     text = text_hidden[:, 0]
     weights = jnp.transpose(w_keyval[0], (1, 0, 2))
-    small = jnp.concatenate([q_gain, jnp.broadcast_to(jnp.tanh(gate)[:, None], (1, 128))])
     wq, wo = w_query[0], w_out[0]
-    pairs, text_all, wq_other, wo_other, attn_other, small_other = image_pairs(
-        image_tokens[0], weights, k_gain, text, wq, wo, attn_gain, small
+    pairs, text_all, wq_other, wo_other, attn_other, small = image_pairs(
+        image_tokens[0], weights, k_gain, q_gain, gate, text, wq, wo, attn_gain
     )
-    gains = (attn_gain, attn_other, small, small_other)
+    gains = (attn_gain, attn_other, small)
     att = attention_first(image_choice, valid_tiles, pairs, text, text_all, wq, wq_other, *gains)
     query, updated = middle(att, text, wo, wo_other, wq, wq_other, *gains)
     att = attention_second(image_choice, valid_tiles, pairs, query)
-    result = last_step(att, updated, wo, wo_other, small, small_other)
+    result = last_step(att, updated, wo, wo_other, small)
     return result[None, :, None]
 
 

time: 247 us -> 233 us (0.943)
  Pallas kernels: 238 us -> 225 us
    pallas_call x1, Pallas kernels: 157 us -> 142 us  [image_pairs(): pl.pallas_call(kv_kernel, name='kv', out_shape=[jax.ShapeDtypeStruct((2,...]
    pallas_call x1, Pallas kernels: 24.7 us -> 32.5 us  [last_step(): pl.pallas_call(last_kernel, name='last', out_shape=jax.ShapeDtypeStruct((...]
    pallas_call x1, Pallas kernels: 39.5 us -> 36.4 us  [middle(): pl.pallas_call(middle_kernel, name='middle', out_shape=[jax.ShapeDtypeStr...]
where the time goes in v4:
time: 233 us
  Pallas kernels  225 us (97%)
  local copies, waits for them, and re-layouts  6.95 us (3%)
    pallas_call x1, Pallas kernels, image_pairs(): pl.pallas_call(kv_kernel, name='kv', out_shape=[jax.ShapeDtypeStruct((2,...  142 us
    pallas_call x1, Pallas kernels, middle(): pl.pallas_call(middle_kernel, name='middle', out_shape=[jax.ShapeDtypeStr...  36.4 us
    pallas_call x1, Pallas kernels, last_step(): pl.pallas_call(last_kernel, name='last', out_shape=jax.ShapeDtypeStruct((...  32.5 us
    pallas_call x1, Pallas kernels, attention_first(): pl.pallas_call(first_attention, name='attend0', out_shape=jax.ShapeDtypeS...  9.07 us
    unnamed x2, local copies, waits for them, and re-layouts  6.95 us
    pallas_call x1, Pallas kernels, attention_second(): pl.pallas_call(second_attention, name='attend1', out_shape=jax.ShapeDtype...  5.14 us

profile of v4, /device:TPU:1, one launch (start us, length us, event | category | flops | bytes accessed | tf_op | source)
XLA Modules:
  0.0 232.9 jit_solution(17218287538242773605)
XLA Ops:
  0.7 5.1 %copy.15 = bf16[1,1024,8,256]{3,1,2,0:T(8,128)(2,1)} copy(bf16[1,1024,8,256]{3,2,1,0:T(8,128)(2,1)} %param.15) | data formatting | bytes 8388608 | tf_op args[4]
  5.7 142.2 %kv.1 = (bf16[2,8,3200,256]{3,2,1,0:T(8,128)(2,1)}, bf16[8,128,1024]{2,1,0:T(8,128)(2,1)}, bf16[8192,512]{1,0:T(8,128)(2,1)}, bf16[512,8192]{1,0:T(8,128)(2,1)},...) custom-call(bf16[1600,1024]{1,0:T(8,128)(2,1)} %bitcast.23, bf16[8,1024,256]{2,1,0:T(8,128)(2,1)} %bitcast.18, ...), custom_call_target="tpu_custom_call" | custom-call | flops 13421772800 | bytes 41943040 | tf_op jit(solution)/shard_map/kv/pallas_call | solution.py:332
  147.9 9.1 %attend0.1.att_ref = bf16[128,512]{1,0:T(8,128)(2,1)} custom-call(s32[2,1,2]{2,1,0:T(1,128)} %choice_ref.3, s32[8]{0:T(128)} %valid_ref.3, bf16[2,8,3200,256]{3,2,1,0:T(8,128)(2,1)} %get-tuple-element.13.pairs_ref, bf16[2,128,1024]{2,1,0:T(8,128)(2,1)} %bitcast.20, bf16[8,128,1024]{2,1,0:T(8,128)(2,1)} %get-tuple-element.14.text_all_ref, ...), custom_call_target="tpu_custom_call" | custom-call | flops 3000000000 | bytes 14680064 | tf_op jit(solution)/shard_map/attend0/pallas_call | solution.py:513
  157.0 36.4 %middle.1 = (bf16[512,128]{1,0:T(8,128)(2,1)}, bf16[128,1024]{1,0:T(8,128)(2,1)}) custom-call(bf16[128,512]{1,0:T(8,128)(2,1)} %attend0.1.att_ref, bf16[2,128,1024]{2,1,0:T(8,128)(2,1)} %bitcast.21, bf16[512,8192]{1,0:T(8,128)(2,1)} %bitcast.13, bf16[512,8192]{1,0:T(8,128)(2,1)} %get-tuple-element.18.wo_other_ref, bf16[8192,512]{1,0:T(8,128)(2,1)} %bitcast.17, ...), custom_call_target="tpu_custom_call" | custom-call | tf_op jit(solution)/shard_map/middle/pallas_call | solution.py:825
  193.4 5.1 %attend1.1.att_ref = bf16[128,512]{1,0:T(8,128)(2,1)} custom-call(s32[2,1,2]{2,1,0:T(1,128)} %choice_ref.3, s32[8]{0:T(128)} %valid_ref.3, bf16[2,8,3200,256]{3,2,1,0:T(8,128)(2,1)} %get-tuple-element.13.pairs_ref, bf16[512,128]{1,0:T(8,128)(2,1)} %get-tuple-element.19.query_ref), custom_call_target="tpu_custom_call" | custom-call | flops 2000000000 | bytes 4194304 | tf_op jit(solution)/shard_map/attend1/pallas_call | solution.py:539
  198.6 32.5 %last.1 = bf16[2,128,1024]{2,1,0:T(8,128)(2,1)} custom-call(bf16[128,512]{1,0:T(8,128)(2,1)} %attend1.1.att_ref, bf16[128,1024]{1,0:T(8,128)(2,1)} %get-tuple-element.20.upd_ref, bf16[512,8192]{1,0:T(8,128)(2,1)} %bitcast.14, bf16[512,8192]{1,0:T(8,128)(2,1)} %get-tuple-element.18.wo_other_ref, f32[2,2,128]{2,1,0:T(2,128)} %get-tuple-element.17.small_ref), custom_call_target="tpu_custom_call" | custom-call | tf_op jit(solution)/shard_map/last/pallas_call | solution.py:853
  231.0 1.9 copy.18

commit v5 on v4

--- a/solution.py
+++ b/solution.py
@@ -405,6 +405,25 @@
         query[head * 128:(head + 1) * 128, :] = (one * q_gain * 128.0 ** -0.5).astype(BF)
 
 
+def add_tile(query, tiles, image, tile, total, norm, weight=None):
+    for start, size in KEY_PARTS:
+        at = slice(tile * TILE_TOK + start, tile * TILE_TOK + start + size)
+        scores = lax.dot_general(
+            query[...], tiles[image, at, 0:128], (((1,), (1,)), ((), ())), preferred_element_type=F32
+        )
+        expo = jnp.exp(scores)
+        sums = jnp.sum(expo, axis=-1, keepdims=True)
+        values = jnp.dot(expo.astype(BF), tiles[image, at, 128:256], preferred_element_type=F32)
+        norm[...] += sums if weight is None else sums * weight
+        total[...] += values if weight is None else values * weight
+
+
+def side_by_side(total, norm, att_ref):
+    for head in range(4):
+        at = slice(head * 128, (head + 1) * 128)
+        att_ref[:, at] = (total[at, :] / norm[at, :1]).astype(BF)
+
+
 def attend(layer, choice_ref, valid_ref, query, pairs_ref, att_ref, tiles, total, norm, sem, before=None):
     core = lax.axis_index("section")
     first = choice_ref[core, 0, 0]
@@ -439,22 +458,11 @@
 
     def one(slot):
         copy(slot).wait()
-        for start, size in KEY_PARTS:
-            scores = lax.dot_general(
-                query[...], tiles[slot, start:start + size, 0:128],
-                (((1,), (1,)), ((), ())), preferred_element_type=F32,
-            )
-            expo = jnp.exp(scores)
-            norm[...] += jnp.sum(expo, axis=-1, keepdims=True)
-            total[...] += jnp.dot(
-                expo.astype(BF), tiles[slot, start:start + size, 128:256], preferred_element_type=F32
-            )
+        add_tile(query, tiles, slot, 0, total, norm)
 
     for slot in range(4):
         run(slot, functools.partial(one, slot))
-    for head in range(4):
-        at = slice(head * 128, (head + 1) * 128)
-        att_ref[:, at] = (total[at, :] / norm[at, :1]).astype(BF)
+    side_by_side(total, norm, att_ref)
 
 
 def first_attention(
@@ -495,10 +503,6 @@
     attend(0, choice_ref, valid_ref, query, pairs_ref, att_ref, tiles, total, norm, sem, before)
 
 
-def second_attention(choice_ref, valid_ref, pairs_ref, query_ref, att_ref, tiles, total, norm, sem):
-    attend(1, choice_ref, valid_ref, query_ref, pairs_ref, att_ref, tiles, total, norm, sem)
-
-
 ATTEND_SCRATCH = [
     pltpu.VMEM((4, TILE_TOK, 256), BF),
     pltpu.VMEM((512, 128), F32),
@@ -532,43 +536,34 @@
     )(choice, valid, *arrays)
 
 
-def attention_second(choice, valid, pairs, query):
-    any_spec = pl.BlockSpec(memory_space=pl.ANY)
-    smem = pl.BlockSpec(memory_space=pltpu.SMEM)
-    vmem = pl.BlockSpec(memory_space=pltpu.VMEM)
-    return pl.pallas_call(
-        second_attention,
-        name="attend1",
-        out_shape=jax.ShapeDtypeStruct((128, 512), BF),
-        in_specs=[smem, smem, any_spec, vmem],
-        out_specs=vmem,
-        scratch_shapes=ATTEND_SCRATCH,
-        compiler_params=pltpu.CompilerParams(vmem_limit_bytes=60 * 2**20),
-        cost_estimate=pl.CostEstimate(flops=2 * 10**9, bytes_accessed=4 * 2**20, transcendentals=3 * 10**6),
-    )(choice, valid, pairs, query)
-
-
 Y_ROWS = 80
 NEAR = pl.ds(0, Y_ROWS)
 REST = pl.ds(Y_ROWS, 128 - Y_ROWS)
 HALF = (pl.ds(0, 512), pl.ds(512, 512))
 
 
-def project_and_sum(layer, att_ref, wo_ref, wo_other_ref, scratch, greet):
-    wo, part, from_y1, from_y2, from_z, from_c, from_c1, from_c2, wo_sem, send, recv = scratch
-    x, zh, zl, y, core = position()
-    y_up, y_dn = (y + 1) % 4, (y + 3) % 4
-    to_y = (device(x, zh, zl, y_up, core), device(x, zh, zl, y_dn, core))
-    to_z = device(x, zh, 1 - zl, y, core)
-    order = ((0, 0), (0, 1), (2, 0), (1, 1), (1, 0), (2, 1), (3, 0), (3, 1))
+OUT_ORDER = ((0, 0), (0, 1), (2, 0), (1, 1), (1, 0), (2, 1), (3, 0), (3, 1))
+
+
+def load_out(layer, wo_ref, wo_other_ref, scratch):
+    wo, wo_sem = scratch[0], scratch[8]
+    y = position()[3]
     loads = {}
-    for ring, side in order:
-        block = side * 4 + ((y + 2) % 4, y_up, y_dn, y)[ring]
+    for ring, side in OUT_ORDER:
+        block = side * 4 + ((y + 2) % 4, (y + 1) % 4, (y + 3) % 4, y)[ring]
         at = pl.ds(pl.multiple_of(block * 1024, 1024), 1024)
         loads[ring, side] = LayerLoad(
             layer, wo_ref.at[:, at], wo_other_ref.at[:, at], wo.at[ring, side], wo_sem.at[ring * 2 + side]
         )
         loads[ring, side].start()
+    return loads
+
+
+def project_and_sum(att_ref, loads, scratch, greet=None):
+    wo, part, from_y1, from_y2, from_z, from_c, from_c1, from_c2, _, send, recv = scratch
+    x, zh, zl, y, core = position()
+    to_y = (device(x, zh, zl, (y + 1) % 4, core), device(x, zh, zl, (y + 3) % 4, core))
+    to_z = device(x, zh, 1 - zl, y, core)
 
     def remote(kind, src, dst, peer):
         return pltpu.make_async_remote_copy(
@@ -589,10 +584,10 @@
     last = remote(14, part.at[3, 1 - zl, NEAR], from_z, to_z)
     at_once = {(0, 0): far[0], (0, 1): far[1], (2, 0): near[2, 0], (1, 1): near[1, 1]}
 
-    for ring, side in order:
+    for ring, side in OUT_ORDER:
         loads[ring, side].wait()
         part[ring, side] = jnp.dot(att_ref[...], wo[ring, side], preferred_element_type=F32).astype(BF)
-        if (ring, side) == (0, 0):
+        if (ring, side) == (0, 0) and greet is not None:
             greet()
         if (ring, side) in at_once:
             at_once[ring, side].start()
@@ -663,16 +658,23 @@
     pl.semaphore_wait(barrier, len(peers))
 
 
-def middle_kernel(
-    att_ref, text_ref, wo_ref, wo_other_ref, wq_ref, wq_other_ref,
-    attn_ref, attn_other_ref, small_ref, query_ref, upd_ref, *scratch,
+def text_kernel(
+    choice_ref, valid_ref, att_ref, pairs_ref, text_ref, wo_ref, wo_other_ref, wq_ref, wq_other_ref,
+    attn_ref, attn_other_ref, small_ref, out_ref, *scratch,
 ):
-    hidden, wq, attn, small, text, acc, sq, wq_sem, ag_send, ag_recv, par_sem = scratch[len(SUM_SCRATCH):]
+    count = len(SUM_SCRATCH)
+    sums, last_sums = scratch[:count], scratch[count:2 * count]
+    (
+        images, hidden, wq, attn, small, text, acc, sq, query, total, norm, att, new,
+        wq_sem, ag_send, ag_recv, par_sem, core_send, core_recv,
+    ) = scratch[2 * count:]
     x, zh, zl, y, core = position()
     y_up, y_dn = (y + 1) % 4, (y + 3) % 4
     to_up = device(x, zh, zl, y_up, core)
     to_dn = device(x, zh, zl, y_dn, core)
     to_z = device(x, zh, 1 - zl, y, core)
+    to_core = device(x, zh, zl, y, 1 - core)
+    loads = load_out(0, wo_ref, wo_other_ref, sums)
     par_copies = [
         pltpu.make_async_copy(small_ref, small, par_sem.at[0]),
         LayerLoad(1, attn_ref, attn_other_ref, attn, par_sem.at[1]),
@@ -680,9 +682,10 @@
     ]
     for copy in par_copies:
         copy.start()
+    images_copy = pltpu.make_async_copy(pairs_ref.at[1], images, par_sem.at[3])
 
     first, second, drain = project_and_sum(
-        0, att_ref, wo_ref, wo_other_ref, scratch[:len(SUM_SCRATCH)], lambda: greeting([to_up, to_dn, to_z])
+        att_ref, loads, sums, lambda: greeting([to_up, to_dn, to_z, to_core])
     )
     mine, across = zl * 4, (1 - zl) * 4
     own, left, right, far = mine + y, mine + y_dn, mine + y_up, mine + (y + 2) % 4
@@ -693,6 +696,8 @@
         at = pl.ds(pl.multiple_of(block * 1024, 1024), 1024)
         chunks.append(LayerLoad(1, wq_ref.at[at], wq_other_ref.at[at], wq.at[k], wq_sem.at[k]))
         chunks[k].start()
+    images_copy.start()
+    last_loads = load_out(1, wo_ref, wo_other_ref, last_sums)
     for copy in par_copies:
         copy.wait()
     gate = small[0, 1:2, 0:1]
@@ -732,7 +737,23 @@
     begin(0)
     hidden[own, REST, :] = (text[REST, :].astype(F32) + gate * second).astype(BF)
     begin(3, 4, 1, 2, 5)
-    upd_ref[...] = hidden[own]
+    send_first = pltpu.make_async_remote_copy(
+        src_ref=hidden.at[own], dst_ref=out_ref.at[1], send_sem=core_send.at[0], recv_sem=core_recv.at[0],
+        device_id=to_core, device_id_type=MESH,
+    )
+    send_last = pltpu.make_async_remote_copy(
+        src_ref=new, dst_ref=out_ref.at[0], send_sem=core_send.at[1], recv_sem=core_recv.at[1],
+        device_id=to_core, device_id_type=MESH,
+    )
+
+    @pl.when(core == 1)
+    def _():
+        send_first.start()
+
+    @pl.when(core == 0)
+    def _():
+        out_ref[0] = hidden[own]
+
     acc[...] = jnp.zeros_like(acc)
     sq[...] = jnp.zeros_like(sq)
     use(0)
@@ -764,71 +785,54 @@
     use(6)
     arrive(10, 15, 16)
     use(7)
-    finish_query(acc, sq, small[1, 0:1, :], query_ref)
-    drain()
-    for copy in copies:
-        copy.wait_send()
-
-
-def last_kernel(
-    att_ref, upd_ref, wo_ref, wo_other_ref, small_ref, out_ref, *scratch,
-):
-    small, last, core_send, core_recv, par_sem = scratch[len(SUM_SCRATCH):]
-    x, zh, zl, y, core = position()
-    to_y_up = device(x, zh, zl, (y + 1) % 4, core)
-    to_y_dn = device(x, zh, zl, (y + 3) % 4, core)
-    to_z_lo = device(x, zh, 1 - zl, y, core)
-    to_core = device(x, zh, zl, y, 1 - core)
-    par_copy = pltpu.make_async_copy(small_ref.at[1], small, par_sem.at[0])
-    par_copy.start()
-    send_first = pltpu.make_async_remote_copy(
-        src_ref=upd_ref, dst_ref=out_ref.at[1], send_sem=core_send.at[0], recv_sem=core_recv.at[0],
-        device_id=to_core, device_id_type=MESH,
-    )
-    send_last = pltpu.make_async_remote_copy(
-        src_ref=last, dst_ref=out_ref.at[0], send_sem=core_send.at[1], recv_sem=core_recv.at[1],
-        device_id=to_core, device_id_type=MESH,
-    )
-
-    def greet():
-        greeting([to_y_up, to_y_dn, to_z_lo, to_core])
-
-        @pl.when(core == 1)
-        def _():
-            send_first.start()
-
-    first, second, drain = project_and_sum(1, att_ref, wo_ref, wo_other_ref, scratch[:len(SUM_SCRATCH)], greet)
-    par_copy.wait()
-    gate = small[1:2, 0:1]
-    last[NEAR, :] = (upd_ref[NEAR, :].astype(F32) + gate * first).astype(BF)
-    last[REST, :] = (upd_ref[REST, :].astype(F32) + gate * second).astype(BF)
+    finish_query(acc, sq, small[1, 0:1, :], query)
+
+    total[...] = jnp.zeros_like(total)
+    norm[...] = jnp.zeros_like(norm)
+    one_image, two_image = choice_ref[core, 0, 0], choice_ref[core, 0, 1]
+    other = jnp.where(two_image != one_image, 1.0, 0.0)
+    images_copy.wait()
+    add_tile(query, images, one_image, 0, total, norm)
+    add_tile(query, images, one_image, 1, total, norm, (valid_ref[one_image] - 1).astype(F32))
+    add_tile(query, images, two_image, 0, total, norm, other)
+    add_tile(query, images, two_image, 1, total, norm, other * (valid_ref[two_image] - 1).astype(F32))
+    side_by_side(total, norm, att)
+
+    first, second, last_drain = project_and_sum(att, last_loads, last_sums)
+    gate = small[1, 1:2, 0:1]
+    new[NEAR, :] = (hidden[own, NEAR, :].astype(F32) + gate * first).astype(BF)
+    new[REST, :] = (hidden[own, REST, :].astype(F32) + gate * second).astype(BF)
 
     @pl.when(core == 0)
     def _():
         send_last.start()
-        out_ref[0] = upd_ref[...]
         send_first.wait_recv()
         send_last.wait_send()
 
     @pl.when(core == 1)
     def _():
-        out_ref[1] = last[...]
+        out_ref[1] = new[...]
         send_first.wait_send()
         send_last.wait_recv()
 
     drain()
-
-
-def middle(att, text, *weights):
+    last_drain()
+    for copy in copies:
+        copy.wait_send()
+
+
+def text_steps(choice, valid, att, *arrays):
     any_spec = pl.BlockSpec(memory_space=pl.ANY)
     vmem = pl.BlockSpec(memory_space=pltpu.VMEM)
+    smem = pl.BlockSpec(memory_space=pltpu.SMEM)
     return pl.pallas_call(
-        middle_kernel,
-        name="middle",
-        out_shape=[jax.ShapeDtypeStruct((512, 128), BF), jax.ShapeDtypeStruct((128, 1024), BF)],
-        in_specs=[vmem] + [any_spec] * 8,
-        out_specs=[vmem] * 2,
-        scratch_shapes=SUM_SCRATCH + [
+        text_kernel,
+        name="text",
+        out_shape=jax.ShapeDtypeStruct((2, 128, 1024), BF),
+        in_specs=[smem, smem, vmem] + [any_spec] * len(arrays),
+        out_specs=vmem,
+        scratch_shapes=SUM_SCRATCH * 2 + [
+            pltpu.VMEM(arrays[0].shape[1:], BF),
             pltpu.VMEM((8, 128, 1024), BF),
             pltpu.VMEM((8, 1024, 512), BF),
             pltpu.VMEM((1, 8192), F32),
@@ -836,37 +840,22 @@
             pltpu.VMEM((128, 1024), BF),
             pltpu.VMEM((128, 512), F32),
             pltpu.VMEM((128, 128), F32),
+            pltpu.VMEM((512, 128), BF),
+            pltpu.VMEM((512, 128), F32),
+            pltpu.VMEM((512, 128), F32),
+            pltpu.VMEM((128, 512), BF),
+            pltpu.VMEM((128, 1024), BF),
             pltpu.SemaphoreType.DMA((8,)),
             pltpu.SemaphoreType.DMA((17,)),
             pltpu.SemaphoreType.DMA((17,)),
-            pltpu.SemaphoreType.DMA((3,)),
+            pltpu.SemaphoreType.DMA((4,)),
+            pltpu.SemaphoreType.DMA((2,)),
+            pltpu.SemaphoreType.DMA((2,)),
         ],
         compiler_params=pltpu.CompilerParams(
             collective_id=1, has_side_effects=True, vmem_limit_bytes=60 * 2**20
         ),
-    )(att, text, *weights)
-
-
-def last_step(att, upd, *weights):
-    any_spec = pl.BlockSpec(memory_space=pl.ANY)
-    vmem = pl.BlockSpec(memory_space=pltpu.VMEM)
-    return pl.pallas_call(
-        last_kernel,
-        name="last",
-        out_shape=jax.ShapeDtypeStruct((2, 128, 1024), BF),
-        in_specs=[vmem, vmem] + [any_spec] * 3,
-        out_specs=vmem,
-        scratch_shapes=SUM_SCRATCH + [
-            pltpu.VMEM((2, 128), F32),
-            pltpu.VMEM((128, 1024), BF),
-            pltpu.SemaphoreType.DMA((2,)),
-            pltpu.SemaphoreType.DMA((2,)),
-            pltpu.SemaphoreType.DMA((1,)),
-        ],
-        compiler_params=pltpu.CompilerParams(
-            collective_id=2, has_side_effects=True, vmem_limit_bytes=60 * 2**20
-        ),
-    )(att, upd, *weights)
+    )(choice, valid, att, *arrays)
 
 
 def local(
@@ -890,9 +879,9 @@
     )
     gains = (attn_gain, attn_other, small)
     att = attention_first(image_choice, valid_tiles, pairs, text, text_all, wq, wq_other, *gains)
-    query, updated = middle(att, text, wo, wo_other, wq, wq_other, *gains)
-    att = attention_second(image_choice, valid_tiles, pairs, query)
-    result = last_step(att, updated, wo, wo_other, small)
+    result = text_steps(
+        image_choice, valid_tiles, att, pairs, text, wo, wo_other, wq, wq_other, *gains
+    )
     return result[None, :, None]
 
 

time: 233 us -> 224 us (0.961)
  Pallas kernels: 225 us -> 215 us
    pallas_call x3 -> x1, Pallas kernels: 74 us -> 63.9 us  [text_steps(): pl.pallas_call(text_kernel, name='text', out_shape=jax.ShapeDtypeStruct((...]
where the time goes in v5:
time: 224 us; the launch traced here: 223 us
  Pallas kernels  215 us (96%)
  local copies, waits for them, and re-layouts  6.96 us (3%)
    pallas_call x1, Pallas kernels, image_pairs(): pl.pallas_call(kv_kernel, name='kv', out_shape=[jax.ShapeDtypeStruct((2,...  142 us
    pallas_call x1, Pallas kernels, text_steps(): pl.pallas_call(text_kernel, name='text', out_shape=jax.ShapeDtypeStruct((...  63.9 us
    pallas_call x1, Pallas kernels, attention_first(): pl.pallas_call(first_attention, name='attend0', out_shape=jax.ShapeDtypeS...  9.08 us
    unnamed x2, local copies, waits for them, and re-layouts  6.96 us

profile of v5, /device:TPU:1, one launch (start us, length us, event | category | flops | bytes accessed | tf_op | source)
XLA Modules:
  0.0 222.8 jit_solution(1516942242367971957)
XLA Ops:
  0.7 5.1 %copy.15 = bf16[1,1024,8,256]{3,1,2,0:T(8,128)(2,1)} copy(bf16[1,1024,8,256]{3,2,1,0:T(8,128)(2,1)} %param.15) | data formatting | bytes 8388608 | tf_op args[4]
  5.7 142.2 %kv.1 = (bf16[2,8,3200,256]{3,2,1,0:T(8,128)(2,1)}, bf16[8,128,1024]{2,1,0:T(8,128)(2,1)}, bf16[8192,512]{1,0:T(8,128)(2,1)}, bf16[512,8192]{1,0:T(8,128)(2,1)},...) custom-call(bf16[1600,1024]{1,0:T(8,128)(2,1)} %bitcast.22, bf16[8,1024,256]{2,1,0:T(8,128)(2,1)} %bitcast.17, ...), custom_call_target="tpu_custom_call" | custom-call | flops 13421772800 | bytes 41943040 | tf_op jit(solution)/shard_map/kv/pallas_call | solution.py:332
  147.9 9.1 %attend0.1.att_ref = bf16[128,512]{1,0:T(8,128)(2,1)} custom-call(s32[2,1,2]{2,1,0:T(1,128)} %choice_ref.3, s32[8]{0:T(128)} %valid_ref.3, bf16[2,8,3200,256]{3,2,1,0:T(8,128)(2,1)} %get-tuple-element.11.pairs_ref, bf16[2,128,1024]{2,1,0:T(8,128)(2,1)} %bitcast.19, bf16[8,128,1024]{2,1,0:T(8,128)(2,1)} %get-tuple-element.12.text_all_ref, ...), custom_call_target="tpu_custom_call" | custom-call | flops 3000000000 | bytes 14680064 | tf_op jit(solution)/shard_map/attend0/pallas_call | solution.py:517
  157.0 63.9 %text.1 = bf16[2,128,1024]{2,1,0:T(8,128)(2,1)} custom-call(s32[2,1,2]{2,1,0:T(1,128)} %choice_ref.3, s32[8]{0:T(128)} %valid_ref.3, bf16[128,512]{1,0:T(8,128)(2,1)} %attend0.1.att_ref, bf16[2,8,3200,256]{3,2,1,0:T(8,128)(2,1)} %get-tuple-element.11.pairs_ref, bf16[2,128,1024]{2,1,0:T(8,128)(2,1)} %bitcast.20, bf16[512,8192]{1,0:T(8,128)(2,1)} %bitcast.16, ...), custom_call_target="tpu_custom_call" | custom-call | tf_op jit(solution)/shard_map/text/pallas_call | solution.py:828
  220.9 1.9 copy.18

commit v6 on v5

--- a/solution.py
+++ b/solution.py
@@ -26,11 +26,39 @@
     return (x * 2 + zh, zl * 4 + y, core)
 
 
+class LayerLoad:
+    def __init__(self, layer, own, other, dst, sem):
+        self.here = lax.axis_index("section") == layer
+        self.own = pltpu.make_async_copy(own, dst, sem)
+        self.other = pltpu.make_async_copy(other, dst, sem)
+
+    def start(self):
+        pl.when(self.here)(lambda: self.own.start())
+        pl.when(jnp.logical_not(self.here))(lambda: self.other.start())
+
+    def wait(self):
+        self.own.wait()
+
+
+def add_to_query(acc, sq, block, gain, weights):
+    values = block.astype(F32)
+    sq[...] += jnp.sum(values * values, axis=-1, keepdims=True)
+    acc[...] += jnp.dot((values * gain).astype(BF), weights, preferred_element_type=F32)
+
+
+def finish_query(acc, sq, q_gain, query):
+    inverse = lax.rsqrt(sq[:, :1] * (1.0 / 8192.0) + 1e-05)
+    for head in range(4):
+        one = acc[:, head * 128:(head + 1) * 128] * inverse
+        one = one * lax.rsqrt(jnp.mean(one * one, axis=-1, keepdims=True) + 1e-05)
+        query[head * 128:(head + 1) * 128, :] = (one * q_gain * 128.0 ** -0.5).astype(BF)
+
+
 def kv_kernel(
     tok_ref, w_ref, gain_ref, q_gain_ref, gate_ref, text_ref, wq_ref, wo_ref, attn_ref,
-    pairs_ref, text_out_ref, wq_out_ref, wo_out_ref, attn_out_ref, small_out_ref,
-    small, tok, wgt, part, from_y1, from_y2, from_z, done,
-    tok_sem, w_sem, loc_sem, core_send, core_recv, text_send, text_recv, send, recv, mirror_recv,
+    pairs_ref, query_ref, wq_out_ref, wo_out_ref, attn_out_ref, small_out_ref,
+    hidden, wq, attn, layer_small, acc, sq, small, tok, wgt, part, from_y1, from_y2, from_z, done,
+    tok_sem, w_sem, loc_sem, core_send, core_recv, text_send, text_recv, send, recv, mirror_recv, load_sem, wq_sem,
 ):
     x, zh, zl, y, core = position()
     dp = x * 2 + zh
@@ -90,7 +118,7 @@
         block = (
             own + y, own + y, own + y, other + y, other + y, own + y_dn, own + y_up, other + y_dn, other + y_up
         )[kind]
-        dst = text_out_ref.at[block]
+        dst = hidden.at[block]
         src = text_ref.at[core] if kind < 3 else dst
         if kind >= 5:
             at = pl.ds(((kind - 5) % 2) * 64, 64)
@@ -169,11 +197,34 @@
     small[1:2, :] = jnp.tanh(jnp.broadcast_to(gate_ref[0], (1, 128)))
     small_own = pltpu.make_async_copy(small, small_out_ref.at[core], loc_sem.at[1])
     small_own.start()
+    text_own = pltpu.make_async_copy(text_ref.at[core], hidden.at[zl * 4 + y], load_sem.at[0])
+    text_own.start()
+    acc[...] = jnp.zeros_like(acc)
+    sq[...] = jnp.zeros_like(sq)
     pl.semaphore_wait(barrier, len(peers))
     to_other_core(0).start()
     text_copy(2).start()
     for kind in range(1, 5):
         to_other_core(kind).start()
+
+    own, other = zl * 4, (1 - zl) * 4
+    blocks = [own + y, other + y, own + y_dn, own + y_up, other + y_dn, other + y_up]
+    blocks += [own + (y + 2) % 4, other + (y + 2) % 4]
+    columns = [pl.ds(pl.multiple_of(block * 1024, 1024), 1024) for block in blocks]
+
+    def query_loads():
+        return [
+            LayerLoad(0, attn_ref, attn_out_ref, attn, load_sem.at[1]),
+            pltpu.make_async_copy(small_out_ref.at[0], layer_small, load_sem.at[2]),
+        ]
+
+    def wq_load(k):
+        return LayerLoad(0, wq_ref.at[columns[k]], wq_out_ref.at[columns[k]], wq.at[k], wq_sem.at[k])
+
+    def use(*which):
+        for k in which:
+            wq_load(k).wait()
+            add_to_query(acc, sq, hidden[blocks[k]], attn[:, columns[k]], wq[k])
 
     def add(ring, side, at, addend):
         part[ring, side, at, :] = (part[ring, side, at, :].astype(F32) + addend.astype(F32)).astype(BF)
@@ -232,6 +283,16 @@
                 from_y2[0, 1 - zl, at, :].astype(F32) + from_y2[1, 1 - zl, at, :].astype(F32),
             )
             z_copy(piece).start()
+
+            @pl.when(piece == PIECES - 1)
+            def _():
+                small_own.wait()
+                for kind in range(1, 4):
+                    to_other_core(kind).wait_recv()
+                for copy in query_loads():
+                    copy.start()
+                for k in range(8):
+                    wq_load(k).start()
 
         @pl.when((it >= 3) & (it < PIECES + 3))
         def _():
@@ -264,6 +325,10 @@
                 for kind in (0, 1):
                     text_copy(kind).wait_recv()
                     text_copy(kind + 5).start()
+                text_own.wait()
+                for copy in query_loads():
+                    copy.wait()
+                use(0, 1)
             mirror((1,), piece)
 
         @pl.when((it >= 5) & (it < PIECES + 5))
@@ -282,6 +347,7 @@
                 for kind in (3, 4):
                     text_copy(kind).wait_recv()
                     text_copy(kind + 4).start()
+                use(2, 3)
 
         @pl.when(it >= 6)
         def _():
@@ -290,9 +356,21 @@
                 forward_copy(way, piece).wait_recv()
             mirror((6, 7), piece)
 
+            @pl.when(piece == PIECES - 1)
+            def _():
+                use(4, 5)
+
         return carry
 
     lax.fori_loop(0, PIECES + 6, step_fn, 0)
+
+    for kind in (5, 6):
+        text_copy(kind).wait_recv()
+    use(6)
+    for kind in (7, 8):
+        text_copy(kind).wait_recv()
+    use(7)
+    finish_query(acc, sq, layer_small[0:1, :], query_ref)
 
     whole = pl.ds(0, half * 2)
 
@@ -310,14 +388,11 @@
     for kind in range(8):
         mirror_copy(kind, whole).wait()
     pltpu.make_async_copy(done, out_ref.at[dp], loc_sem.at[0]).wait()
-    small_own.wait()
-    to_other_core(0).wait_send()
-    for kind in range(1, 5):
-        to_other_core(kind).wait()
+    for kind in range(4):
+        to_other_core(kind).wait_send()
+    to_other_core(4).wait()
     for kind in range(9):
         text_copy(kind).wait_send()
-    for kind in range(5, 9):
-        text_copy(kind).wait_recv()
 
 
 def image_pairs(tokens, weights, gain, q_gain, gate, text, w_query, w_out, attn_gain):
@@ -334,7 +409,7 @@
         name="kv",
         out_shape=[
             jax.ShapeDtypeStruct((2, 8, patches, 256), BF),
-            jax.ShapeDtypeStruct((8,) + text.shape[1:], BF),
+            jax.ShapeDtypeStruct((512, 128), BF),
             like(w_query),
             like(w_out),
             like(attn_gain),
@@ -344,8 +419,14 @@
         + [pl.BlockSpec(memory_space=pltpu.VMEM)] * 2
         + [pl.BlockSpec(memory_space=pltpu.SMEM)]
         + [any_spec] * 4,
-        out_specs=[any_spec] * 6,
+        out_specs=[any_spec, pl.BlockSpec(memory_space=pltpu.VMEM)] + [any_spec] * 4,
         scratch_shapes=[
+            pltpu.VMEM((8, 128, 1024), BF),
+            pltpu.VMEM((8, 1024, 512), BF),
+            pltpu.VMEM((1, 8192), F32),
+            pltpu.VMEM((2, 128), F32),
+            pltpu.VMEM((128, 512), F32),
+            pltpu.VMEM((128, 128), F32),
             pltpu.VMEM((2, 128), F32),
             pltpu.VMEM((patches, width), BF),
             pltpu.VMEM((4, 2, width, 256), BF),
@@ -364,6 +445,8 @@
             pltpu.SemaphoreType.DMA((20,)),
             pltpu.SemaphoreType.DMA((12, PIECES)),
             pltpu.SemaphoreType.DMA((8,)),
+            pltpu.SemaphoreType.DMA((3,)),
+            pltpu.SemaphoreType.DMA((8,)),
         ],
         compiler_params=pltpu.CompilerParams(
             collective_id=0, has_side_effects=True, vmem_limit_bytes=60 * 2**20
@@ -377,34 +460,6 @@
 KEY_PARTS = ((0, 512), (512, 512), (1024, 576))
 
 
-class LayerLoad:
-    def __init__(self, layer, own, other, dst, sem):
-        self.here = lax.axis_index("section") == layer
-        self.own = pltpu.make_async_copy(own, dst, sem)
-        self.other = pltpu.make_async_copy(other, dst, sem)
-
-    def start(self):
-        pl.when(self.here)(lambda: self.own.start())
-        pl.when(jnp.logical_not(self.here))(lambda: self.other.start())
-
-    def wait(self):
-        self.own.wait()
-
-
-def add_to_query(acc, sq, block, gain, weights):
-    values = block.astype(F32)
-    sq[...] += jnp.sum(values * values, axis=-1, keepdims=True)
-    acc[...] += jnp.dot((values * gain).astype(BF), weights, preferred_element_type=F32)
-
-
-def finish_query(acc, sq, q_gain, query):
-    inverse = lax.rsqrt(sq[:, :1] * (1.0 / 8192.0) + 1e-05)
-    for head in range(4):
-        one = acc[:, head * 128:(head + 1) * 128] * inverse
-        one = one * lax.rsqrt(jnp.mean(one * one, axis=-1, keepdims=True) + 1e-05)
-        query[head * 128:(head + 1) * 128, :] = (one * q_gain * 128.0 ** -0.5).astype(BF)
-
-
 def add_tile(query, tiles, image, tile, total, norm, weight=None):
     for start, size in KEY_PARTS:
         at = slice(tile * TILE_TOK + start, tile * TILE_TOK + start + size)
@@ -424,7 +479,7 @@
         att_ref[:, at] = (total[at, :] / norm[at, :1]).astype(BF)
 
 
-def attend(layer, choice_ref, valid_ref, query, pairs_ref, att_ref, tiles, total, norm, sem, before=None):
+def attend(layer, choice_ref, valid_ref, query, pairs_ref, att_ref, tiles, total, norm, sem):
     core = lax.axis_index("section")
     first = choice_ref[core, 0, 0]
     second = choice_ref[core, 0, 1]
@@ -453,8 +508,6 @@
         run(slot, lambda slot=slot: copy(slot).start())
     total[...] = jnp.zeros_like(total)
     norm[...] = jnp.zeros_like(norm)
-    if before is not None:
-        before()
 
     def one(slot):
         copy(slot).wait()
@@ -465,42 +518,8 @@
     side_by_side(total, norm, att_ref)
 
 
-def first_attention(
-    choice_ref, valid_ref, pairs_ref, text_ref, text_all_ref, wq_ref, wq_other_ref,
-    attn_ref, attn_other_ref, small_ref, att_ref,
-    tiles, total, norm, sem, hidden, wq, attn, small, acc, sq, query, load_sem, wq_sem,
-):
-    core = lax.axis_index("section")
-    tensor = lax.axis_index("tensor")
-    attn_load = LayerLoad(0, attn_ref, attn_other_ref, attn, load_sem.at[8])
-    small_load = pltpu.make_async_copy(small_ref.at[0], small, load_sem.at[9])
-    attn_load.start()
-    small_load.start()
-    chunks = []
-    for step in range(8):
-        block = (tensor + step) % 8
-        src = text_ref.at[core] if step == 0 else text_all_ref.at[block]
-        at = pl.ds(pl.multiple_of(block * 1024, 1024), 1024)
-        chunks.append((
-            at,
-            pltpu.make_async_copy(src, hidden.at[step], load_sem.at[step]),
-            LayerLoad(0, wq_ref.at[at], wq_other_ref.at[at], wq.at[step], wq_sem.at[step]),
-        ))
-        chunks[-1][1].start()
-        chunks[-1][2].start()
-
-    def before():
-        acc[...] = jnp.zeros_like(acc)
-        sq[...] = jnp.zeros_like(sq)
-        attn_load.wait()
-        small_load.wait()
-        for step, (at, text_load, wq_load) in enumerate(chunks):
-            text_load.wait()
-            wq_load.wait()
-            add_to_query(acc, sq, hidden[step], attn[:, at], wq[step])
-        finish_query(acc, sq, small[0:1, :], query)
-
-    attend(0, choice_ref, valid_ref, query, pairs_ref, att_ref, tiles, total, norm, sem, before)
+def first_attention(choice_ref, valid_ref, pairs_ref, query_ref, att_ref, tiles, total, norm, sem):
+    attend(0, choice_ref, valid_ref, query_ref, pairs_ref, att_ref, tiles, total, norm, sem)
 
 
 ATTEND_SCRATCH = [
@@ -511,29 +530,20 @@
 ]
 
 
-def attention_first(choice, valid, *arrays):
+def attention_first(choice, valid, pairs, query):
     any_spec = pl.BlockSpec(memory_space=pl.ANY)
     smem = pl.BlockSpec(memory_space=pltpu.SMEM)
+    vmem = pl.BlockSpec(memory_space=pltpu.VMEM)
     return pl.pallas_call(
         first_attention,
-        name="attend0",
+        name="attend",
         out_shape=jax.ShapeDtypeStruct((128, 512), BF),
-        in_specs=[smem, smem] + [any_spec] * 8,
-        out_specs=pl.BlockSpec(memory_space=pltpu.VMEM),
-        scratch_shapes=ATTEND_SCRATCH + [
-            pltpu.VMEM((8, 128, 1024), BF),
-            pltpu.VMEM((8, 1024, 512), BF),
-            pltpu.VMEM((1, 8192), F32),
-            pltpu.VMEM((2, 128), F32),
-            pltpu.VMEM((128, 512), F32),
-            pltpu.VMEM((128, 128), F32),
-            pltpu.VMEM((512, 128), BF),
-            pltpu.SemaphoreType.DMA((10,)),
-            pltpu.SemaphoreType.DMA((8,)),
-        ],
+        in_specs=[smem, smem, any_spec, vmem],
+        out_specs=vmem,
+        scratch_shapes=ATTEND_SCRATCH,
         compiler_params=pltpu.CompilerParams(vmem_limit_bytes=60 * 2**20),
-        cost_estimate=pl.CostEstimate(flops=3 * 10**9, bytes_accessed=14 * 2**20, transcendentals=3 * 10**6),
-    )(choice, valid, *arrays)
+        cost_estimate=pl.CostEstimate(flops=2 * 10**9, bytes_accessed=4 * 2**20, transcendentals=3 * 10**6),
+    )(choice, valid, pairs, query)
 
 
 Y_ROWS = 80
@@ -874,11 +884,11 @@
     text = text_hidden[:, 0]
     weights = jnp.transpose(w_keyval[0], (1, 0, 2))
     wq, wo = w_query[0], w_out[0]
-    pairs, text_all, wq_other, wo_other, attn_other, small = image_pairs(
+    pairs, query, wq_other, wo_other, attn_other, small = image_pairs(
         image_tokens[0], weights, k_gain, q_gain, gate, text, wq, wo, attn_gain
     )
     gains = (attn_gain, attn_other, small)
-    att = attention_first(image_choice, valid_tiles, pairs, text, text_all, wq, wq_other, *gains)
+    att = attention_first(image_choice, valid_tiles, pairs, query)
     result = text_steps(
         image_choice, valid_tiles, att, pairs, text, wo, wo_other, wq, wq_other, *gains
     )

time: 224 us -> 223 us (level)
    pallas_call x1, Pallas kernels: 9.08 us -> 6.43 us  [attention_first(): pl.pallas_call(first_attention, name='attend', out_shape=jax.ShapeDtypeSt...]
where the time goes in v6:
time: 223 us
  Pallas kernels  215 us (96%)
  local copies, waits for them, and re-layouts  6.96 us (3%)
    pallas_call x1, Pallas kernels, image_pairs(): pl.pallas_call(kv_kernel, name='kv', out_shape=[jax.ShapeDtypeStruct((2,...  144 us
    pallas_call x1, Pallas kernels, text_steps(): pl.pallas_call(text_kernel, name='text', out_shape=jax.ShapeDtypeStruct((...  64.7 us
    unnamed x2, local copies, waits for them, and re-layouts  6.96 us
    pallas_call x1, Pallas kernels, attention_first(): pl.pallas_call(first_attention, name='attend', out_shape=jax.ShapeDtypeSt...  6.43 us

profile of v6, /device:TPU:1, one launch (start us, length us, event | category | flops | bytes accessed | tf_op | source)
XLA Modules:
  0.0 223.1 jit_solution(17802827207726878835)
XLA Ops:
  0.7 5.1 %copy.15 = bf16[1,1024,8,256]{3,1,2,0:T(8,128)(2,1)} copy(bf16[1,1024,8,256]{3,2,1,0:T(8,128)(2,1)} %param.15) | data formatting | bytes 8388608 | tf_op args[4]
  5.7 144.3 %kv.1 = (bf16[2,8,3200,256]{3,2,1,0:T(8,128)(2,1)}, bf16[512,128]{1,0:T(8,128)(2,1)}, bf16[8192,512]{1,0:T(8,128)(2,1)}, bf16[512,8192]{1,0:T(8,128)(2,1)}, f32[1,8192]{1,0:T(1,128)}, /*index=5*/f32[2,2,128]{2,1,0:T(2,128)}) custom-call(bf16[1600,1024]{1,0:T(8,128)(2,1)} %bitcast.20, bf16[8,1024,256]{2,1,0:T(8,128)(2,1)} %bitcast.16, f32[1,128]{1,0:T(1,128)} %gain_ref.1, ...), custom_call_target="tpu_custom_call" | custom-call | flops 13421772800 | bytes 41943040 | tf_op jit(solution)/shard_map/kv/pallas_call | solution.py:407
  150.0 6.4 %attend.1.att_ref = bf16[128,512]{1,0:T(8,128)(2,1)} custom-call(s32[2,1,2]{2,1,0:T(1,128)} %choice_ref.3, s32[8]{0:T(128)} %valid_ref.3, bf16[2,8,3200,256]{3,2,1,0:T(8,128)(2,1)} %get-tuple-element.11.pairs_ref, bf16[512,128]{1,0:T(8,128)(2,1)} %get-tuple-element.12.query_ref), custom_call_target="tpu_custom_call" | custom-call | flops 2000000000 | bytes 4194304 | tf_op jit(solution)/shard_map/attend/pallas_call | solution.py:537
  156.5 64.7 %text.1 = bf16[2,128,1024]{2,1,0:T(8,128)(2,1)} custom-call(s32[2,1,2]{2,1,0:T(1,128)} %choice_ref.3, s32[8]{0:T(128)} %valid_ref.3, bf16[128,512]{1,0:T(8,128)(2,1)} %attend.1.att_ref, bf16[2,8,3200,256]{3,2,1,0:T(8,128)(2,1)} %get-tuple-element.11.pairs_ref, bf16[2,128,1024]{2,1,0:T(8,128)(2,1)} %bitcast.19, bf16[512,8192]{1,0:T(8,128)(2,1)} %bitcast.15, ...), custom_call_target="tpu_custom_call" | custom-call | tf_op jit(solution)/shard_map/text/pallas_call | solution.py:838
  221.2 1.9 copy.18

commit v7 on v6

--- a/solution.py
+++ b/solution.py
@@ -546,7 +546,7 @@
     )(choice, valid, pairs, query)
 
 
-Y_ROWS = 80
+Y_ROWS = 64
 NEAR = pl.ds(0, Y_ROWS)
 REST = pl.ds(Y_ROWS, 128 - Y_ROWS)
 HALF = (pl.ds(0, 512), pl.ds(512, 512))

time: 223 us -> 223 us (level)
  no operation moved by 1% of the time
where the time goes in v7:
time: 223 us
  Pallas kernels  216 us (97%)
  local copies, waits for them, and re-layouts  6.96 us (3%)
    pallas_call x1, Pallas kernels, image_pairs(): pl.pallas_call(kv_kernel, name='kv', out_shape=[jax.ShapeDtypeStruct((2,...  144 us
    pallas_call x1, Pallas kernels, text_steps(): pl.pallas_call(text_kernel, name='text', out_shape=jax.ShapeDtypeStruct((...  63.8 us
    pallas_call x1, Pallas kernels, attention_first(): pl.pallas_call(first_attention, name='attend', out_shape=jax.ShapeDtypeSt...  7.55 us
    unnamed x2, local copies, waits for them, and re-layouts  6.96 us

profile of v7, /device:TPU:1, one launch (start us, length us, event | category | flops | bytes accessed | tf_op | source)
XLA Modules:
  0.0 223.3 jit_solution(9835186255093346059)
XLA Ops:
  0.7 5.1 %copy.15 = bf16[1,1024,8,256]{3,1,2,0:T(8,128)(2,1)} copy(bf16[1,1024,8,256]{3,2,1,0:T(8,128)(2,1)} %param.15) | data formatting | bytes 8388608 | tf_op args[4]
  5.7 144.3 %kv.1 = (bf16[2,8,3200,256]{3,2,1,0:T(8,128)(2,1)}, bf16[512,128]{1,0:T(8,128)(2,1)}, bf16[8192,512]{1,0:T(8,128)(2,1)}, bf16[512,8192]{1,0:T(8,128)(2,1)}, f32[1,8192]{1,0:T(1,128)}, /*index=5*/f32[2,2,128]{2,1,0:T(2,128)}) custom-call(bf16[1600,1024]{1,0:T(8,128)(2,1)} %bitcast.20, bf16[8,1024,256]{2,1,0:T(8,128)(2,1)} %bitcast.16, f32[1,128]{1,0:T(1,128)} %gain_ref.1, ...), custom_call_target="tpu_custom_call" | custom-call | flops 13421772800 | bytes 41943040 | tf_op jit(solution)/shard_map/kv/pallas_call | solution.py:407
  150.0 7.5 %attend.1.att_ref = bf16[128,512]{1,0:T(8,128)(2,1)} custom-call(s32[2,1,2]{2,1,0:T(1,128)} %choice_ref.3, s32[8]{0:T(128)} %valid_ref.3, bf16[2,8,3200,256]{3,2,1,0:T(8,128)(2,1)} %get-tuple-element.11.pairs_ref, bf16[512,128]{1,0:T(8,128)(2,1)} %get-tuple-element.12.query_ref), custom_call_target="tpu_custom_call" | custom-call | flops 2000000000 | bytes 4194304 | tf_op jit(solution)/shard_map/attend/pallas_call | solution.py:537
  157.6 63.8 %text.1 = bf16[2,128,1024]{2,1,0:T(8,128)(2,1)} custom-call(s32[2,1,2]{2,1,0:T(1,128)} %choice_ref.3, s32[8]{0:T(128)} %valid_ref.3, bf16[128,512]{1,0:T(8,128)(2,1)} %attend.1.att_ref, bf16[2,8,3200,256]{3,2,1,0:T(8,128)(2,1)} %get-tuple-element.11.pairs_ref, bf16[2,128,1024]{2,1,0:T(8,128)(2,1)} %bitcast.19, bf16[512,8192]{1,0:T(8,128)(2,1)} %bitcast.15, ...), custom_call_target="tpu_custom_call" | custom-call | tf_op jit(solution)/shard_map/text/pallas_call | solution.py:838
  221.4 1.9 copy.18
